TPU v7x, 512 devices: a whole 4x8x8 slice. The times are simulated.
512 devices in a mesh: dp: 4 (over x_hi, core), head: 8 (over y), ctx: 16 (over z, x_lo).
Axes of the slice: x: 4 (x_hi: 2, x_lo: 2; x = x_hi * 2 + x_lo), y: 8, z: 8, core: 2. Of those that a mesh axis runs over, the one named last changes fastest.
Arguments:
- queries: bfloat16 [8192, 64, 128], P(('dp', 'ctx'), 'head'), parts along dimension 0, may hold values from -8 to 8
- keys: bfloat16 [8192, 8, 128], P(('dp', 'ctx'), 'head'), parts along dimension 0, may hold values from -5 to 5
- values: bfloat16 [8192, 8, 128], P(('dp', 'ctx'), 'head'), parts along dimension 0, may hold values from -6 to 6
- output_gradient: bfloat16 [8192, 64, 128], P(('dp', 'ctx'), 'head'), parts along dimension 0, may hold values from -6 to 6
- block_order: int32 [128], P('dp'), parts along dimension 0, may hold values from 0 to 31, each once
Outputs:
- attn_out: bfloat16 [8192, 64, 128], P(('dp', 'ctx'), 'head'), parts along dimension 0
- grad_queries: bfloat16 [8192, 64, 128], P(('dp', 'ctx'), 'head'), parts along dimension 0
- grad_keys: bfloat16 [8192, 8, 128], P(('dp', 'ctx'), 'head'), parts along dimension 0
- grad_values: bfloat16 [8192, 8, 128], P(('dp', 'ctx'), 'head'), parts along dimension 0
There are 4 independent parts, one for each index of `dp`. A program takes and returns all parts, laid end to end along the dimension named above; each array names one. Nothing has to cross between parts.
Inputs may be any that keep to these rules, and one draw needn't show every extreme that they name: `block_order`: each of the 32 places occurs once.
All inputs are finite; a program needn't handle non-finite values.
Results may differ from a plain program's by a relative error of at most 0.035.
Values may be sent and summed in bfloat16 or wider, within the bound.
No kernel may reach another device: no remote copies, remote signals or barrier semaphores. Data moves between devices by JAX's collectives and lax.ppermute only.
A program may use at most 64 MiB of HBM per device.

v0:
```python
import math

import jax
import jax.numpy as jnp
from jax import lax
from jax.sharding import PartitionSpec as P

NEG_FILL = -1e30


def positions(first_row, row_count, block_order, block_rows):
    row_ids = first_row + jnp.arange(row_count, dtype=jnp.int32)
    blocks = row_ids // block_rows
    block_ids = jnp.arange(block_order.shape[0], dtype=jnp.int32)
    picked = jnp.sum(
        jnp.where(blocks[:, None] == block_ids[None, :], block_order[None, :], 0), axis=1
    )
    return picked * block_rows + row_ids % block_rows


def over_blocks(step_fn, carried, key_rows, value_rows, block_width):
    pieces = key_rows.shape[0] // block_width

    def advance(number, current):
        keys_now = lax.dynamic_slice_in_dim(key_rows, number * block_width, block_width, 0)
        values_now = lax.dynamic_slice_in_dim(value_rows, number * block_width, block_width, 0)
        return step_fn(current, keys_now, values_now, number * block_width)

    return lax.fori_loop(0, pieces, advance, carried)


def shards(queries, keys, values, output_gradient, block_order):
    tok_rows, heads_here, head_dim = queries.shape
    kv_here = keys.shape[1]
    repeat_count = heads_here // kv_here
    block_rows = tok_rows // 2
    score_scale = 1.0 / math.sqrt(head_dim)
    total_rows = tok_rows * lax.axis_size("ctx")
    query_rows = queries.reshape(tok_rows, kv_here, repeat_count, head_dim)
    grad_rows = output_gradient.reshape(tok_rows, kv_here, repeat_count, head_dim)
    query_pos = positions(lax.axis_index("ctx") * tok_rows, tok_rows, block_order, block_rows)

    def tile_scores(key_rows, first_row):
        key_pos = positions(first_row, key_rows.shape[0], block_order, block_rows)
        visible = (key_pos[None, :] <= query_pos[:, None])[None, :, None, :]
        scores = (
            jnp.einsum("sare,nae->asrn", query_rows, key_rows, preferred_element_type=jnp.float32)
            * score_scale
        )
        return (visible, scores)

    def forward_tile(carried, key_rows, value_rows, first_row):
        running_max, running_sum, accumulated = carried
        visible, scores = tile_scores(key_rows, first_row)
        row_top = jnp.max(jnp.where(visible, scores, NEG_FILL), axis=-1)
        new_max = jnp.maximum(running_max, row_top)
        weights = jnp.where(visible, jnp.exp(scores - new_max[..., None]), 0.0)
        factor = jnp.exp(running_max - new_max)
        running_sum = running_sum * factor + jnp.sum(weights, axis=-1)
        accumulated = accumulated * factor[..., None] + jnp.einsum(
            "asrn,nae->asre",
            weights.astype(jnp.bfloat16),
            value_rows,
            preferred_element_type=jnp.float32,
        )
        return (new_max, running_sum, accumulated)

    start_state = (
        jnp.full((kv_here, tok_rows, repeat_count), NEG_FILL, jnp.float32),
        jnp.zeros((kv_here, tok_rows, repeat_count), jnp.float32),
        jnp.zeros((kv_here, tok_rows, repeat_count, head_dim), jnp.float32),
    )

    def tile_weights(key_rows, value_rows, first_row, log_total, row_delta):
        visible, scores = tile_scores(key_rows, first_row)
        probs = jnp.where(visible, jnp.exp(scores - log_total[..., None]), 0.0)
        grad_probs = jnp.einsum(
            "sare,nae->asrn", grad_rows, value_rows, preferred_element_type=jnp.float32
        )
        grad_scores = probs * (grad_probs - row_delta[..., None])
        return (probs.astype(jnp.bfloat16), grad_scores.astype(jnp.bfloat16))

    def key_value_terms(probs_half, grad_half):
        grad_value = jnp.einsum(
            "asrn,sare->nae", probs_half, grad_rows, preferred_element_type=jnp.float32
        )
        grad_key = (
            jnp.einsum("asrn,sare->nae", grad_half, query_rows, preferred_element_type=jnp.float32)
            * score_scale
        )
        return jnp.stack([grad_key, grad_value], axis=1)

    def query_term(grad_half, key_rows):
        return (
            jnp.einsum("asrn,nae->asre", grad_half, key_rows, preferred_element_type=jnp.float32)
            * score_scale
        )

    empty_query = jnp.zeros((kv_here, tok_rows, repeat_count, head_dim), jnp.float32)

    def backward_tile(carried, key_rows, value_rows, first_row):
        grad_query, grad_terms = carried
        probs_half, grad_half = tile_weights(key_rows, value_rows, first_row, log_total, row_delta)
        grad_query = grad_query + query_term(grad_half, key_rows)
        grad_terms = lax.dynamic_update_slice_in_dim(
            grad_terms, key_value_terms(probs_half, grad_half), first_row, 0
        )
        return (grad_query, grad_terms)

    empty_terms = jnp.zeros((total_rows, 2, kv_here, head_dim), jnp.float32)
    arrived = (
        lax.all_gather(keys, "ctx", axis=0, tiled=True),
        lax.all_gather(values, "ctx", axis=0, tiled=True),
    )
    width_now = math.gcd(arrived[0].shape[0], tok_rows)
    running_max, running_sum, accumulated = over_blocks(
        forward_tile, start_state, arrived[0], arrived[1], width_now
    )
    normed = accumulated / running_sum[..., None]
    attn_out = (
        jnp.transpose(normed, (1, 0, 2, 3))
        .reshape(tok_rows, heads_here, head_dim)
        .astype(jnp.bfloat16)
    )
    finish_log_total = running_max + jnp.log(running_sum)
    rounded_back = attn_out.reshape(tok_rows, kv_here, repeat_count, head_dim).astype(jnp.float32)
    finish_row_delta = jnp.transpose(
        jnp.sum(rounded_back * grad_rows.astype(jnp.float32), axis=-1), (1, 0, 2)
    )
    attn_out, log_total, row_delta = (attn_out, finish_log_total, finish_row_delta)
    arrived = (
        lax.all_gather(keys, "ctx", axis=0, tiled=True),
        lax.all_gather(values, "ctx", axis=0, tiled=True),
    )
    width_now = math.gcd(arrived[0].shape[0], tok_rows)
    grad_query, grad_terms = over_blocks(
        backward_tile, (empty_query, empty_terms), arrived[0], arrived[1], width_now
    )
    summed = lax.psum_scatter(
        grad_terms.astype(jnp.bfloat16), "ctx", scatter_dimension=0, tiled=True
    ).astype(jnp.float32)
    grad_queries = (
        jnp.transpose(grad_query, (1, 0, 2, 3))
        .reshape(tok_rows, heads_here, head_dim)
        .astype(jnp.bfloat16)
    )
    grad_keys = summed[:, 0].astype(jnp.bfloat16)
    grad_values = summed[:, 1].astype(jnp.bfloat16)
    return (attn_out, grad_queries, grad_keys, grad_values)


def solution(mesh):
    in_specs = (
        P(("dp", "ctx"), "head", None),
        P(("dp", "ctx"), "head", None),
        P(("dp", "ctx"), "head", None),
        P(("dp", "ctx"), "head", None),
        P("dp"),
    )
    out_specs = (
        P(("dp", "ctx"), "head", None),
        P(("dp", "ctx"), "head", None),
        P(("dp", "ctx"), "head", None),
        P(("dp", "ctx"), "head", None),
    )
    return jax.shard_map(shards, mesh=mesh, in_specs=in_specs, out_specs=out_specs, check_vma=False)
```

profile of v0, /device:TPU:8, one launch (start us, length us, event | category | flops | bytes accessed | tf_op | source)
XLA Modules:
  0.0 208.2 jit_solution(3880812979295556627)
XLA Ops:
  7.3 0.6 copy-done.4
  8.0 42.7 %all_gather.8 = bf16[2048,1,128]{2,0,1:T(8,128)(2,1)S(1)} all-gather(bf16[128,1,128]{2,0,1:T(8,128)(2,1)} %param.10), channel_id=1, replica_groups=mesh['dp'=4,'head'=8,'ctx'=16] {'ctx'}, dimensions={0}, use_global_device_ids=true | all-gather | bytes 557056 | tf_op jit(solution)/shard_map/all_gather | solution.py:112
  50.7 32.5 %all_gather.9 = bf16[2048,1,128]{2,0,1:T(8,128)(2,1)S(1)} all-gather(bf16[128,1,128]{2,0,1:T(8,128)(2,1)S(1)} %copy-done.3), channel_id=1, replica_groups=mesh['dp'=4,'head'=8,'ctx'=16] {'ctx'}, dimensions={0}, use_global_device_ids=true | all-gather | bytes 557056 | tf_op jit(solution)/shard_map/all_gather | solution.py:113
  83.3 17.2 %while.38 = (s32[]{:T(128)}, f32[1,128,8]{1,2,0:T(8,128)S(1)}, f32[1,128,8]{1,2,0:T(8,128)S(1)}, f32[1,128,8,128]{3,1,2,0:T(8,128)S(1)}, s32[32]{0:T(128)S(1)}, ...) while((s32[]{:T(128)}, f32[1,128,8]{1,2,0:T(8,128)S(1)}, ...), condition=%wide.region_5.6_spmd.clone, body=%wide.region_1.5_spmd.clone.sunk | while | flops 68720264 | bytes 3084111 | solution.py:29
  84.0 0.4 fusion.77
  85.0 0.4 fusion.77
  86.1 0.4 fusion.77
  87.2 0.4 fusion.77
  88.2 0.4 fusion.77
  89.3 0.4 fusion.77
  90.4 0.4 fusion.77
  91.5 0.4 fusion.77
  92.5 0.4 fusion.77
  93.6 0.4 fusion.77
  94.7 0.4 fusion.77
  95.8 0.4 fusion.77
  96.8 0.4 fusion.77
  97.9 0.4 fusion.77
  99.0 0.4 fusion.77
  100.1 0.4 fusion.77
  100.6 1.1 multiply_reduce_fusion
  102.0 24.5 %while.39 = (s32[]{:T(128)}, f32[1,128,8,128]{3,1,2,0:T(8,128)S(1)}, bf16[2048,2,1,128]{3,0,2,1:T(8,128)(2,1)S(1)}, s32[32]{0:T(128)S(1)}, s32[128]{0:T(128)S(1)...) while((s32[]{:T(128)}, ...), condition=%wide.region_9.10_spmd.clone, body=%wide.region_7.9_spmd.clone.sunk | while | flops 169279104 | bytes 4796261 | solution.py:29
  102.2 0.3 fusion.89
  103.2 0.3 fusion.91
  103.7 0.3 fusion.89
  104.7 0.3 fusion.91
  105.3 0.3 fusion.89
  106.2 0.3 fusion.91
  106.8 0.3 fusion.89
  107.8 0.3 fusion.91
  108.3 0.3 fusion.89
  109.3 0.3 fusion.91
  110.8 0.3 fusion.91
  111.4 0.3 fusion.89
  112.4 0.3 fusion.91
  113.9 0.3 fusion.91
  115.4 0.3 fusion.91
  117.0 0.3 fusion.91
  118.5 0.3 fusion.91
  120.0 0.3 fusion.91
  121.6 0.3 fusion.91
  123.1 0.3 fusion.91
  124.6 0.3 fusion.91
  126.2 0.3 fusion.91
  126.5 1.0 copy-done
  127.5 1.0 copy.45
  128.5 71.4 %reduce-scatter.2.cloned.1.call-done = bf16[128,2,1,128]{3,0,2,1:T(8,128)(2,1)} async-done(((bf16[2048,2,1,128]{3,0,2,1:T(8,128)(2,1)}), bf16[128,2,1,128]{3,0,2,1:T(8,128)(2,1)}) %reduce-scatter.2.cloned.1.call-update) | async-done | bytes 65552 | tf_op jit(solution)/shard_map/reduce_scatter | solution.py:139
  199.9 1.4 slice_bitcast_fusion
  (304 shorter events, 26.6 us)
Async XLA Ops:
  7.2 192.8 %reduce-scatter.2.cloned.1.call-start = ((), (), s32[]{:S(2)}) async-start(), calls=%async_computation.1 | async-start | bytes 1114112 | tf_op jit(solution)/shard_map/reduce_scatter | solution.py:139
  7.3 0.7 copy-start.4
  8.0 42.7 %copy-start.3 = (bf16[128,1,128]{2,0,1:T(8,128)(2,1)S(1)}, bf16[128,1,128]{2,0,1:T(8,128)(2,1)}, u32[]{:S(2)}) copy-start(bf16[128,1,128]{2,0,1:T(8,128)(2,1)} %param.11) | copy-start | bytes 98308
  50.7 32.5 %copy-start.1 = (bf16[128,8,128]{2,1,0:T(8,128)(2,1)S(1)}, bf16[128,8,128]{2,1,0:T(8,128)(2,1)}, u32[]{:S(2)}) copy-start(bf16[128,8,128]{2,1,0:T(8,128)(2,1)} %param.12) | copy-start | bytes 786436
  50.7 32.5 %copy-start.2 = (bf16[128,8,128]{2,1,0:T(8,128)(2,1)S(1)}, bf16[128,8,128]{2,1,0:T(8,128)(2,1)}, u32[]{:S(2)}) copy-start(bf16[128,8,128]{2,1,0:T(8,128)(2,1)} %param.9) | copy-start | bytes 786436
  126.5 1.0 copy-start
Sparse Core Ops, SparseCore 0:
  127.6 72.2 reduce-scatter.1
where the time goes:
time: 208 us
  blocking collectives  75.2 us (36%)
  waiting for transfers between devices  71.4 us (34%)
  matrix products  30.4 us (15%)
  between operations  14.1 us (7%)
  other arithmetic  10 us (5%)
  local copies, waits for them, and re-layouts  4.48 us (2%)
  loops' own time  2.51 us (1%)
    reduce_scatter x1, waiting for transfers between devices, shards(): lax.psum_scatter(grad_terms.astype(jnp.bfloat16), 'ctx', scatter_dimensio...  71.4 us
    all_gather x1, blocking collectives, shards(): lax.all_gather(keys, 'ctx', axis=0, tiled=True)  42.7 us
    all_gather x1, blocking collectives, shards(): lax.all_gather(values, 'ctx', axis=0, tiled=True)  32.5 us
    dot_general x32, matrix products, tile_scores(): jnp.einsum('sare,nae->asrn', query_rows, key_rows, preferred_element_type...  8.02 us
    dot_general x16, matrix products, forward_tile(): jnp.einsum('asrn,nae->asre', weights.astype(jnp.bfloat16), value_rows, pr...  6.73 us
    dot_general x16, matrix products, query_term(): jnp.einsum('asrn,nae->asre', grad_half, key_rows, preferred_element_type=...  4.88 us
  transfers between devices with their start and end apart: 1, of which 1 were waited for; matrix products, arithmetic and copies ran while one was open for 0% of the time, Pallas kernels for 0%

commit v1 on v0

v1 whole, which is shorter than its diff:
```python
import functools
import math

import jax
import jax.numpy as jnp
from jax import lax
from jax.experimental import pallas as pl
from jax.experimental.pallas import tpu as pltpu
from jax.sharding import PartitionSpec as P

NEG_FILL = -1e30
TILE = 256
BLOCK = 64


def dot_nt(a, b):
    return lax.dot_general(a, b, (((1,), (1,)), ((), ())), preferred_element_type=jnp.float32)


def dot_nn(a, b):
    return lax.dot_general(a, b, (((1,), (0,)), ((), ())), preferred_element_type=jnp.float32)


def forward_kernel(
    order_ref, place_ref, q_own, q_far, g_own, g_far, kv_ref, p_ref, o_ref, stat_ref, vt_ref,
    *, own_tiles, repeat, scale
):
    step = pl.program_id(0)
    holders, _, rows, width = kv_ref.shape
    chunks = holders * rows // TILE
    per = TILE // rows

    @pl.when(step == 0)
    def _():
        for c in range(chunks):
            vals = kv_ref[c * per : (c + 1) * per, 1].reshape(TILE, width)
            vt_ref[:, c * TILE : (c + 1) * TILE] = vals.astype(jnp.float32).T.astype(jnp.bfloat16)

    mine = step < own_tiles
    q = jnp.where(mine, q_own[...], q_far[...])
    g = jnp.where(mine, g_own[...], g_far[...])
    side = place_ref[0] % 2
    ctx = jnp.where(mine, place_ref[0], place_ref[0] + 1 - 2 * side)
    token = lax.rem(step, own_tiles) * (TILE // repeat)
    blocks_here = rows // BLOCK
    row_place = order_ref[ctx * blocks_here + token // BLOCK] * BLOCK + token % BLOCK
    diff = lax.broadcasted_iota(jnp.int32, (BLOCK, TILE), 0) - (
        lax.broadcasted_iota(jnp.int32, (BLOCK, TILE), 1) // repeat
    )
    scaled = []
    top = None
    for c in range(chunks):
        keys = kv_ref[c * per : (c + 1) * per, 0].reshape(TILE, width)
        s = dot_nt(keys, q) * scale
        parts = []
        for b in range(TILE // BLOCK):
            at = c * (TILE // BLOCK) + b
            stored = ((at // blocks_here) * 2 + side) * blocks_here + at % blocks_here
            limit = row_place - order_ref[stored] * BLOCK
            parts.append(jnp.where(diff <= limit, s[b * BLOCK : (b + 1) * BLOCK], NEG_FILL))
        s = jnp.concatenate(parts, axis=0)
        scaled.append(s)
        here = jnp.max(s, axis=0, keepdims=True)
        top = here if top is None else jnp.maximum(top, here)
    total = jnp.zeros((1, TILE), jnp.float32)
    out = jnp.zeros((width, TILE), jnp.float32)
    for c in range(chunks):
        p = jnp.exp2(scaled[c] - top)
        total = total + jnp.sum(p, axis=0, keepdims=True)
        p = p.astype(jnp.bfloat16)
        p_ref[0, c * TILE : (c + 1) * TILE] = p
        out = out + dot_nn(vt_ref[:, c * TILE : (c + 1) * TILE], p)
    o_ref[0] = out
    delta = jnp.sum(out * g.astype(jnp.float32).T, axis=0, keepdims=True)
    stat_ref[0, 0:1] = top
    stat_ref[0, 1:2] = total
    stat_ref[0, 2:3] = delta
    stat_ref[0, 3:8] = jnp.zeros((5, TILE), jnp.float32)


def backward_kernel(
    q_own, q_far, g_own, g_far, kv_ref, p_ref, o_ref, here_ref, there_ref,
    dkv_ref, o_own, dq_own, send_ref, kt_ref, dk_ref, dv_ref,
    *, own_tiles, scale
):
    step = pl.program_id(0)
    holders, _, rows, width = kv_ref.shape
    chunks = holders * rows // TILE
    per = TILE // rows

    @pl.when(step == 0)
    def _():
        for c in range(chunks):
            keys = kv_ref[c * per : (c + 1) * per, 0].reshape(TILE, width)
            kt_ref[:, c * TILE : (c + 1) * TILE] = keys.astype(jnp.float32).T.astype(jnp.bfloat16)
        dk_ref[...] = jnp.zeros_like(dk_ref)
        dv_ref[...] = jnp.zeros_like(dv_ref)

    mine = step < own_tiles
    q = jnp.where(mine, q_own[...], q_far[...])
    g = jnp.where(mine, g_own[...], g_far[...])
    top_a, sum_a, delta_a = here_ref[0, 0:1], here_ref[0, 1:2], here_ref[0, 2:3]
    top_b, sum_b, delta_b = there_ref[0, 0:1], there_ref[0, 1:2], there_ref[0, 2:3]
    top = jnp.maximum(top_a, top_b)
    fa, fb = jnp.exp2(top_a - top), jnp.exp2(top_b - top)
    inverse = 1.0 / (sum_a * fa + sum_b * fb)
    factor = fa * inverse
    delta = (delta_a * fa + delta_b * fb) * inverse
    dq = jnp.zeros((width, TILE), jnp.float32)
    for c in range(chunks):
        span = slice(c * TILE, (c + 1) * TILE)
        vals = kv_ref[c * per : (c + 1) * per, 1].reshape(TILE, width)
        probs = p_ref[0, span].astype(jnp.float32) * factor
        grad_probs = dot_nt(vals, g)
        grad = (probs * (grad_probs - delta)).astype(jnp.bfloat16)
        dv_ref[span] += dot_nn(probs.astype(jnp.bfloat16), g)
        dk_ref[span] += dot_nn(grad, q)
        dq = dq + dot_nn(kt_ref[:, span], grad)
    dq = (dq * scale).T
    o = (o_ref[0] * factor).T

    @pl.when(mine)
    def _():
        o_own[...] = o
        dq_own[...] = dq

    @pl.when(jnp.logical_not(mine))
    def _():
        send_ref[0] = o.astype(jnp.bfloat16)
        send_ref[1] = dq.astype(jnp.bfloat16)

    @pl.when(step == pl.num_programs(0) - 1)
    def _():
        for z in range(holders):
            dkv_ref[z, 0] = (dk_ref[z * rows : (z + 1) * rows] * scale).astype(jnp.bfloat16)
            dkv_ref[z, 1] = dv_ref[z * rows : (z + 1) * rows].astype(jnp.bfloat16)


def shards(queries, keys, values, output_gradient, block_order):
    tok, heads, width = queries.shape
    ctx_size = lax.axis_size("ctx")
    holders = ctx_size // 2
    columns = [[2 * z + x for z in range(holders)] for x in range(2)]
    swap = [(i, i ^ 1) for i in range(ctx_size)]
    own_rows = tok * heads
    own_tiles = own_rows // TILE
    tiles = 2 * own_tiles
    col_keys = holders * tok
    score_scale = 1.0 / math.sqrt(width)

    q = queries.reshape(own_rows, width)
    g = output_gradient.reshape(own_rows, width)
    kv = jnp.stack([keys.reshape(tok, width), values.reshape(tok, width)])
    spread = jnp.broadcast_to(kv[None], (holders, 2, tok, width))
    kv_all = lax.all_to_all(spread, "ctx", 0, 0, axis_index_groups=columns, tiled=True)
    q_far = lax.ppermute(q, "ctx", swap)
    g_far = lax.ppermute(g, "ctx", swap)
    place = lax.axis_index("ctx").astype(jnp.int32).reshape(1)

    own_map = lambda i: (jnp.minimum(i, own_tiles - 1), 0)
    far_map = lambda i: (jnp.maximum(i - own_tiles, 0), 0)
    row_specs = [
        pl.BlockSpec((TILE, width), own_map),
        pl.BlockSpec((TILE, width), far_map),
        pl.BlockSpec((TILE, width), own_map),
        pl.BlockSpec((TILE, width), far_map),
        pl.BlockSpec((holders, 2, tok, width), lambda i: (0, 0, 0, 0)),
    ]
    smem = pl.BlockSpec(memory_space=pltpu.SMEM)
    p_spec = pl.BlockSpec((1, col_keys, TILE), lambda i: (i, 0, 0))
    o_spec = pl.BlockSpec((1, width, TILE), lambda i: (i, 0, 0))
    stat_spec = pl.BlockSpec((1, 8, TILE), lambda i: (i, 0, 0))
    pairs = 2 * own_rows * col_keys
    weights, partial_out, stats = pl.pallas_call(
        functools.partial(
            forward_kernel, own_tiles=own_tiles, repeat=heads,
            scale=score_scale * math.log2(math.e),
        ),
        grid=(tiles,),
        in_specs=[smem, smem] + row_specs,
        out_specs=[p_spec, o_spec, stat_spec],
        out_shape=[
            jax.ShapeDtypeStruct((tiles, col_keys, TILE), jnp.bfloat16),
            jax.ShapeDtypeStruct((tiles, width, TILE), jnp.float32),
            jax.ShapeDtypeStruct((tiles, 8, TILE), jnp.float32),
        ],
        scratch_shapes=[pltpu.VMEM((width, col_keys), jnp.bfloat16)],
        compiler_params=pltpu.CompilerParams(vmem_limit_bytes=40 * 2**20),
        cost_estimate=pl.CostEstimate(
            flops=4 * pairs * width, bytes_accessed=2 * pairs, transcendentals=pairs
        ),
        name="forward",
    )(block_order, place, q, q_far, g, g_far, kv_all)

    far_stats = lax.ppermute(stats, "ctx", swap)

    dkv, o_own, dq_own, send = pl.pallas_call(
        functools.partial(backward_kernel, own_tiles=own_tiles, scale=score_scale),
        grid=(tiles,),
        in_specs=row_specs
        + [
            p_spec,
            o_spec,
            stat_spec,
            pl.BlockSpec((1, 8, TILE), lambda i: (lax.rem(i + own_tiles, tiles), 0, 0)),
        ],
        out_specs=[
            pl.BlockSpec((holders, 2, tok, width), lambda i: (0, 0, 0, 0)),
            pl.BlockSpec((TILE, width), own_map),
            pl.BlockSpec((TILE, width), own_map),
            pl.BlockSpec((2, TILE, width), lambda i: (0, jnp.maximum(i - own_tiles, 0), 0)),
        ],
        out_shape=[
            jax.ShapeDtypeStruct((holders, 2, tok, width), jnp.bfloat16),
            jax.ShapeDtypeStruct((own_rows, width), jnp.float32),
            jax.ShapeDtypeStruct((own_rows, width), jnp.float32),
            jax.ShapeDtypeStruct((2, own_rows, width), jnp.bfloat16),
        ],
        scratch_shapes=[
            pltpu.VMEM((width, col_keys), jnp.bfloat16),
            pltpu.VMEM((col_keys, width), jnp.float32),
            pltpu.VMEM((col_keys, width), jnp.float32),
        ],
        compiler_params=pltpu.CompilerParams(vmem_limit_bytes=40 * 2**20),
        cost_estimate=pl.CostEstimate(
            flops=8 * pairs * width, bytes_accessed=2 * pairs, transcendentals=0
        ),
        name="backward",
    )(q, q_far, g, g_far, kv_all, weights, partial_out, stats, far_stats)

    terms = lax.all_to_all(dkv, "ctx", 0, 0, axis_index_groups=columns, tiled=True)
    received = lax.ppermute(send, "ctx", swap).astype(jnp.float32)
    attn_out = (o_own + received[0]).astype(jnp.bfloat16).reshape(tok, heads, width)
    grad_queries = (dq_own + received[1]).astype(jnp.bfloat16).reshape(tok, heads, width)
    summed = jnp.sum(terms.astype(jnp.float32), axis=0).astype(jnp.bfloat16)
    grad_keys = summed[0].reshape(tok, 1, width)
    grad_values = summed[1].reshape(tok, 1, width)
    return attn_out, grad_queries, grad_keys, grad_values


def solution(mesh):
    tokens = P(("dp", "ctx"), "head", None)
    return jax.shard_map(
        shards,
        mesh=mesh,
        in_specs=(tokens, tokens, tokens, tokens, P("dp")),
        out_specs=(tokens, tokens, tokens, tokens),
        check_vma=False,
    )
```

time: 208 us -> 76.8 us (0.37)
  the two profiles are of different devices: /device:TPU:8 before, /device:TPU:58 now
where the time goes in v1:
time: 76.8 us; the launch traced here: 76.3 us
  waiting for transfers between devices  27.2 us (35%)
  starting transfers between devices  26 us (34%)
  Pallas kernels  16.5 us (21%)
  local copies, waits for them, and re-layouts  4.09 us (5%)
  other arithmetic  1.87 us (2%)
    ppermute x1, waiting for transfers between devices, shards(): received = lax.ppermute(send, 'ctx', swap).astype(jnp.float32)  10.7 us
    all_to_all x1, starting transfers between devices, shards(): lax.all_to_all(spread, 'ctx', 0, 0, axis_index_groups=columns, tiled=True)  10.3 us
    pallas_call x1, Pallas kernels, shards(): pl.pallas_call(functools.partial(backward_kernel, own_tiles=own_tiles, sc...  8.99 us
    pallas_call x1, Pallas kernels, shards(): pl.pallas_call(functools.partial(forward_kernel, own_tiles=own_tiles, rep...  7.47 us
    ppermute x1, waiting for transfers between devices, shards(): q_far = lax.ppermute(q, 'ctx', swap)  5.47 us
    all_to_all x1, starting transfers between devices, shards(): lax.all_to_all(dkv, 'ctx', 0, 0, axis_index_groups=columns, tiled=True)  4.92 us
    ppermute x1, waiting for transfers between devices, shards(): g_far = lax.ppermute(g, 'ctx', swap)  4.15 us
    ppermute x1, waiting for transfers between devices, shards(): far_stats = lax.ppermute(stats, 'ctx', swap)  3.7 us
  transfers between devices with their start and end apart: 6, of which 6 were waited for; matrix products, arithmetic and copies ran while one was open for 1% of the time, Pallas kernels for 0%

profile of v1, /device:TPU:58, one launch (start us, length us, event | category | flops | bytes accessed | tf_op | source)
XLA Modules:
  0.0 76.3 jit_solution(16358410669728361357)
XLA Ops:
  0.6 0.0 copy-start.1
  0.6 0.0 copy-start.3
  0.7 0.8 %pad_maximum_fusion = bf16[2,128,128]{2,1,0:T(8,128)(2,1)S(1)} fusion(bf16[1,128,128]{2,1,0:T(8,128)(2,1)} %bitcast.35, bf16[1,128,128]{2,1,0:T(8,128)(2,1)} %bitcast.36), kind=kLoop, calls=%fused_computation.8 | loop fusion | flops 32768 | bytes 131072 | tf_op jit(solution)/shard_map/stack | solution.py:153
  1.5 0.9 %broadcast_in_dim.2 = bf16[8,2,128,128]{3,2,1,0:T(8,128)(2,1)} broadcast(bf16[2,128,128]{2,1,0:T(8,128)(2,1)S(1)} %pad_maximum_fusion), dimensions={1,2,3} | broadcast | bytes 589824 | tf_op jit(solution)/shard_map/broadcast_in_dim | solution.py:154
  2.4 10.3 %all-to-all-start = ((bf16[8,2,128,128]{3,2,1,0:T(8,128)(2,1)}), bf16[8,2,128,128]{3,2,1,0:T(8,128)(2,1)S(1)}, u32[]{:S(2)}, u32[]{:S(2)}) async-start(bf16[8,2,128,128]{3,2,1,0:T(8,128)(2,1)} %broadcast_in_dim.2), calls=%async_computation | async-start | bytes 1048576 | tf_op jit(solution)/shard_map/all_to_all | solution.py:155
  12.7 2.4 %collective-permute-start = (bf16[1024,128]{1,0:T(8,128)(2,1)}, bf16[1024,128]{1,0:T(8,128)(2,1)S(1)}, u32[]{:S(2)}, u32[]{:S(2)}) collective-permute-start(bf16[1024,128]{1,0:T(8,128)(2,1)} %bitcast.29), channel_id=1, source_target_pairs={{0,1},{1,0},{2,3},{3,2},{4,5},{5,4},{6,7},{7,6},{8,9},{9,8},{10,11... | collective-permute-start | bytes 786440 | tf_op jit(solution)/shard_map/ppermute | solution.py:156
  15.1 3.4 %collective-permute-start.1 = (bf16[1024,128]{1,0:T(8,128)(2,1)}, bf16[1024,128]{1,0:T(8,128)(2,1)S(1)}, u32[]{:S(2)}, u32[]{:S(2)}) collective-permute-start(bf16[1024,128]{1,0:T(8,128)(2,1)} %bitcast.32), channel_id=1, source_target_pairs={{0,1},{1,0},{2,3},{3,2},{4,5},{5,4},{6,7},{7,6},{8,9},{9,8},{10,11... | collective-permute-start | bytes 786440 | tf_op jit(solution)/shard_map/ppermute | solution.py:157
  18.6 5.5 %collective-permute-done.q_far = bf16[1024,128]{1,0:T(8,128)(2,1)S(1)} collective-permute-done((bf16[1024,128]{1,0:T(8,128)(2,1)}, bf16[1024,128]{1,0:T(8,128)(2,1)S(1)}, u32[]{:S(2)}, u32[]{:S(2)}) %collective-permute-start) | collective-permute-done | bytes 262176 | tf_op jit(solution)/shard_map/ppermute | solution.py:156
  24.0 4.2 %collective-permute-done.1.g_far = bf16[1024,128]{1,0:T(8,128)(2,1)S(1)} collective-permute-done((bf16[1024,128]{1,0:T(8,128)(2,1)}, bf16[1024,128]{1,0:T(8,128)(2,1)S(1)}, u32[]{:S(2)}, u32[]{:S(2)}) %collective-permute-start.1) | collective-permute-done | bytes 262176 | tf_op jit(solution)/shard_map/ppermute | solution.py:157
  28.2 2.0 %all-to-all-done.kv_ref = bf16[8,2,128,128]{3,2,1,0:T(8,128)(2,1)S(1)} async-done(((bf16[8,2,128,128]{3,2,1,0:T(8,128)(2,1)}), bf16[8,2,128,128]{3,2,1,0:T(8,128)(2,1)S(1)}, u32[]{:S(2)}, u32[]{:S(2)}) %all-to-all-start) | async-done | bytes 524320 | tf_op jit(solution)/shard_map/all_to_all | solution.py:155
  30.2 0.0 copy-start
  30.2 0.9 %copy-done = bf16[128,8,128]{2,1,0:T(8,128)(2,1)S(1)} copy-done((bf16[128,8,128]{2,1,0:T(8,128)(2,1)S(1)}, bf16[128,8,128]{2,1,0:T(8,128)(2,1)}, u32[]{:S(2)}) %copy-start) | copy-done | bytes 262168
  31.1 0.0 copy-start.2
  31.2 0.9 %copy-done.2 = bf16[128,8,128]{2,1,0:T(8,128)(2,1)S(1)} copy-done((bf16[128,8,128]{2,1,0:T(8,128)(2,1)S(1)}, bf16[128,8,128]{2,1,0:T(8,128)(2,1)}, u32[]{:S(2)}) %copy-start.2) | copy-done | bytes 262168
  32.1 0.0 copy-start.4
  32.1 0.7 copy-done.4
  32.8 7.5 %forward.1 = (bf16[8,1024,256]{2,1,0:T(8,128)(2,1)S(1)}, f32[8,128,256]{2,1,0:T(8,128)S(1)}, f32[8,8,256]{2,1,0:T(8,128)S(1)}) custom-call(s32[32]{0:T(128)S(1)} %copy-done.4, s32[1]{0:T(128)} %bitcast.4.place_ref, bf16[1024,128]{1,0:T(8,128)(2,1)S(1)} %bitcast.30, bf16[1024,128]{1,0:T(8,128)(2,1)S(1)} %collective-permute-done.q_far, ...), custom_call_target="tpu_custom_call" | custom-call | flops 1073741824 | bytes 4194304 | tf_op jit(solution)/shard_map/forward/pallas_call | solution.py:174
  40.2 2.5 %collective-permute-start.2 = (f32[8,8,256]{2,1,0:T(8,128)S(1)}, f32[8,8,256]{2,1,0:T(8,128)S(1)}, u32[]{:S(2)}, u32[]{:S(2)}) collective-permute-start(f32[8,8,256]{2,1,0:T(8,128)S(1)} %get-tuple-element.13.here_ref), channel_id=1, source_target_pairs={{0,1},{1,0},{2,3},{3,2},{4,5},{5,4},{6,7},{7,6},{8,9},{9,8},{10,11... | collective-permute-start | bytes 196616 | tf_op jit(solution)/shard_map/ppermute | solution.py:195
  42.7 3.7 %collective-permute-done.2.there_ref = f32[8,8,256]{2,1,0:T(8,128)S(1)} collective-permute-done((f32[8,8,256]{2,1,0:T(8,128)S(1)}, f32[8,8,256]{2,1,0:T(8,128)S(1)}, u32[]{:S(2)}, u32[]{:S(2)}) %collective-permute-start.2) | collective-permute-done | bytes 65568 | tf_op jit(solution)/shard_map/ppermute | solution.py:195
  46.4 0.0 copy-done.1
  46.4 0.0 copy-done.3
  46.4 9.0 %backward.1 = (bf16[8,2,128,128]{3,2,1,0:T(8,128)(2,1)}, f32[1024,128]{1,0:T(8,128)S(1)}, f32[1024,128]{1,0:T(8,128)S(1)}, bf16[2,1024,128]{2,1,0:T(8,128)(2,1)S(1)}) custom-call(bf16[1024,128]{1,0:T(8,128)(2,1)S(1)} %bitcast.31, bf16[1024,128]{1,0:T(8,128)(2,1)S(1)} %collective-permute-done.q_far, bf16[1024,128]{1,0:T(8,128)(2,1)S(1)} %bitcast.34, ...), custom_call_target="tpu_custom_call" | custom-call | flops 2147483648 | bytes 4194304 | tf_op jit(solution)/shard_map/backward/pallas_call | solution.py:197
  55.4 4.9 %all-to-all-start.1 = ((bf16[8,2,128,128]{3,2,1,0:T(8,128)(2,1)}), bf16[8,2,128,128]{3,2,1,0:T(8,128)(2,1)S(1)}, u32[]{:S(2)}, u32[]{:S(2)}) async-start(bf16[8,2,128,128]{3,2,1,0:T(8,128)(2,1)} %get-tuple-element.17), calls=%async_computation.1 | async-start | bytes 1048576 | tf_op jit(solution)/shard_map/all_to_all | solution.py:231
  60.3 2.5 %collective-permute-start.3 = (bf16[2,1024,128]{2,1,0:T(8,128)(2,1)S(1)}, bf16[2,1024,128]{2,1,0:T(8,128)(2,1)S(1)}, u32[]{:S(2)}, u32[]{:S(2)}) collective-permute-start(bf16[2,1024,128]{2,1,0:T(8,128)(2,1)S(1)} %get-tuple-element.15), channel_id=1, source_target_pairs={{0,1},{1,0},{2,3},{3,2},{4,5},{5,4},{6,7},{7,6},{8,9},{9,8},{10,11... | collective-permute-start | bytes 1572872 | tf_op jit(solution)/shard_map/ppermute | solution.py:232
  62.8 10.7 %collective-permute-done.3 = bf16[2,1024,128]{2,1,0:T(8,128)(2,1)S(1)} collective-permute-done((bf16[2,1024,128]{2,1,0:T(8,128)(2,1)S(1)}, bf16[2,1024,128]{2,1,0:T(8,128)(2,1)S(1)}, u32[]{:S(2)}, u32[]{:S(2)}) %collective-permute-start.3) | collective-permute-done | bytes 524320 | tf_op jit(solution)/shard_map/ppermute | solution.py:232
  73.5 0.1 convert_element_type.11
  73.6 0.9 %fusion.5 = (bf16[128,8,128]{2,1,0:T(8,128)(2,1)}, bf16[128,8,128]{2,1,0:T(8,128)(2,1)}) fusion(f32[1024,128]{1,0:T(8,128)S(1)} %get-tuple-element.16, f32[2,1024,128]{2,1,0:T(8,128)S(1)} %convert_element_type.11, f32[1024,128]{1,0:T(8,128)S(1)} %get-tuple-element.14), kind=kLoop, calls=%fused_computation.7 | loop fusion | flops 524288 | bytes 2621440 | tf_op jit(solution)/shard_map/reshape | solution.py:234
  74.5 1.2 %all-to-all-done.1 = bf16[8,2,128,128]{3,2,1,0:T(8,128)(2,1)S(1)} async-done(((bf16[8,2,128,128]{3,2,1,0:T(8,128)(2,1)}), bf16[8,2,128,128]{3,2,1,0:T(8,128)(2,1)S(1)}, u32[]{:S(2)}, u32[]{:S(2)}) %all-to-all-start.1) | async-done | bytes 524320 | tf_op jit(solution)/shard_map/all_to_all | solution.py:231
  75.6 0.1 reduce_sum.12
  75.7 0.6 slice_bitcast_fusion.2
Async XLA Ops:
  0.6 45.8 %copy-start.1 = (bf16[128,8,128]{2,1,0:T(8,128)(2,1)S(1)}, bf16[128,8,128]{2,1,0:T(8,128)(2,1)}, u32[]{:S(2)}) copy-start(bf16[128,8,128]{2,1,0:T(8,128)(2,1)} %param.5) | copy-start | bytes 786436
  0.6 45.8 %copy-start.3 = (bf16[128,8,128]{2,1,0:T(8,128)(2,1)S(1)}, bf16[128,8,128]{2,1,0:T(8,128)(2,1)}, u32[]{:S(2)}) copy-start(bf16[128,8,128]{2,1,0:T(8,128)(2,1)} %param.8) | copy-start | bytes 786436
  2.4 27.8 %all-to-all-start = ((bf16[8,2,128,128]{3,2,1,0:T(8,128)(2,1)}), bf16[8,2,128,128]{3,2,1,0:T(8,128)(2,1)S(1)}, u32[]{:S(2)}, u32[]{:S(2)}) async-start(bf16[8,2,128,128]{3,2,1,0:T(8,128)(2,1)} %broadcast_in_dim.2), calls=%async_computation | async-start | bytes 1048576 | tf_op jit(solution)/shard_map/all_to_all | solution.py:155
  12.7 11.3 %collective-permute-start = (bf16[1024,128]{1,0:T(8,128)(2,1)}, bf16[1024,128]{1,0:T(8,128)(2,1)S(1)}, u32[]{:S(2)}, u32[]{:S(2)}) collective-permute-start(bf16[1024,128]{1,0:T(8,128)(2,1)} %bitcast.29), channel_id=1, source_target_pairs={{0,1},{1,0},{2,3},{3,2},{4,5},{5,4},{6,7},{7,6},{8,9},{9,8},{10,11... | collective-permute-start | bytes 786440 | tf_op jit(solution)/shard_map/ppermute | solution.py:156
  15.1 13.0 %collective-permute-start.1 = (bf16[1024,128]{1,0:T(8,128)(2,1)}, bf16[1024,128]{1,0:T(8,128)(2,1)S(1)}, u32[]{:S(2)}, u32[]{:S(2)}) collective-permute-start(bf16[1024,128]{1,0:T(8,128)(2,1)} %bitcast.32), channel_id=1, source_target_pairs={{0,1},{1,0},{2,3},{3,2},{4,5},{5,4},{6,7},{7,6},{8,9},{9,8},{10,11... | collective-permute-start | bytes 786440 | tf_op jit(solution)/shard_map/ppermute | solution.py:157
  30.2 1.0 %copy-start = (bf16[128,8,128]{2,1,0:T(8,128)(2,1)S(1)}, bf16[128,8,128]{2,1,0:T(8,128)(2,1)}, u32[]{:S(2)}) copy-start(bf16[128,8,128]{2,1,0:T(8,128)(2,1)} %param.5) | copy-start | bytes 786436
  31.1 0.9 %copy-start.2 = (bf16[128,8,128]{2,1,0:T(8,128)(2,1)S(1)}, bf16[128,8,128]{2,1,0:T(8,128)(2,1)}, u32[]{:S(2)}) copy-start(bf16[128,8,128]{2,1,0:T(8,128)(2,1)} %param.8) | copy-start | bytes 786436
  32.1 0.7 copy-start.4
  40.2 6.2 %collective-permute-start.2 = (f32[8,8,256]{2,1,0:T(8,128)S(1)}, f32[8,8,256]{2,1,0:T(8,128)S(1)}, u32[]{:S(2)}, u32[]{:S(2)}) collective-permute-start(f32[8,8,256]{2,1,0:T(8,128)S(1)} %get-tuple-element.13.here_ref), channel_id=1, source_target_pairs={{0,1},{1,0},{2,3},{3,2},{4,5},{5,4},{6,7},{7,6},{8,9},{9,8},{10,11... | collective-permute-start | bytes 196616 | tf_op jit(solution)/shard_map/ppermute | solution.py:195
  55.4 20.2 %all-to-all-start.1 = ((bf16[8,2,128,128]{3,2,1,0:T(8,128)(2,1)}), bf16[8,2,128,128]{3,2,1,0:T(8,128)(2,1)S(1)}, u32[]{:S(2)}, u32[]{:S(2)}) async-start(bf16[8,2,128,128]{3,2,1,0:T(8,128)(2,1)} %get-tuple-element.17), calls=%async_computation.1 | async-start | bytes 1048576 | tf_op jit(solution)/shard_map/all_to_all | solution.py:231
  60.3 13.2 %collective-permute-start.3 = (bf16[2,1024,128]{2,1,0:T(8,128)(2,1)S(1)}, bf16[2,1024,128]{2,1,0:T(8,128)(2,1)S(1)}, u32[]{:S(2)}, u32[]{:S(2)}) collective-permute-start(bf16[2,1024,128]{2,1,0:T(8,128)(2,1)S(1)} %get-tuple-element.15), channel_id=1, source_target_pairs={{0,1},{1,0},{2,3},{3,2},{4,5},{5,4},{6,7},{7,6},{8,9},{9,8},{10,11... | collective-permute-start | bytes 1572872 | tf_op jit(solution)/shard_map/ppermute | solution.py:232

commit v2 on v0

v2 whole, which is shorter than its diff:
```python
import functools
import math

import jax
import jax.numpy as jnp
from jax import lax
from jax.experimental import pallas as pl
from jax.experimental.pallas import tpu as pltpu
from jax.sharding import PartitionSpec as P

NEG_FILL = -1e30
TILE = 256
BLOCK = 64
VMEM = pl.BlockSpec(memory_space=pltpu.VMEM)
SMEM = pl.BlockSpec(memory_space=pltpu.SMEM)
HBM = pl.BlockSpec(memory_space=pltpu.HBM)
F32 = jnp.float32
HALF = jnp.bfloat16


def dot_nt(a, b):
    return lax.dot_general(a, b, (((1,), (1,)), ((), ())), preferred_element_type=F32)


def dot_nn(a, b):
    return lax.dot_general(a, b, (((1,), (0,)), ((), ())), preferred_element_type=F32)


def flipped(a):
    return a.astype(F32).T


def spread_kernel(k_ref, v_ref, out_ref, held, sems):
    loads = [
        pltpu.make_async_copy(ref, held.at[i], sems.at[i]) for i, ref in enumerate((k_ref, v_ref))
    ]
    for load in loads:
        load.start()
    for load in loads:
        load.wait()
    stores = [
        pltpu.make_async_copy(held, out_ref.at[z], sems.at[2 + z]) for z in range(out_ref.shape[0])
    ]
    for store in stores:
        store.start()
    for store in stores:
        store.wait()


def stage_kernel(q_ref, g_ref, q_out, g_out, gt_out):
    q_out[...] = q_ref[...]
    g_out[...] = g_ref[...]
    for t in range(gt_out.shape[0]):
        gt_out[t] = flipped(g_ref[t * TILE : (t + 1) * TILE]).astype(HALF)


def flip_kernel(g_ref, gt_out):
    for t in range(gt_out.shape[0]):
        gt_out[t] = flipped(g_ref[t * TILE : (t + 1) * TILE]).astype(HALF)


def forward_kernel(
    info_ref, q_own, q_far, gt_own, gt_far, kv_ref, p_ref, o_own, o_far, stat_ref, vt_ref, s_ref,
    *, repeat, scale
):
    holders, _, rows, width = kv_ref.shape
    col_keys = holders * rows
    chunks = col_keys // TILE
    per = TILE // rows
    own_tiles = o_own.shape[0]
    blocks_here = rows // BLOCK
    ctx = info_ref[info_ref.shape[0] - 1]
    side = ctx % 2

    for c in range(chunks):
        vals = kv_ref[c * per : (c + 1) * per, 1].reshape(TILE, width)
        vt_ref[:width, c * TILE : (c + 1) * TILE] = flipped(vals).astype(HALF)
    vt_ref[width:] = jnp.ones((vt_ref.shape[0] - width, col_keys), HALF)
    diff = lax.broadcasted_iota(jnp.int32, (BLOCK, TILE), 0) - (
        lax.broadcasted_iota(jnp.int32, (BLOCK, TILE), 1) // repeat
    )

    def scores(tile):
        mine = tile < own_tiles
        device = ctx if mine else ctx + 1 - 2 * side
        local = tile % own_tiles
        token = local * (TILE // repeat)
        place = info_ref[device * blocks_here + token // BLOCK] * BLOCK + token % BLOCK
        q = (q_own if mine else q_far)[local * TILE : (local + 1) * TILE]
        top = None
        for c in range(chunks):
            keys = kv_ref[c * per : (c + 1) * per, 0].reshape(TILE, width)
            s = dot_nt(keys, q) * scale
            parts = []
            for b in range(TILE // BLOCK):
                at = c * (TILE // BLOCK) + b
                stored = ((at // blocks_here) * 2 + side) * blocks_here + at % blocks_here
                limit = place - info_ref[stored] * BLOCK
                parts.append(jnp.where(diff <= limit, s[b * BLOCK : (b + 1) * BLOCK], NEG_FILL))
            s = jnp.concatenate(parts, axis=0)
            s_ref[tile % 2, c * TILE : (c + 1) * TILE] = s
            here = jnp.max(s.reshape(TILE // 8, 8, TILE), axis=0)
            top = here if top is None else jnp.maximum(top, here)
        return jnp.max(top, axis=0, keepdims=True)

    def weigh(tile, top):
        out = None
        for c in range(chunks):
            span = slice(c * TILE, (c + 1) * TILE)
            p = jnp.exp2(s_ref[tile % 2, span] - top).astype(HALF)
            p_ref[span, tile * TILE : (tile + 1) * TILE] = p
            o = dot_nn(vt_ref[:, span], p)
            out = o if out is None else out + o
        total, out = out[width : width + 1], out[:width]
        mine = tile < own_tiles
        local = tile % own_tiles
        if mine:
            o_own[local] = out
        else:
            o_far[local] = out.astype(HALF)
        stat_ref[tile, 0:1] = top
        stat_ref[tile, 1:2] = total
        stat_ref[tile, 2:3] = jnp.sum(
            out * (gt_own if mine else gt_far)[local].astype(F32), axis=0, keepdims=True
        )
        stat_ref[tile, 3:8] = jnp.zeros((5, TILE), F32)

    top = scores(0)
    for tile in range(2 * own_tiles):
        later = scores(tile + 1) if tile + 1 < 2 * own_tiles else None
        weigh(tile, top)
        top = later


def backward_kernel(
    q_own, q_far, g_own, g_far, gt_own, gt_far, kv_ref, p_ref, here_ref, there_ref,
    dkv_ref, dq_own, dq_far, factor_ref, qs_ref, gs_ref, ds_ref, kt_ref, done_ref, sems,
    *, scale
):
    holders, _, rows, width = kv_ref.shape
    chunks = holders * rows // TILE
    per = TILE // rows
    own_tiles = gt_own.shape[0]
    tiles = 2 * own_tiles
    flip_keys(kv_ref, kt_ref)
    deltas, factors = [], []
    for tile in range(tiles):
        mine = tile < own_tiles
        local = tile % own_tiles
        other = (tile + own_tiles) % tiles
        top_a, sum_a, delta_a = (here_ref[tile, i : i + 1] for i in range(3))
        top_b, sum_b, delta_b = (there_ref[other, i : i + 1] for i in range(3))
        top = jnp.maximum(top_a, top_b)
        fa, fb = jnp.exp2(top_a - top), jnp.exp2(top_b - top)
        inverse = 1.0 / (sum_a * fa + sum_b * fb)
        factor = fa * inverse
        deltas.append((delta_a * fa + delta_b * fb) * inverse)
        factors.append(factor)
        if mine:
            factor_ref[tile, 0:1] = factor
            factor_ref[tile, 1:2] = fb * inverse
            factor_ref[tile, 2:8] = jnp.zeros((6, TILE), F32)
        down = jnp.broadcast_to(factor, (8, TILE)).T[:, 0:1]
        span = slice(local * TILE, (local + 1) * TILE)
        put = slice(tile * TILE, (tile + 1) * TILE)
        qs_ref[put] = ((q_own if mine else q_far)[span].astype(F32) * down).astype(HALF)
        gs_ref[put] = ((g_own if mine else g_far)[span].astype(F32) * down).astype(HALF)

    def grads(c):
        span = slice(c * TILE, (c + 1) * TILE)
        vals = kv_ref[c * per : (c + 1) * per, 1].reshape(TILE, width)
        for tile in range(tiles):
            mine = tile < own_tiles
            local = tile % own_tiles
            p = p_ref[span, tile * TILE : (tile + 1) * TILE].astype(F32)
            grad = p * (dot_nn(vals, (gt_own if mine else gt_far)[local]) - deltas[tile])
            ds_ref[span, tile * TILE : (tile + 1) * TILE] = grad.astype(HALF)

    copies = []
    grads(0)
    for c in range(chunks):
        span = slice(c * TILE, (c + 1) * TILE)
        if c + 1 < chunks:
            grads(c + 1)
        dv = dot_nn(p_ref[span], gs_ref[...])
        dk = dot_nn(ds_ref[span], qs_ref[...])
        for z in range(per):
            at = c * per + z
            done_ref[at, 0] = (dk[z * rows : (z + 1) * rows] * scale).astype(HALF)
            done_ref[at, 1] = dv[z * rows : (z + 1) * rows].astype(HALF)
            copies.append(pltpu.make_async_copy(done_ref.at[at], dkv_ref.at[at], sems.at[at]))
            copies[-1].start()
    for tile in range(tiles):
        dq = dot_nn(kt_ref[...], ds_ref[:, tile * TILE : (tile + 1) * TILE])
        dq = dq * (factors[tile] * scale)
        if tile < own_tiles:
            dq_own[tile] = dq
        else:
            dq_far[tile - own_tiles] = dq.astype(HALF)
    for copy in copies:
        copy.wait()


def flip_keys(kv_ref, kt_ref):
    holders, _, rows, width = kv_ref.shape
    per = TILE // rows
    for c in range(holders // per):
        keys = kv_ref[c * per : (c + 1) * per, 0].reshape(TILE, width)
        kt_ref[:, c * TILE : (c + 1) * TILE] = flipped(keys).astype(HALF)


def out_kernel(factor_ref, o_own, o_recv, out_ref):
    for t in range(o_own.shape[0]):
        o = o_own[t] * factor_ref[t, 0:1] + o_recv[t].astype(F32) * factor_ref[t, 1:2]
        out_ref[t * TILE : (t + 1) * TILE] = o.T.astype(HALF)


def join_kernel(dq_own, dq_recv, out_ref):
    for t in range(dq_own.shape[0]):
        dq = dq_own[t] + dq_recv[t].astype(F32)
        out_ref[t * TILE : (t + 1) * TILE] = dq.T.astype(HALF)


def total_kernel(terms_ref, dk_ref, dv_ref):
    for i, out in enumerate((dk_ref, dv_ref)):
        total = terms_ref[0, i].astype(F32)
        for z in range(1, terms_ref.shape[0]):
            total = total + terms_ref[z, i].astype(F32)
        out[...] = total.astype(HALF)


def call(kernel, name, ins, outs, scratch=(), flops=0, moved=0, exps=0, specs=None, out_specs=None, limit=24):
    return pl.pallas_call(
        kernel,
        in_specs=specs or [VMEM] * len(ins),
        out_specs=out_specs or [VMEM] * len(outs),
        out_shape=[jax.ShapeDtypeStruct(s, d) for s, d in outs],
        scratch_shapes=scratch,
        compiler_params=pltpu.CompilerParams(vmem_limit_bytes=limit * 2**20),
        cost_estimate=pl.CostEstimate(flops=flops, bytes_accessed=moved, transcendentals=exps),
        name=name,
    )(*ins)


def shards(queries, keys, values, output_gradient, block_order):
    tok, heads, width = queries.shape
    ctx_size = lax.axis_size("ctx")
    holders = ctx_size // 2
    columns = [[2 * z + x for z in range(holders)] for x in range(2)]
    swap = [(i, i ^ 1) for i in range(ctx_size)]
    own_rows = tok * heads
    own_tiles = own_rows // TILE
    tiles = 2 * own_tiles
    col_keys = holders * tok
    score_scale = 1.0 / math.sqrt(width)
    product = 2 * own_rows * col_keys * width
    flip_shape = (own_tiles, width, TILE)
    kv_shape = (holders, 2, tok, width)
    flat_shape = (own_rows, width)
    moved = own_rows * width * 8

    q = queries.reshape(flat_shape)
    g = output_gradient.reshape(flat_shape)
    (spread,) = call(
        spread_kernel, "spread", (keys.reshape(tok, width), values.reshape(tok, width)),
        [(kv_shape, HALF)], [pltpu.VMEM((2, tok, width), HALF), pltpu.SemaphoreType.DMA((2 + holders,))],
        moved=2 * col_keys * width, specs=[HBM, HBM], out_specs=[HBM], limit=60,
    )
    kv_all = lax.all_to_all(spread, "ctx", 0, 0, axis_index_groups=columns, tiled=True)
    q_far = lax.ppermute(q, "ctx", swap)
    g_far = lax.ppermute(g, "ctx", swap)
    info = jnp.concatenate([block_order, lax.axis_index("ctx").astype(jnp.int32).reshape(1)])
    q, g, gt_own = call(
        stage_kernel, "stage", (q, g), [(flat_shape, HALF), (flat_shape, HALF), (flip_shape, HALF)],
        moved=moved,
    )
    (gt_far,) = call(flip_kernel, "flip", (g_far,), [(flip_shape, HALF)], moved=moved)

    weights, o_own, o_far, stats = call(
        functools.partial(
            forward_kernel, repeat=heads, scale=score_scale * math.log2(math.e)
        ),
        "forward", (info, q, q_far, gt_own, gt_far, kv_all),
        [
            ((col_keys, 2 * own_rows), HALF),
            (flip_shape, F32),
            (flip_shape, HALF),
            ((tiles, 8, TILE), F32),
        ],
        [pltpu.VMEM((width + 16, col_keys), HALF), pltpu.VMEM((2, col_keys, TILE), F32)],
        flops=4 * product, exps=2 * own_rows * col_keys, specs=[SMEM] + [VMEM] * 5,
    )
    far_stats = lax.ppermute(stats, "ctx", swap)
    o_recv = lax.ppermute(o_far, "ctx", swap)

    dkv, dq_own, dq_far, factors = call(
        functools.partial(backward_kernel, scale=score_scale),
        "backward",
        (q, q_far, g, g_far, gt_own, gt_far, kv_all, weights, stats, far_stats),
        [
            (kv_shape, HALF),
            (flip_shape, F32),
            (flip_shape, HALF),
            ((own_tiles, 8, TILE), F32),
        ],
        [
            pltpu.VMEM((2 * own_rows, width), HALF),
            pltpu.VMEM((2 * own_rows, width), HALF),
            pltpu.VMEM((col_keys, 2 * own_rows), HALF),
            pltpu.VMEM((width, col_keys), HALF),
            pltpu.VMEM(kv_shape, HALF),
            pltpu.SemaphoreType.DMA((holders,)),
        ],
        flops=8 * product, out_specs=[HBM, VMEM, VMEM, VMEM],
    )
    terms = lax.all_to_all(dkv, "ctx", 0, 0, axis_index_groups=columns, tiled=True)

    dq_recv = lax.ppermute(dq_far, "ctx", swap)
    (attn_out,) = call(
        out_kernel, "out", (factors, o_own, o_recv), [(flat_shape, HALF)], moved=moved
    )
    (grad_queries,) = call(
        join_kernel, "join", (dq_own, dq_recv), [(flat_shape, HALF)], moved=moved
    )
    grad_keys, grad_values = call(
        total_kernel, "total", (terms,), [((tok, width), HALF), ((tok, width), HALF)],
        moved=2 * col_keys * width * 2,
    )
    return (
        attn_out.reshape(tok, heads, width),
        grad_queries.reshape(tok, heads, width),
        grad_keys.reshape(tok, 1, width),
        grad_values.reshape(tok, 1, width),
    )


def solution(mesh):
    tokens = P(("dp", "ctx"), "head", None)
    return jax.shard_map(
        shards,
        mesh=mesh,
        in_specs=(tokens, tokens, tokens, tokens, P("dp")),
        out_specs=(tokens, tokens, tokens, tokens),
        check_vma=False,
    )
```

time: 208 us -> 66.7 us (0.32)
  the two profiles are of different devices: /device:TPU:8 before, /device:TPU:52 now
where the time goes in v2:
time: 66.7 us; the launch traced here: 66.2 us
  starting transfers between devices  30 us (45%)
  waiting for transfers between devices  19.5 us (29%)
  Pallas kernels  12.6 us (19%)
  local copies, waits for them, and re-layouts  2.59 us (4%)
  between operations  0.74 us (1%)
  other arithmetic  0.73 us (1%)
    pallas_call x8, Pallas kernels, call(): pl.pallas_call(kernel, in_specs=specs or [VMEM] * len(ins), out_specs=out...  12.6 us
    all_to_all x1, starting transfers between devices, shards(): lax.all_to_all(spread, 'ctx', 0, 0, axis_index_groups=columns, tiled=True)  10.3 us
    all_to_all x1, starting transfers between devices, shards(): lax.all_to_all(dkv, 'ctx', 0, 0, axis_index_groups=columns, tiled=True)  4.92 us
    ppermute x1, waiting for transfers between devices, shards(): o_recv = lax.ppermute(o_far, 'ctx', swap)  4.76 us
    ppermute x1, waiting for transfers between devices, shards(): q_far = lax.ppermute(q, 'ctx', swap)  4.01 us
    ppermute x1, starting transfers between devices, shards(): far_stats = lax.ppermute(stats, 'ctx', swap)  3.12 us
    ppermute x1, starting transfers between devices, shards(): g_far = lax.ppermute(g, 'ctx', swap)  3.1 us
    ppermute x1, starting transfers between devices, shards(): o_recv = lax.ppermute(o_far, 'ctx', swap)  3.09 us
  transfers between devices with their start and end apart: 7, of which 7 were waited for; matrix products, arithmetic and copies ran while one was open for 1% of the time, Pallas kernels for 3%

profile of v2, /device:TPU:52, one launch (start us, length us, event | category | flops | bytes accessed | tf_op | source)
XLA Modules:
  0.0 66.2 jit_solution(140334793853553385)
XLA Ops:
  0.6 1.7 %spread.1 = bf16[8,2,128,128]{3,2,1,0:T(8,128)(2,1)} custom-call(bf16[128,128]{1,0:T(8,128)(2,1)} %bitcast.15, bf16[128,128]{1,0:T(8,128)(2,1)} %bitcast.16), custom_call_target="tpu_custom_call" | custom-call | bytes 262144 | tf_op jit(solution)/shard_map/spread/pallas_call | solution.py:233
  2.3 10.3 %all-to-all-start = ((bf16[8,2,128,128]{3,2,1,0:T(8,128)(2,1)}), bf16[8,2,128,128]{3,2,1,0:T(8,128)(2,1)S(1)}, u32[]{:S(2)}, u32[]{:S(2)}) async-start(bf16[8,2,128,128]{3,2,1,0:T(8,128)(2,1)} %spread.1), calls=%async_computation | async-start | bytes 1048576 | tf_op jit(solution)/shard_map/all_to_all | solution.py:269
  12.6 3.1 %collective-permute-start.1 = (bf16[1024,128]{1,0:T(8,128)(2,1)}, bf16[1024,128]{1,0:T(8,128)(2,1)S(1)}, u32[]{:S(2)}, u32[]{:S(2)}) collective-permute-start(bf16[1024,128]{1,0:T(8,128)(2,1)} %bitcast.9), channel_id=1, source_target_pairs={{0,1},{1,0},{2,3},{3,2},{4,5},{5,4},{6,7},{7,6},{8,9},{9,8},{10,11... | collective-permute-start | bytes 786440 | tf_op jit(solution)/shard_map/ppermute | solution.py:271
  15.7 2.7 %collective-permute-start = (bf16[1024,128]{1,0:T(8,128)(2,1)}, bf16[1024,128]{1,0:T(8,128)(2,1)S(1)}, u32[]{:S(2)}, u32[]{:S(2)}) collective-permute-start(bf16[1024,128]{1,0:T(8,128)(2,1)} %bitcast.11), channel_id=1, source_target_pairs={{0,1},{1,0},{2,3},{3,2},{4,5},{5,4},{6,7},{7,6},{8,9},{9,8},{10,11... | collective-permute-start | bytes 786440 | tf_op jit(solution)/shard_map/ppermute | solution.py:270
  18.5 0.0 copy-start
  18.5 0.9 %copy-done = bf16[128,8,128]{2,1,0:T(8,128)(2,1)S(1)} copy-done((bf16[128,8,128]{2,1,0:T(8,128)(2,1)S(1)}, bf16[128,8,128]{2,1,0:T(8,128)(2,1)}, u32[]{:S(2)}) %copy-start) | copy-done | bytes 262168
  19.4 0.0 copy-start.1
  19.4 0.9 %copy-done.1 = bf16[128,8,128]{2,1,0:T(8,128)(2,1)S(1)} copy-done((bf16[128,8,128]{2,1,0:T(8,128)(2,1)S(1)}, bf16[128,8,128]{2,1,0:T(8,128)(2,1)}, u32[]{:S(2)}) %copy-start.1) | copy-done | bytes 262168
  20.4 0.1 stage.1
  20.5 0.7 %pad_add_fusion.info_ref = s32[33]{0:T(128)S(1)} fusion(s32[1]{0:T(128)} %bitcast.4, s32[32]{0:T(128)} %param.9), kind=kLoop, calls=%fused_computation | loop fusion | flops 33 | bytes 264 | tf_op jit(solution)/shard_map/concatenate | solution.py:272
  21.3 2.7 %collective-permute-done.1.g_ref.g_far = bf16[1024,128]{1,0:T(8,128)(2,1)S(1)} collective-permute-done((bf16[1024,128]{1,0:T(8,128)(2,1)}, bf16[1024,128]{1,0:T(8,128)(2,1)S(1)}, u32[]{:S(2)}, u32[]{:S(2)}) %collective-permute-start.1) | collective-permute-done | bytes 262176 | tf_op jit(solution)/shard_map/ppermute | solution.py:271
  23.9 0.1 flip.1.gt_far
  24.1 4.0 %collective-permute-done.q_far = bf16[1024,128]{1,0:T(8,128)(2,1)S(1)} collective-permute-done((bf16[1024,128]{1,0:T(8,128)(2,1)}, bf16[1024,128]{1,0:T(8,128)(2,1)S(1)}, u32[]{:S(2)}, u32[]{:S(2)}) %collective-permute-start) | collective-permute-done | bytes 262176 | tf_op jit(solution)/shard_map/ppermute | solution.py:270
  28.1 2.0 %all-to-all-done.kv_ref = bf16[8,2,128,128]{3,2,1,0:T(8,128)(2,1)S(1)} async-done(((bf16[8,2,128,128]{3,2,1,0:T(8,128)(2,1)}), bf16[8,2,128,128]{3,2,1,0:T(8,128)(2,1)S(1)}, u32[]{:S(2)}, u32[]{:S(2)}) %all-to-all-start) | async-done | bytes 524320 | tf_op jit(solution)/shard_map/all_to_all | solution.py:269
  30.1 4.0 %forward.1 = (bf16[1024,2048]{1,0:T(8,128)(2,1)S(1)}, f32[4,128,256]{2,1,0:T(8,128)S(1)}, bf16[4,128,256]{2,1,0:T(8,128)(2,1)S(1)}, f32[8,8,256]{2,1,0:T(8,128)S(1)}) custom-call(s32[33]{0:T(128)S(1)} %pad_add_fusion.info_ref, bf16[1024,128]{1,0:T(8,128)(2,1)S(1)} %get-tuple-element.17.q_own, bf16[1024,128]{1,0:T(8,128)(2,1)S(1)} %collective-permute-done.q_far, ...), custom_call_target="tpu_custom_call" | custom-call | flops 1073741824 | tf_op jit(solution)/shard_map/forward/pallas_call | solution.py:233
  34.1 3.1 %collective-permute-start.2 = (f32[8,8,256]{2,1,0:T(8,128)S(1)}, f32[8,8,256]{2,1,0:T(8,128)S(1)}, u32[]{:S(2)}, u32[]{:S(2)}) collective-permute-start(f32[8,8,256]{2,1,0:T(8,128)S(1)} %get-tuple-element.21.here_ref), channel_id=1, source_target_pairs={{0,1},{1,0},{2,3},{3,2},{4,5},{5,4},{6,7},{7,6},{8,9},{9,8},{10,11... | collective-permute-start | bytes 196616 | tf_op jit(solution)/shard_map/ppermute | solution.py:293
  37.2 3.0 %collective-permute-done.2.there_ref = f32[8,8,256]{2,1,0:T(8,128)S(1)} collective-permute-done((f32[8,8,256]{2,1,0:T(8,128)S(1)}, f32[8,8,256]{2,1,0:T(8,128)S(1)}, u32[]{:S(2)}, u32[]{:S(2)}) %collective-permute-start.2) | collective-permute-done | bytes 65568 | tf_op jit(solution)/shard_map/ppermute | solution.py:293
  40.3 4.3 %backward.1 = (bf16[8,2,128,128]{3,2,1,0:T(8,128)(2,1)}, f32[4,128,256]{2,1,0:T(8,128)S(1)}, bf16[4,128,256]{2,1,0:T(8,128)(2,1)S(1)}, f32[4,8,256]{2,1,0:T(8,128)S(1)}) custom-call(bf16[1024,128]{1,0:T(8,128)(2,1)S(1)} %get-tuple-element.17.q_own, bf16[1024,128]{1,0:T(8,128)(2,1)S(1)} %collective-permute-done.q_far, ...), custom_call_target="tpu_custom_call" | custom-call | flops 2147483648 | tf_op jit(solution)/shard_map/backward/pallas_call | solution.py:233
  44.6 0.0 copy-start.2
  44.6 0.7 %copy-done.2 = bf16[4,128,256]{2,1,0:T(8,128)(2,1)} copy-done((bf16[4,128,256]{2,1,0:T(8,128)(2,1)}, bf16[4,128,256]{2,1,0:T(8,128)(2,1)S(1)}, u32[]{:S(2)}) %copy-start.2) | copy-done | bytes 262168
  45.3 4.9 %all-to-all-start.1 = ((bf16[8,2,128,128]{3,2,1,0:T(8,128)(2,1)}), bf16[8,2,128,128]{3,2,1,0:T(8,128)(2,1)S(1)}, u32[]{:S(2)}, u32[]{:S(2)}) async-start(bf16[8,2,128,128]{3,2,1,0:T(8,128)(2,1)} %get-tuple-element.27), calls=%async_computation.1 | async-start | bytes 1048576 | tf_op jit(solution)/shard_map/all_to_all | solution.py:316
  50.2 3.1 %collective-permute-start.3 = (bf16[4,128,256]{2,1,0:T(8,128)(2,1)S(1)}, bf16[4,128,256]{2,1,0:T(8,128)(2,1)S(1)}, u32[]{:S(2)}, u32[]{:S(2)}) collective-permute-start(bf16[4,128,256]{2,1,0:T(8,128)(2,1)S(1)} %get-tuple-element.24), channel_id=1, source_target_pairs={{0,1},{1,0},{2,3},{3,2},{4,5},{5,4},{6,7},{7,6},{8,9},{9,8},{10,11... | collective-permute-start | bytes 786440 | tf_op jit(solution)/shard_map/ppermute | solution.py:294
  53.3 2.7 %collective-permute-start.4 = (bf16[4,128,256]{2,1,0:T(8,128)(2,1)}, bf16[4,128,256]{2,1,0:T(8,128)(2,1)S(1)}, u32[]{:S(2)}, u32[]{:S(2)}) collective-permute-start(bf16[4,128,256]{2,1,0:T(8,128)(2,1)} %copy-done.2), channel_id=1, source_target_pairs={{0,1},{1,0},{2,3},{3,2},{4,5},{5,4},{6,7},{7,6},{8,9},{9,8},{10,11... | collective-permute-start | bytes 786440 | tf_op jit(solution)/shard_map/ppermute | solution.py:318
  56.1 4.8 %collective-permute-done.3.o_recv = bf16[4,128,256]{2,1,0:T(8,128)(2,1)S(1)} collective-permute-done((bf16[4,128,256]{2,1,0:T(8,128)(2,1)S(1)}, bf16[4,128,256]{2,1,0:T(8,128)(2,1)S(1)}, u32[]{:S(2)}, u32[]{:S(2)}) %collective-permute-start.3) | collective-permute-done | bytes 262176 | tf_op jit(solution)/shard_map/ppermute | solution.py:294
  60.8 0.9 %out.1 = bf16[1024,128]{1,0:T(8,128)(2,1)} custom-call(f32[4,8,256]{2,1,0:T(8,128)S(1)} %get-tuple-element.22.factor_ref, f32[4,128,256]{2,1,0:T(8,128)S(1)} %get-tuple-element.23.o_own, bf16[4,128,256]{2,1,0:T(8,128)(2,1)S(1)} %collective-permute-done.3.o_recv), custom_call_target="tpu_custom_call" | custom-call | bytes 1048576 | tf_op jit(solution)/shard_map/out/pallas_call | solution.py:233
  61.7 2.0 %collective-permute-done.4.dq_recv = bf16[4,128,256]{2,1,0:T(8,128)(2,1)S(1)} collective-permute-done((bf16[4,128,256]{2,1,0:T(8,128)(2,1)}, bf16[4,128,256]{2,1,0:T(8,128)(2,1)S(1)}, u32[]{:S(2)}, u32[]{:S(2)}) %collective-permute-start.4) | collective-permute-done | bytes 262176 | tf_op jit(solution)/shard_map/ppermute | solution.py:318
  63.6 0.8 %join.1 = bf16[1024,128]{1,0:T(8,128)(2,1)} custom-call(f32[4,128,256]{2,1,0:T(8,128)S(1)} %get-tuple-element.25.dq_own, bf16[4,128,256]{2,1,0:T(8,128)(2,1)S(1)} %collective-permute-done.4.dq_recv), custom_call_target="tpu_custom_call" | custom-call | bytes 1048576 | tf_op jit(solution)/shard_map/join/pallas_call | solution.py:233
  64.5 1.1 %all-to-all-done.1.terms_ref = bf16[8,2,128,128]{3,2,1,0:T(8,128)(2,1)S(1)} async-done(((bf16[8,2,128,128]{3,2,1,0:T(8,128)(2,1)}), bf16[8,2,128,128]{3,2,1,0:T(8,128)(2,1)S(1)}, u32[]{:S(2)}, u32[]{:S(2)}) %all-to-all-start.1) | async-done | bytes 524320 | tf_op jit(solution)/shard_map/all_to_all | solution.py:316
  65.5 0.7 %total.1 = (bf16[128,128]{1,0:T(8,128)(2,1)}, bf16[128,128]{1,0:T(8,128)(2,1)}) custom-call(bf16[8,2,128,128]{3,2,1,0:T(8,128)(2,1)S(1)} %all-to-all-done.1.terms_ref), custom_call_target="tpu_custom_call" | custom-call | bytes 524288 | tf_op jit(solution)/shard_map/total/pallas_call | solution.py:233
Async XLA Ops:
  2.3 27.8 %all-to-all-start = ((bf16[8,2,128,128]{3,2,1,0:T(8,128)(2,1)}), bf16[8,2,128,128]{3,2,1,0:T(8,128)(2,1)S(1)}, u32[]{:S(2)}, u32[]{:S(2)}) async-start(bf16[8,2,128,128]{3,2,1,0:T(8,128)(2,1)} %spread.1), calls=%async_computation | async-start | bytes 1048576 | tf_op jit(solution)/shard_map/all_to_all | solution.py:269
  12.6 11.3 %collective-permute-start.1 = (bf16[1024,128]{1,0:T(8,128)(2,1)}, bf16[1024,128]{1,0:T(8,128)(2,1)S(1)}, u32[]{:S(2)}, u32[]{:S(2)}) collective-permute-start(bf16[1024,128]{1,0:T(8,128)(2,1)} %bitcast.9), channel_id=1, source_target_pairs={{0,1},{1,0},{2,3},{3,2},{4,5},{5,4},{6,7},{7,6},{8,9},{9,8},{10,11... | collective-permute-start | bytes 786440 | tf_op jit(solution)/shard_map/ppermute | solution.py:271
  15.7 12.4 %collective-permute-start = (bf16[1024,128]{1,0:T(8,128)(2,1)}, bf16[1024,128]{1,0:T(8,128)(2,1)S(1)}, u32[]{:S(2)}, u32[]{:S(2)}) collective-permute-start(bf16[1024,128]{1,0:T(8,128)(2,1)} %bitcast.11), channel_id=1, source_target_pairs={{0,1},{1,0},{2,3},{3,2},{4,5},{5,4},{6,7},{7,6},{8,9},{9,8},{10,11... | collective-permute-start | bytes 786440 | tf_op jit(solution)/shard_map/ppermute | solution.py:270
  18.5 1.0 %copy-start = (bf16[128,8,128]{2,1,0:T(8,128)(2,1)S(1)}, bf16[128,8,128]{2,1,0:T(8,128)(2,1)}, u32[]{:S(2)}) copy-start(bf16[128,8,128]{2,1,0:T(8,128)(2,1)} %param.8) | copy-start | bytes 786436
  19.4 0.9 %copy-start.1 = (bf16[128,8,128]{2,1,0:T(8,128)(2,1)S(1)}, bf16[128,8,128]{2,1,0:T(8,128)(2,1)}, u32[]{:S(2)}) copy-start(bf16[128,8,128]{2,1,0:T(8,128)(2,1)} %param.5) | copy-start | bytes 786436
  34.1 6.2 %collective-permute-start.2 = (f32[8,8,256]{2,1,0:T(8,128)S(1)}, f32[8,8,256]{2,1,0:T(8,128)S(1)}, u32[]{:S(2)}, u32[]{:S(2)}) collective-permute-start(f32[8,8,256]{2,1,0:T(8,128)S(1)} %get-tuple-element.21.here_ref), channel_id=1, source_target_pairs={{0,1},{1,0},{2,3},{3,2},{4,5},{5,4},{6,7},{7,6},{8,9},{9,8},{10,11... | collective-permute-start | bytes 196616 | tf_op jit(solution)/shard_map/ppermute | solution.py:293
  44.6 0.7 %copy-start.2 = (bf16[4,128,256]{2,1,0:T(8,128)(2,1)}, bf16[4,128,256]{2,1,0:T(8,128)(2,1)S(1)}, u32[]{:S(2)}) copy-start(bf16[4,128,256]{2,1,0:T(8,128)(2,1)S(1)} %get-tuple-element.26) | copy-start | bytes 786436
  45.3 20.2 %all-to-all-start.1 = ((bf16[8,2,128,128]{3,2,1,0:T(8,128)(2,1)}), bf16[8,2,128,128]{3,2,1,0:T(8,128)(2,1)S(1)}, u32[]{:S(2)}, u32[]{:S(2)}) async-start(bf16[8,2,128,128]{3,2,1,0:T(8,128)(2,1)} %get-tuple-element.27), calls=%async_computation.1 | async-start | bytes 1048576 | tf_op jit(solution)/shard_map/all_to_all | solution.py:316
  50.2 10.6 %collective-permute-start.3 = (bf16[4,128,256]{2,1,0:T(8,128)(2,1)S(1)}, bf16[4,128,256]{2,1,0:T(8,128)(2,1)S(1)}, u32[]{:S(2)}, u32[]{:S(2)}) collective-permute-start(bf16[4,128,256]{2,1,0:T(8,128)(2,1)S(1)} %get-tuple-element.24), channel_id=1, source_target_pairs={{0,1},{1,0},{2,3},{3,2},{4,5},{5,4},{6,7},{7,6},{8,9},{9,8},{10,11... | collective-permute-start | bytes 786440 | tf_op jit(solution)/shard_map/ppermute | solution.py:294
  53.3 10.3 %collective-permute-start.4 = (bf16[4,128,256]{2,1,0:T(8,128)(2,1)}, bf16[4,128,256]{2,1,0:T(8,128)(2,1)S(1)}, u32[]{:S(2)}, u32[]{:S(2)}) collective-permute-start(bf16[4,128,256]{2,1,0:T(8,128)(2,1)} %copy-done.2), channel_id=1, source_target_pairs={{0,1},{1,0},{2,3},{3,2},{4,5},{5,4},{6,7},{7,6},{8,9},{9,8},{10,11... | collective-permute-start | bytes 786440 | tf_op jit(solution)/shard_map/ppermute | solution.py:318

commit v3 on v2

--- a/solution.py
+++ b/solution.py
@@ -47,56 +47,65 @@
         store.wait()
 
 
-def stage_kernel(q_ref, g_ref, q_out, g_out, gt_out):
-    q_out[...] = q_ref[...]
-    g_out[...] = g_ref[...]
-    for t in range(gt_out.shape[0]):
-        gt_out[t] = flipped(g_ref[t * TILE : (t + 1) * TILE]).astype(HALF)
-
-
-def flip_kernel(g_ref, gt_out):
-    for t in range(gt_out.shape[0]):
-        gt_out[t] = flipped(g_ref[t * TILE : (t + 1) * TILE]).astype(HALF)
+def flip_rows(source, out_ref):
+    for t in range(out_ref.shape[0]):
+        out_ref[t] = flipped(source[t * TILE : (t + 1) * TILE]).astype(HALF)
+
+
+def stage_kernel(info_ref, q_ref, g_ref, qt_out, gt_out, limit_ref, side_ref, *, repeat):
+    own_tiles = gt_out.shape[0]
+    tiles, blocks, _ = limit_ref.shape
+    last = info_ref.shape[0] - 1
+    ctx = info_ref[last]
+    side = ctx % 2
+    blocks_here = own_tiles * TILE // repeat // BLOCK
+    flip_rows(q_ref, qt_out)
+    flip_rows(g_ref, gt_out)
+    token_of = lax.broadcasted_iota(jnp.int32, (1, TILE), 1) // repeat
+    for t in range(tiles):
+        device = ctx if t < own_tiles else ctx + 1 - 2 * side
+        token = (t % own_tiles) * (TILE // repeat)
+        place = info_ref[device * blocks_here + token // BLOCK] * BLOCK + token % BLOCK
+        for b in range(blocks):
+            stored = ((b // blocks_here) * 2 + side) * blocks_here + b % blocks_here
+            limit_ref[t, b : b + 1] = token_of + (place - info_ref[stored] * BLOCK)
+    side_ref[...] = jnp.zeros(side_ref.shape, jnp.int32) + side
+
+
+def flip_kernel(q_ref, g_ref, qt_out, gt_out):
+    flip_rows(q_ref, qt_out)
+    flip_rows(g_ref, gt_out)
 
 
 def forward_kernel(
-    info_ref, q_own, q_far, gt_own, gt_far, kv_ref, p_ref, o_own, o_far, stat_ref, vt_ref, s_ref,
-    *, repeat, scale
+    limit_ref, qt_own, qt_far, gt_own, gt_far, kv_ref, p_ref, o_own, o_far, stat_ref, vt_ref, s_ref,
+    *, scale
 ):
     holders, _, rows, width = kv_ref.shape
     col_keys = holders * rows
     chunks = col_keys // TILE
     per = TILE // rows
     own_tiles = o_own.shape[0]
-    blocks_here = rows // BLOCK
-    ctx = info_ref[info_ref.shape[0] - 1]
-    side = ctx % 2
 
     for c in range(chunks):
         vals = kv_ref[c * per : (c + 1) * per, 1].reshape(TILE, width)
         vt_ref[:width, c * TILE : (c + 1) * TILE] = flipped(vals).astype(HALF)
     vt_ref[width:] = jnp.ones((vt_ref.shape[0] - width, col_keys), HALF)
-    diff = lax.broadcasted_iota(jnp.int32, (BLOCK, TILE), 0) - (
-        lax.broadcasted_iota(jnp.int32, (BLOCK, TILE), 1) // repeat
-    )
+    key_of = lax.broadcasted_iota(jnp.int32, (BLOCK, TILE), 0)
 
     def scores(tile):
         mine = tile < own_tiles
-        device = ctx if mine else ctx + 1 - 2 * side
         local = tile % own_tiles
-        token = local * (TILE // repeat)
-        place = info_ref[device * blocks_here + token // BLOCK] * BLOCK + token % BLOCK
-        q = (q_own if mine else q_far)[local * TILE : (local + 1) * TILE]
+        qt = (qt_own if mine else qt_far)[local]
         top = None
         for c in range(chunks):
             keys = kv_ref[c * per : (c + 1) * per, 0].reshape(TILE, width)
-            s = dot_nt(keys, q) * scale
+            s = dot_nn(keys, qt) * scale
             parts = []
             for b in range(TILE // BLOCK):
                 at = c * (TILE // BLOCK) + b
-                stored = ((at // blocks_here) * 2 + side) * blocks_here + at % blocks_here
-                limit = place - info_ref[stored] * BLOCK
-                parts.append(jnp.where(diff <= limit, s[b * BLOCK : (b + 1) * BLOCK], NEG_FILL))
+                seen = key_of <= limit_ref[tile, at : at + 1]
+                parts.append(jnp.where(seen, s[b * BLOCK : (b + 1) * BLOCK], NEG_FILL))
             s = jnp.concatenate(parts, axis=0)
             s_ref[tile % 2, c * TILE : (c + 1) * TILE] = s
             here = jnp.max(s.reshape(TILE // 8, 8, TILE), axis=0)
@@ -104,13 +113,11 @@
         return jnp.max(top, axis=0, keepdims=True)
 
     def weigh(tile, top):
-        out = None
+        put = slice(tile * TILE, (tile + 1) * TILE)
         for c in range(chunks):
             span = slice(c * TILE, (c + 1) * TILE)
-            p = jnp.exp2(s_ref[tile % 2, span] - top).astype(HALF)
-            p_ref[span, tile * TILE : (tile + 1) * TILE] = p
-            o = dot_nn(vt_ref[:, span], p)
-            out = o if out is None else out + o
+            p_ref[span, put] = jnp.exp2(s_ref[tile % 2, span] - top).astype(HALF)
+        out = dot_nn(vt_ref[...], p_ref[:, put])
         total, out = out[width : width + 1], out[:width]
         mine = tile < own_tiles
         local = tile % own_tiles
@@ -118,12 +125,10 @@
             o_own[local] = out
         else:
             o_far[local] = out.astype(HALF)
-        stat_ref[tile, 0:1] = top
-        stat_ref[tile, 1:2] = total
-        stat_ref[tile, 2:3] = jnp.sum(
+        delta = jnp.sum(
             out * (gt_own if mine else gt_far)[local].astype(F32), axis=0, keepdims=True
         )
-        stat_ref[tile, 3:8] = jnp.zeros((5, TILE), F32)
+        stat_ref[3 * tile : 3 * tile + 3] = jnp.concatenate([top, total, delta], axis=0)
 
     top = scores(0)
     for tile in range(2 * own_tiles):
@@ -133,7 +138,7 @@
 
 
 def backward_kernel(
-    q_own, q_far, g_own, g_far, gt_own, gt_far, kv_ref, p_ref, here_ref, there_ref,
+    side_ref, qt_own, qt_far, gt_own, gt_far, kv_ref, p_ref, stat_ref,
     dkv_ref, dq_own, dq_far, factor_ref, qs_ref, gs_ref, ds_ref, kt_ref, done_ref, sems,
     *, scale
 ):
@@ -144,27 +149,35 @@
     tiles = 2 * own_tiles
     flip_keys(kv_ref, kt_ref)
     deltas, factors = [], []
+    right = side_ref[0:1] > 0
     for tile in range(tiles):
         mine = tile < own_tiles
         local = tile % own_tiles
         other = (tile + own_tiles) % tiles
-        top_a, sum_a, delta_a = (here_ref[tile, i : i + 1] for i in range(3))
-        top_b, sum_b, delta_b = (there_ref[other, i : i + 1] for i in range(3))
+        here, there = (
+            [jnp.where(right, stat_ref[1 - s, at], stat_ref[s, at]) for at in spans]
+            for s, spans in (
+                (0, [slice(3 * tile + i, 3 * tile + i + 1) for i in range(3)]),
+                (1, [slice(3 * other + i, 3 * other + i + 1) for i in range(3)]),
+            )
+        )
+        top_a, sum_a, delta_a = here
+        top_b, sum_b, delta_b = there
         top = jnp.maximum(top_a, top_b)
         fa, fb = jnp.exp2(top_a - top), jnp.exp2(top_b - top)
         inverse = 1.0 / (sum_a * fa + sum_b * fb)
         factor = fa * inverse
         deltas.append((delta_a * fa + delta_b * fb) * inverse)
         factors.append(factor)
-        if mine:
-            factor_ref[tile, 0:1] = factor
-            factor_ref[tile, 1:2] = fb * inverse
-            factor_ref[tile, 2:8] = jnp.zeros((6, TILE), F32)
-        down = jnp.broadcast_to(factor, (8, TILE)).T[:, 0:1]
-        span = slice(local * TILE, (local + 1) * TILE)
+        factor_ref[tile, 0:1] = factor
+        factor_ref[tile, 1:2] = fb * inverse
+        factor_ref[tile, 2:8] = jnp.zeros((6, TILE), F32)
         put = slice(tile * TILE, (tile + 1) * TILE)
-        qs_ref[put] = ((q_own if mine else q_far)[span].astype(F32) * down).astype(HALF)
-        gs_ref[put] = ((g_own if mine else g_far)[span].astype(F32) * down).astype(HALF)
+        for source, target in (
+            (qt_own if mine else qt_far, qs_ref),
+            (gt_own if mine else gt_far, gs_ref),
+        ):
+            target[put] = (source[local].astype(F32) * factor).T.astype(HALF)
 
     def grads(c):
         span = slice(c * TILE, (c + 1) * TILE)
@@ -192,11 +205,8 @@
             copies[-1].start()
     for tile in range(tiles):
         dq = dot_nn(kt_ref[...], ds_ref[:, tile * TILE : (tile + 1) * TILE])
-        dq = dq * (factors[tile] * scale)
-        if tile < own_tiles:
-            dq_own[tile] = dq
-        else:
-            dq_far[tile - own_tiles] = dq.astype(HALF)
+        dq = (dq * (factors[tile] * scale)).astype(HALF)
+        (dq_own if tile < own_tiles else dq_far)[tile % own_tiles] = dq
     for copy in copies:
         copy.wait()
 
@@ -215,9 +225,13 @@
         out_ref[t * TILE : (t + 1) * TILE] = o.T.astype(HALF)
 
 
+def pack_kernel(dq_ref, out_ref):
+    out_ref[...] = dq_ref[...]
+
+
 def join_kernel(dq_own, dq_recv, out_ref):
     for t in range(dq_own.shape[0]):
-        dq = dq_own[t] + dq_recv[t].astype(F32)
+        dq = dq_own[t].astype(F32) + dq_recv[t].astype(F32)
         out_ref[t * TILE : (t + 1) * TILE] = dq.T.astype(HALF)
 
 
@@ -229,7 +243,7 @@
         out[...] = total.astype(HALF)
 
 
-def call(kernel, name, ins, outs, scratch=(), flops=0, moved=0, exps=0, specs=None, out_specs=None, limit=24):
+def call(kernel, name, ins, outs, scratch=(), flops=0, moved=0, exps=0, specs=None, out_specs=None, limit=8):
     return pl.pallas_call(
         kernel,
         in_specs=specs or [VMEM] * len(ins),
@@ -270,38 +284,45 @@
     q_far = lax.ppermute(q, "ctx", swap)
     g_far = lax.ppermute(g, "ctx", swap)
     info = jnp.concatenate([block_order, lax.axis_index("ctx").astype(jnp.int32).reshape(1)])
-    q, g, gt_own = call(
-        stage_kernel, "stage", (q, g), [(flat_shape, HALF), (flat_shape, HALF), (flip_shape, HALF)],
-        moved=moved,
-    )
-    (gt_far,) = call(flip_kernel, "flip", (g_far,), [(flip_shape, HALF)], moved=moved)
+    pairs = [[2 * z, 2 * z + 1] for z in range(holders)]
+    qt_own, gt_own, limits, side = call(
+        functools.partial(stage_kernel, repeat=heads), "stage", (info, q, g),
+        [
+            (flip_shape, HALF),
+            (flip_shape, HALF),
+            ((tiles, col_keys // BLOCK, TILE), jnp.int32),
+            ((8, TILE), jnp.int32),
+        ],
+        moved=moved, specs=[SMEM, VMEM, VMEM],
+    )
+    qt_far, gt_far = call(
+        flip_kernel, "flip", (q_far, g_far), [(flip_shape, HALF)] * 2, moved=moved
+    )
 
     weights, o_own, o_far, stats = call(
-        functools.partial(
-            forward_kernel, repeat=heads, scale=score_scale * math.log2(math.e)
-        ),
-        "forward", (info, q, q_far, gt_own, gt_far, kv_all),
+        functools.partial(forward_kernel, scale=score_scale * math.log2(math.e)),
+        "forward", (limits, qt_own, qt_far, gt_own, gt_far, kv_all),
         [
             ((col_keys, 2 * own_rows), HALF),
             (flip_shape, F32),
             (flip_shape, HALF),
-            ((tiles, 8, TILE), F32),
+            ((3 * tiles, TILE), F32),
         ],
         [pltpu.VMEM((width + 16, col_keys), HALF), pltpu.VMEM((2, col_keys, TILE), F32)],
-        flops=4 * product, exps=2 * own_rows * col_keys, specs=[SMEM] + [VMEM] * 5,
-    )
-    far_stats = lax.ppermute(stats, "ctx", swap)
+        flops=4 * product, exps=2 * own_rows * col_keys, limit=12,
+    )
+    both = lax.all_gather(stats, "ctx", axis_index_groups=pairs)
     o_recv = lax.ppermute(o_far, "ctx", swap)
 
     dkv, dq_own, dq_far, factors = call(
         functools.partial(backward_kernel, scale=score_scale),
         "backward",
-        (q, q_far, g, g_far, gt_own, gt_far, kv_all, weights, stats, far_stats),
+        (side, qt_own, qt_far, gt_own, gt_far, kv_all, weights, both),
         [
             (kv_shape, HALF),
-            (flip_shape, F32),
-            (flip_shape, HALF),
-            ((own_tiles, 8, TILE), F32),
+            (flip_shape, HALF),
+            (flip_shape, HALF),
+            ((tiles, 8, TILE), F32),
         ],
         [
             pltpu.VMEM((2 * own_rows, width), HALF),
@@ -311,11 +332,14 @@
             pltpu.VMEM(kv_shape, HALF),
             pltpu.SemaphoreType.DMA((holders,)),
         ],
-        flops=8 * product, out_specs=[HBM, VMEM, VMEM, VMEM],
+        flops=8 * product, limit=16, out_specs=[HBM, VMEM, VMEM, VMEM],
     )
     terms = lax.all_to_all(dkv, "ctx", 0, 0, axis_index_groups=columns, tiled=True)
 
-    dq_recv = lax.ppermute(dq_far, "ctx", swap)
+    (dq_sent,) = call(
+        pack_kernel, "pack", (dq_far,), [(flip_shape, HALF)], moved=own_rows * width * 4
+    )
+    dq_recv = lax.ppermute(dq_sent, "ctx", swap)
     (attn_out,) = call(
         out_kernel, "out", (factors, o_own, o_recv), [(flat_shape, HALF)], moved=moved
     )

time: 66.7 us -> 64 us (0.960)
  the two profiles are of different devices: /device:TPU:52 before, /device:TPU:58 now
where the time goes in v3:
time: 64 us; the launch traced here: 63.5 us
  starting transfers between devices  27.2 us (42%)
  waiting for transfers between devices  15.5 us (24%)
  Pallas kernels  13 us (20%)
  blocking collectives  4.5 us (7%)
  local copies, waits for them, and re-layouts  1.9 us (3%)
  other arithmetic  0.73 us (1%)
  between operations  0.72 us (1%)
    pallas_call x9, Pallas kernels, call(): pl.pallas_call(kernel, in_specs=specs or [VMEM] * len(ins), out_specs=out...  13 us
    all_to_all x1, starting transfers between devices, shards(): lax.all_to_all(spread, 'ctx', 0, 0, axis_index_groups=columns, tiled=True)  10.3 us
    all_to_all x1, starting transfers between devices, shards(): lax.all_to_all(dkv, 'ctx', 0, 0, axis_index_groups=columns, tiled=True)  5.15 us
    all_gather x1, blocking collectives, shards(): both = lax.all_gather(stats, 'ctx', axis_index_groups=pairs)  4.5 us
    ppermute x1, waiting for transfers between devices, shards(): dq_recv = lax.ppermute(dq_sent, 'ctx', swap)  4.3 us
    ppermute x1, waiting for transfers between devices, shards(): g_far = lax.ppermute(g, 'ctx', swap)  4.15 us
    ppermute x1, starting transfers between devices, shards(): g_far = lax.ppermute(g, 'ctx', swap)  3.4 us
    ppermute x1, starting transfers between devices, shards(): o_recv = lax.ppermute(o_far, 'ctx', swap)  3.39 us
  transfers between devices with their start and end apart: 6, of which 6 were waited for; matrix products, arithmetic and copies ran while one was open for 1% of the time, Pallas kernels for 4%

profile of v3, /device:TPU:58, one launch (start us, length us, event | category | flops | bytes accessed | tf_op | source)
XLA Modules:
  0.0 63.5 jit_solution(1844908037448899766)
XLA Ops:
  0.6 1.7 %spread.1 = bf16[8,2,128,128]{3,2,1,0:T(8,128)(2,1)} custom-call(bf16[128,128]{1,0:T(8,128)(2,1)} %bitcast.17, bf16[128,128]{1,0:T(8,128)(2,1)} %bitcast.18), custom_call_target="tpu_custom_call" | custom-call | bytes 262144 | tf_op jit(solution)/shard_map/spread/pallas_call | solution.py:247
  2.3 10.3 %all-to-all-start = ((bf16[8,2,128,128]{3,2,1,0:T(8,128)(2,1)}), bf16[8,2,128,128]{3,2,1,0:T(8,128)(2,1)S(1)}, u32[]{:S(2)}, u32[]{:S(2)}) async-start(bf16[8,2,128,128]{3,2,1,0:T(8,128)(2,1)} %spread.1), calls=%async_computation | async-start | bytes 1048576 | tf_op jit(solution)/shard_map/all_to_all | solution.py:283
  12.6 2.4 %collective-permute-start = (bf16[1024,128]{1,0:T(8,128)(2,1)}, bf16[1024,128]{1,0:T(8,128)(2,1)S(1)}, u32[]{:S(2)}, u32[]{:S(2)}) collective-permute-start(bf16[1024,128]{1,0:T(8,128)(2,1)} %bitcast.10), channel_id=1, source_target_pairs={{0,1},{1,0},{2,3},{3,2},{4,5},{5,4},{6,7},{7,6},{8,9},{9,8},{10,11... | collective-permute-start | bytes 786440 | tf_op jit(solution)/shard_map/ppermute | solution.py:284
  15.1 3.4 %collective-permute-start.1 = (bf16[1024,128]{1,0:T(8,128)(2,1)}, bf16[1024,128]{1,0:T(8,128)(2,1)S(1)}, u32[]{:S(2)}, u32[]{:S(2)}) collective-permute-start(bf16[1024,128]{1,0:T(8,128)(2,1)} %bitcast.12), channel_id=1, source_target_pairs={{0,1},{1,0},{2,3},{3,2},{4,5},{5,4},{6,7},{7,6},{8,9},{9,8},{10,11... | collective-permute-start | bytes 786440 | tf_op jit(solution)/shard_map/ppermute | solution.py:285
  18.5 0.7 %pad_add_fusion.info_ref = s32[33]{0:T(128)S(1)} fusion(s32[1]{0:T(128)} %bitcast, s32[32]{0:T(128)} %param.9), kind=kLoop, calls=%fused_computation | loop fusion | flops 33 | bytes 264 | tf_op jit(solution)/shard_map/concatenate | solution.py:286
  19.2 0.0 copy-start
  19.2 0.9 %copy-done = bf16[128,8,128]{2,1,0:T(8,128)(2,1)S(1)} copy-done((bf16[128,8,128]{2,1,0:T(8,128)(2,1)S(1)}, bf16[128,8,128]{2,1,0:T(8,128)(2,1)}, u32[]{:S(2)}) %copy-start) | copy-done | bytes 262168
  20.2 0.0 copy-start.1
  20.2 0.9 %copy-done.1 = bf16[128,8,128]{2,1,0:T(8,128)(2,1)S(1)} copy-done((bf16[128,8,128]{2,1,0:T(8,128)(2,1)S(1)}, bf16[128,8,128]{2,1,0:T(8,128)(2,1)}, u32[]{:S(2)}) %copy-start.1) | copy-done | bytes 262168
  21.1 0.8 %stage.1 = (bf16[4,128,256]{2,1,0:T(8,128)(2,1)S(1)}, bf16[4,128,256]{2,1,0:T(8,128)(2,1)S(1)}, s32[8,16,256]{2,1,0:T(8,128)S(1)}, s32[8,256]{1,0:T(8,128)S(1)}) custom-call(s32[33]{0:T(128)S(1)} %pad_add_fusion.info_ref, bf16[1024,128]{1,0:T(8,128)(2,1)S(1)} %bitcast.11, bf16[1024,128]{1,0:T(8,128)(2,1)S(1)} %bitcast.13), custom_call_target="tpu_custom_call" | custom-call | bytes 1048576 | tf_op jit(solution)/shard_map/stage/pallas_call | solution.py:247
  21.9 2.0 %collective-permute-done.q_ref = bf16[1024,128]{1,0:T(8,128)(2,1)S(1)} collective-permute-done((bf16[1024,128]{1,0:T(8,128)(2,1)}, bf16[1024,128]{1,0:T(8,128)(2,1)S(1)}, u32[]{:S(2)}, u32[]{:S(2)}) %collective-permute-start) | collective-permute-done | bytes 262176 | tf_op jit(solution)/shard_map/ppermute | solution.py:284
  23.9 4.2 %collective-permute-done.1.g_ref = bf16[1024,128]{1,0:T(8,128)(2,1)S(1)} collective-permute-done((bf16[1024,128]{1,0:T(8,128)(2,1)}, bf16[1024,128]{1,0:T(8,128)(2,1)S(1)}, u32[]{:S(2)}, u32[]{:S(2)}) %collective-permute-start.1) | collective-permute-done | bytes 262176 | tf_op jit(solution)/shard_map/ppermute | solution.py:285
  28.1 0.2 flip.1
  28.3 1.8 %all-to-all-done.kv_ref = bf16[8,2,128,128]{3,2,1,0:T(8,128)(2,1)S(1)} async-done(((bf16[8,2,128,128]{3,2,1,0:T(8,128)(2,1)}), bf16[8,2,128,128]{3,2,1,0:T(8,128)(2,1)S(1)}, u32[]{:S(2)}, u32[]{:S(2)}) %all-to-all-start) | async-done | bytes 524320 | tf_op jit(solution)/shard_map/all_to_all | solution.py:283
  30.1 3.5 %forward.1 = (bf16[1024,2048]{1,0:T(8,128)(2,1)S(1)}, f32[4,128,256]{2,1,0:T(8,128)S(1)}, bf16[4,128,256]{2,1,0:T(8,128)(2,1)S(1)}, f32[24,256]{1,0:T(8,128)S(1)}) custom-call(s32[8,16,256]{2,1,0:T(8,128)S(1)} %get-tuple-element.25.limit_ref, bf16[4,128,256]{2,1,0:T(8,128)(2,1)S(1)} %get-tuple-element.21.qt_own, ...), custom_call_target="tpu_custom_call" | custom-call | flops 1073741824 | tf_op jit(solution)/shard_map/forward/pallas_call | solution.py:247
  33.6 4.5 %all-gather = f32[48,256]{1,0:T(8,128)S(1)} all-gather(f32[24,256]{1,0:T(8,128)S(1)} %get-tuple-element.27), channel_id=2, replica_groups={{0,1},{2,3},{4,5},{6,7},{8,9},{10,11},{12,13},{14,15},{16,17},{18,19},{..., dimensions={0}, use_global_device_ids=true | all-gather | bytes 73728 | tf_op jit(solution)/shard_map/all_gather | solution.py:314
  38.2 4.4 %backward.1 = (bf16[8,2,128,128]{3,2,1,0:T(8,128)(2,1)}, bf16[4,128,256]{2,1,0:T(8,128)(2,1)S(1)}, bf16[4,128,256]{2,1,0:T(8,128)(2,1)S(1)}, f32[8,8,256]{2,1,0:T(8,128)S(1)}) custom-call(s32[8,256]{1,0:T(8,128)S(1)} %get-tuple-element.20.side_ref, bf16[4,128,256]{2,1,0:T(8,128)(2,1)S(1)} %get-tuple-element.21.qt_own, ...), custom_call_target="tpu_custom_call" | custom-call | flops 2147483648 | tf_op jit(solution)/shard_map/backward/pallas_call | solution.py:247
  42.6 5.1 %all-to-all-start.1 = ((bf16[8,2,128,128]{3,2,1,0:T(8,128)(2,1)}), bf16[8,2,128,128]{3,2,1,0:T(8,128)(2,1)S(1)}, u32[]{:S(2)}, u32[]{:S(2)}) async-start(bf16[8,2,128,128]{3,2,1,0:T(8,128)(2,1)} %get-tuple-element.33), calls=%async_computation.1 | async-start | bytes 1048576 | tf_op jit(solution)/shard_map/all_to_all | solution.py:337
  47.8 2.5 %collective-permute-start.3 = (bf16[4,128,256]{2,1,0:T(8,128)(2,1)S(1)}, bf16[4,128,256]{2,1,0:T(8,128)(2,1)S(1)}, u32[]{:S(2)}, u32[]{:S(2)}) collective-permute-start(bf16[4,128,256]{2,1,0:T(8,128)(2,1)S(1)} %pack.1), channel_id=1, source_target_pairs={{0,1},{1,0},{2,3},{3,2},{4,5},{5,4},{6,7},{7,6},{8,9},{9,8},{10,11... | collective-permute-start | bytes 786440 | tf_op jit(solution)/shard_map/ppermute | solution.py:342
  50.2 3.4 %collective-permute-start.2 = (bf16[4,128,256]{2,1,0:T(8,128)(2,1)S(1)}, bf16[4,128,256]{2,1,0:T(8,128)(2,1)S(1)}, u32[]{:S(2)}, u32[]{:S(2)}) collective-permute-start(bf16[4,128,256]{2,1,0:T(8,128)(2,1)S(1)} %get-tuple-element.30), channel_id=1, source_target_pairs={{0,1},{1,0},{2,3},{3,2},{4,5},{5,4},{6,7},{7,6},{8,9},{9,8},{10,11... | collective-permute-start | bytes 786440 | tf_op jit(solution)/shard_map/ppermute | solution.py:315
  53.6 4.3 %collective-permute-done.3.dq_recv = bf16[4,128,256]{2,1,0:T(8,128)(2,1)S(1)} collective-permute-done((bf16[4,128,256]{2,1,0:T(8,128)(2,1)S(1)}, bf16[4,128,256]{2,1,0:T(8,128)(2,1)S(1)}, u32[]{:S(2)}, u32[]{:S(2)}) %collective-permute-start.3) | collective-permute-done | bytes 262176 | tf_op jit(solution)/shard_map/ppermute | solution.py:342
  57.9 0.8 %join.1 = bf16[1024,128]{1,0:T(8,128)(2,1)} custom-call(bf16[4,128,256]{2,1,0:T(8,128)(2,1)S(1)} %get-tuple-element.31.dq_own, bf16[4,128,256]{2,1,0:T(8,128)(2,1)S(1)} %collective-permute-done.3.dq_recv), custom_call_target="tpu_custom_call" | custom-call | bytes 1048576 | tf_op jit(solution)/shard_map/join/pallas_call | solution.py:247
  58.8 2.0 %collective-permute-done.2.o_recv = bf16[4,128,256]{2,1,0:T(8,128)(2,1)S(1)} collective-permute-done((bf16[4,128,256]{2,1,0:T(8,128)(2,1)S(1)}, bf16[4,128,256]{2,1,0:T(8,128)(2,1)S(1)}, u32[]{:S(2)}, u32[]{:S(2)}) %collective-permute-start.2) | collective-permute-done | bytes 262176 | tf_op jit(solution)/shard_map/ppermute | solution.py:315
  60.7 0.9 %out.1 = bf16[1024,128]{1,0:T(8,128)(2,1)} custom-call(f32[8,8,256]{2,1,0:T(8,128)S(1)} %get-tuple-element.28.factor_ref, f32[4,128,256]{2,1,0:T(8,128)S(1)} %get-tuple-element.29.o_own, bf16[4,128,256]{2,1,0:T(8,128)(2,1)S(1)} %collective-permute-done.2.o_recv), custom_call_target="tpu_custom_call" | custom-call | bytes 1048576 | tf_op jit(solution)/shard_map/out/pallas_call | solution.py:247
  61.6 1.2 %all-to-all-done.1.terms_ref = bf16[8,2,128,128]{3,2,1,0:T(8,128)(2,1)S(1)} async-done(((bf16[8,2,128,128]{3,2,1,0:T(8,128)(2,1)}), bf16[8,2,128,128]{3,2,1,0:T(8,128)(2,1)S(1)}, u32[]{:S(2)}, u32[]{:S(2)}) %all-to-all-start.1) | async-done | bytes 524320 | tf_op jit(solution)/shard_map/all_to_all | solution.py:337
  62.8 0.7 %total.1 = (bf16[128,128]{1,0:T(8,128)(2,1)}, bf16[128,128]{1,0:T(8,128)(2,1)}) custom-call(bf16[8,2,128,128]{3,2,1,0:T(8,128)(2,1)S(1)} %all-to-all-done.1.terms_ref), custom_call_target="tpu_custom_call" | custom-call | bytes 524288 | tf_op jit(solution)/shard_map/total/pallas_call | solution.py:247
  (1 shorter events, 0.0 us)
Async XLA Ops:
  2.3 27.8 %all-to-all-start = ((bf16[8,2,128,128]{3,2,1,0:T(8,128)(2,1)}), bf16[8,2,128,128]{3,2,1,0:T(8,128)(2,1)S(1)}, u32[]{:S(2)}, u32[]{:S(2)}) async-start(bf16[8,2,128,128]{3,2,1,0:T(8,128)(2,1)} %spread.1), calls=%async_computation | async-start | bytes 1048576 | tf_op jit(solution)/shard_map/all_to_all | solution.py:283
  12.6 11.3 %collective-permute-start = (bf16[1024,128]{1,0:T(8,128)(2,1)}, bf16[1024,128]{1,0:T(8,128)(2,1)S(1)}, u32[]{:S(2)}, u32[]{:S(2)}) collective-permute-start(bf16[1024,128]{1,0:T(8,128)(2,1)} %bitcast.10), channel_id=1, source_target_pairs={{0,1},{1,0},{2,3},{3,2},{4,5},{5,4},{6,7},{7,6},{8,9},{9,8},{10,11... | collective-permute-start | bytes 786440 | tf_op jit(solution)/shard_map/ppermute | solution.py:284
  15.1 13.0 %collective-permute-start.1 = (bf16[1024,128]{1,0:T(8,128)(2,1)}, bf16[1024,128]{1,0:T(8,128)(2,1)S(1)}, u32[]{:S(2)}, u32[]{:S(2)}) collective-permute-start(bf16[1024,128]{1,0:T(8,128)(2,1)} %bitcast.12), channel_id=1, source_target_pairs={{0,1},{1,0},{2,3},{3,2},{4,5},{5,4},{6,7},{7,6},{8,9},{9,8},{10,11... | collective-permute-start | bytes 786440 | tf_op jit(solution)/shard_map/ppermute | solution.py:285
  19.2 0.9 %copy-start = (bf16[128,8,128]{2,1,0:T(8,128)(2,1)S(1)}, bf16[128,8,128]{2,1,0:T(8,128)(2,1)}, u32[]{:S(2)}) copy-start(bf16[128,8,128]{2,1,0:T(8,128)(2,1)} %param.5) | copy-start | bytes 786436
  20.2 0.9 %copy-start.1 = (bf16[128,8,128]{2,1,0:T(8,128)(2,1)S(1)}, bf16[128,8,128]{2,1,0:T(8,128)(2,1)}, u32[]{:S(2)}) copy-start(bf16[128,8,128]{2,1,0:T(8,128)(2,1)} %param.8) | copy-start | bytes 786436
  42.6 20.2 %all-to-all-start.1 = ((bf16[8,2,128,128]{3,2,1,0:T(8,128)(2,1)}), bf16[8,2,128,128]{3,2,1,0:T(8,128)(2,1)S(1)}, u32[]{:S(2)}, u32[]{:S(2)}) async-start(bf16[8,2,128,128]{3,2,1,0:T(8,128)(2,1)} %get-tuple-element.33), calls=%async_computation.1 | async-start | bytes 1048576 | tf_op jit(solution)/shard_map/all_to_all | solution.py:337
  47.8 10.2 %collective-permute-start.3 = (bf16[4,128,256]{2,1,0:T(8,128)(2,1)S(1)}, bf16[4,128,256]{2,1,0:T(8,128)(2,1)S(1)}, u32[]{:S(2)}, u32[]{:S(2)}) collective-permute-start(bf16[4,128,256]{2,1,0:T(8,128)(2,1)S(1)} %pack.1), channel_id=1, source_target_pairs={{0,1},{1,0},{2,3},{3,2},{4,5},{5,4},{6,7},{7,6},{8,9},{9,8},{10,11... | collective-permute-start | bytes 786440 | tf_op jit(solution)/shard_map/ppermute | solution.py:342
  50.2 10.5 %collective-permute-start.2 = (bf16[4,128,256]{2,1,0:T(8,128)(2,1)S(1)}, bf16[4,128,256]{2,1,0:T(8,128)(2,1)S(1)}, u32[]{:S(2)}, u32[]{:S(2)}) collective-permute-start(bf16[4,128,256]{2,1,0:T(8,128)(2,1)S(1)} %get-tuple-element.30), channel_id=1, source_target_pairs={{0,1},{1,0},{2,3},{3,2},{4,5},{5,4},{6,7},{7,6},{8,9},{9,8},{10,11... | collective-permute-start | bytes 786440 | tf_op jit(solution)/shard_map/ppermute | solution.py:315

commit v4 on v3

--- a/solution.py
+++ b/solution.py
@@ -9,6 +9,7 @@
 from jax.sharding import PartitionSpec as P
 
 NEG_FILL = -1e30
+WIDEST = 2.0**40
 TILE = 256
 BLOCK = 64
 VMEM = pl.BlockSpec(memory_space=pltpu.VMEM)
@@ -92,49 +93,69 @@
         vt_ref[:width, c * TILE : (c + 1) * TILE] = flipped(vals).astype(HALF)
     vt_ref[width:] = jnp.ones((vt_ref.shape[0] - width, col_keys), HALF)
     key_of = lax.broadcasted_iota(jnp.int32, (BLOCK, TILE), 0)
-
-    def scores(tile):
-        mine = tile < own_tiles
-        local = tile % own_tiles
-        qt = (qt_own if mine else qt_far)[local]
-        top = None
-        for c in range(chunks):
-            keys = kv_ref[c * per : (c + 1) * per, 0].reshape(TILE, width)
-            s = dot_nn(keys, qt) * scale
-            parts = []
-            for b in range(TILE // BLOCK):
-                at = c * (TILE // BLOCK) + b
-                seen = key_of <= limit_ref[tile, at : at + 1]
-                parts.append(jnp.where(seen, s[b * BLOCK : (b + 1) * BLOCK], NEG_FILL))
-            s = jnp.concatenate(parts, axis=0)
-            s_ref[tile % 2, c * TILE : (c + 1) * TILE] = s
-            here = jnp.max(s.reshape(TILE // 8, 8, TILE), axis=0)
-            top = here if top is None else jnp.maximum(top, here)
-        return jnp.max(top, axis=0, keepdims=True)
+    tiles = 2 * own_tiles
+
+    def rows_of(own, far, tile):
+        return (own if tile < own_tiles else far)[tile % own_tiles]
+
+    def scores(tile, c):
+        keys = kv_ref[c * per : (c + 1) * per, 0].reshape(TILE, width)
+        s = dot_nn(keys, rows_of(qt_own, qt_far, tile)) * scale
+        parts = []
+        for b in range(TILE // BLOCK):
+            at = c * (TILE // BLOCK) + b
+            seen = key_of <= limit_ref[tile, at : at + 1]
+            parts.append(jnp.where(seen, s[b * BLOCK : (b + 1) * BLOCK], NEG_FILL))
+        return jnp.concatenate(parts, axis=0)
 
     def weigh(tile, top):
         put = slice(tile * TILE, (tile + 1) * TILE)
-        for c in range(chunks):
-            span = slice(c * TILE, (c + 1) * TILE)
-            p_ref[span, put] = jnp.exp2(s_ref[tile % 2, span] - top).astype(HALF)
         out = dot_nn(vt_ref[...], p_ref[:, put])
         total, out = out[width : width + 1], out[:width]
-        mine = tile < own_tiles
-        local = tile % own_tiles
-        if mine:
-            o_own[local] = out
+        if tile < own_tiles:
+            o_own[tile] = out
         else:
-            o_far[local] = out.astype(HALF)
-        delta = jnp.sum(
-            out * (gt_own if mine else gt_far)[local].astype(F32), axis=0, keepdims=True
-        )
+            o_far[tile - own_tiles] = out.astype(HALF)
+        g = rows_of(gt_own, gt_far, tile).astype(F32)
+        delta = jnp.sum(out * g, axis=0, keepdims=True)
         stat_ref[3 * tile : 3 * tile + 3] = jnp.concatenate([top, total, delta], axis=0)
-
-    top = scores(0)
-    for tile in range(2 * own_tiles):
-        later = scores(tile + 1) if tile + 1 < 2 * own_tiles else None
-        weigh(tile, top)
-        top = later
+        return total
+
+    first = kv_ref[0, 0, :BLOCK]
+    guesses = [
+        jnp.max(dot_nn(first, rows_of(qt_own, qt_far, t)) * scale, axis=0, keepdims=True)
+        for t in range(tiles)
+    ]
+
+    def guessed(tile):
+        put = slice(tile * TILE, (tile + 1) * TILE)
+        for c in range(chunks):
+            p = jnp.exp2(scores(tile, c) - guesses[tile])
+            p_ref[c * TILE : (c + 1) * TILE, put] = p.astype(HALF)
+
+    wrong = jnp.zeros((1, TILE), F32)
+    guessed(0)
+    for tile in range(tiles):
+        if tile + 1 < tiles:
+            guessed(tile + 1)
+        seen = jnp.max(limit_ref[tile], axis=0, keepdims=True) >= 0
+        total = weigh(tile, jnp.where(seen, guesses[tile], NEG_FILL))
+        fine = jnp.logical_and(total >= 1.0 / WIDEST, total <= WIDEST)
+        wrong = jnp.where(jnp.logical_and(seen, jnp.logical_not(fine)), 1.0, wrong)
+
+    @pl.when(jnp.max(wrong) > 0.0)
+    def _():
+        for tile in range(tiles):
+            put = slice(tile * TILE, (tile + 1) * TILE)
+            top = jnp.full((1, TILE), NEG_FILL, F32)
+            for c in range(chunks):
+                s = scores(tile, c)
+                s_ref[c * TILE : (c + 1) * TILE] = s
+                top = jnp.maximum(top, jnp.max(s, axis=0, keepdims=True))
+            for c in range(chunks):
+                span = slice(c * TILE, (c + 1) * TILE)
+                p_ref[span, put] = jnp.exp2(s_ref[span] - top).astype(HALF)
+            weigh(tile, top)
 
 
 def backward_kernel(
@@ -173,11 +194,10 @@
         factor_ref[tile, 1:2] = fb * inverse
         factor_ref[tile, 2:8] = jnp.zeros((6, TILE), F32)
         put = slice(tile * TILE, (tile + 1) * TILE)
-        for source, target in (
-            (qt_own if mine else qt_far, qs_ref),
-            (gt_own if mine else gt_far, gs_ref),
-        ):
-            target[put] = (source[local].astype(F32) * factor).T.astype(HALF)
+        qt = (qt_own if mine else qt_far)[local].astype(F32) * factor
+        gt = (gt_own if mine else gt_far)[local].astype(F32) * factor
+        qs_ref[put] = qt.T.astype(HALF)
+        gs_ref[:, put] = gt.astype(HALF)
 
     def grads(c):
         span = slice(c * TILE, (c + 1) * TILE)
@@ -195,7 +215,7 @@
         span = slice(c * TILE, (c + 1) * TILE)
         if c + 1 < chunks:
             grads(c + 1)
-        dv = dot_nn(p_ref[span], gs_ref[...])
+        dv = dot_nt(gs_ref[...], p_ref[span]).T
         dk = dot_nn(ds_ref[span], qs_ref[...])
         for z in range(per):
             at = c * per + z
@@ -308,7 +328,7 @@
             (flip_shape, HALF),
             ((3 * tiles, TILE), F32),
         ],
-        [pltpu.VMEM((width + 16, col_keys), HALF), pltpu.VMEM((2, col_keys, TILE), F32)],
+        [pltpu.VMEM((width + 16, col_keys), HALF), pltpu.VMEM((col_keys, TILE), F32)],
         flops=4 * product, exps=2 * own_rows * col_keys, limit=12,
     )
     both = lax.all_gather(stats, "ctx", axis_index_groups=pairs)
@@ -326,7 +346,7 @@
         ],
         [
             pltpu.VMEM((2 * own_rows, width), HALF),
-            pltpu.VMEM((2 * own_rows, width), HALF),
+            pltpu.VMEM((width, 2 * own_rows), HALF),
             pltpu.VMEM((col_keys, 2 * own_rows), HALF),
             pltpu.VMEM((width, col_keys), HALF),
             pltpu.VMEM(kv_shape, HALF),

time: 64 us -> 67.7 us (1.058)
  the two profiles are of different devices: /device:TPU:58 before, /device:TPU:36 now
where the time goes in v4:
time: 67.7 us; the launch traced here: 67.1 us
  starting transfers between devices  27.2 us (40%)
  Pallas kernels  16.7 us (25%)
  waiting for transfers between devices  15.5 us (23%)
  blocking collectives  4.5 us (7%)
  local copies, waits for them, and re-layouts  1.9 us (3%)
  other arithmetic  0.73 us (1%)
  between operations  0.72 us (1%)
    pallas_call x9, Pallas kernels, call(): pl.pallas_call(kernel, in_specs=specs or [VMEM] * len(ins), out_specs=out...  16.7 us
    all_to_all x1, starting transfers between devices, shards(): lax.all_to_all(spread, 'ctx', 0, 0, axis_index_groups=columns, tiled=True)  10.3 us
    all_to_all x1, starting transfers between devices, shards(): lax.all_to_all(dkv, 'ctx', 0, 0, axis_index_groups=columns, tiled=True)  5.15 us
    all_gather x1, blocking collectives, shards(): both = lax.all_gather(stats, 'ctx', axis_index_groups=pairs)  4.5 us
    ppermute x1, waiting for transfers between devices, shards(): dq_recv = lax.ppermute(dq_sent, 'ctx', swap)  4.29 us
    ppermute x1, waiting for transfers between devices, shards(): g_far = lax.ppermute(g, 'ctx', swap)  4.15 us
    ppermute x1, starting transfers between devices, shards(): o_recv = lax.ppermute(o_far, 'ctx', swap)  3.92 us
    ppermute x1, starting transfers between devices, shards(): q_far = lax.ppermute(q, 'ctx', swap)  3.1 us
  transfers between devices with their start and end apart: 6, of which 6 were waited for; matrix products, arithmetic and copies ran while one was open for 1% of the time, Pallas kernels for 4%

profile of v4, /device:TPU:36, one launch (start us, length us, event | category | flops | bytes accessed | tf_op | source)
XLA Modules:
  0.0 67.1 jit_solution(14442151115176001743)
XLA Ops:
  0.6 1.7 %spread.1 = bf16[8,2,128,128]{3,2,1,0:T(8,128)(2,1)} custom-call(bf16[128,128]{1,0:T(8,128)(2,1)} %bitcast.17, bf16[128,128]{1,0:T(8,128)(2,1)} %bitcast.18), custom_call_target="tpu_custom_call" | custom-call | bytes 262144 | tf_op jit(solution)/shard_map/spread/pallas_call | solution.py:267
  2.3 10.3 %all-to-all-start = ((bf16[8,2,128,128]{3,2,1,0:T(8,128)(2,1)}), bf16[8,2,128,128]{3,2,1,0:T(8,128)(2,1)S(1)}, u32[]{:S(2)}, u32[]{:S(2)}) async-start(bf16[8,2,128,128]{3,2,1,0:T(8,128)(2,1)} %spread.1), calls=%async_computation | async-start | bytes 1048576 | tf_op jit(solution)/shard_map/all_to_all | solution.py:303
  12.6 3.1 %collective-permute-start = (bf16[1024,128]{1,0:T(8,128)(2,1)}, bf16[1024,128]{1,0:T(8,128)(2,1)S(1)}, u32[]{:S(2)}, u32[]{:S(2)}) collective-permute-start(bf16[1024,128]{1,0:T(8,128)(2,1)} %bitcast.10), channel_id=1, source_target_pairs={{0,1},{1,0},{2,3},{3,2},{4,5},{5,4},{6,7},{7,6},{8,9},{9,8},{10,11... | collective-permute-start | bytes 786440 | tf_op jit(solution)/shard_map/ppermute | solution.py:304
  15.7 2.7 %collective-permute-start.1 = (bf16[1024,128]{1,0:T(8,128)(2,1)}, bf16[1024,128]{1,0:T(8,128)(2,1)S(1)}, u32[]{:S(2)}, u32[]{:S(2)}) collective-permute-start(bf16[1024,128]{1,0:T(8,128)(2,1)} %bitcast.12), channel_id=1, source_target_pairs={{0,1},{1,0},{2,3},{3,2},{4,5},{5,4},{6,7},{7,6},{8,9},{9,8},{10,11... | collective-permute-start | bytes 786440 | tf_op jit(solution)/shard_map/ppermute | solution.py:305
  18.5 0.7 %pad_add_fusion.info_ref = s32[33]{0:T(128)S(1)} fusion(s32[1]{0:T(128)} %bitcast, s32[32]{0:T(128)} %param.9), kind=kLoop, calls=%fused_computation | loop fusion | flops 33 | bytes 264 | tf_op jit(solution)/shard_map/concatenate | solution.py:306
  19.2 0.0 copy-start
  19.2 0.9 %copy-done = bf16[128,8,128]{2,1,0:T(8,128)(2,1)S(1)} copy-done((bf16[128,8,128]{2,1,0:T(8,128)(2,1)S(1)}, bf16[128,8,128]{2,1,0:T(8,128)(2,1)}, u32[]{:S(2)}) %copy-start) | copy-done | bytes 262168
  20.2 0.0 copy-start.1
  20.2 0.9 %copy-done.1 = bf16[128,8,128]{2,1,0:T(8,128)(2,1)S(1)} copy-done((bf16[128,8,128]{2,1,0:T(8,128)(2,1)S(1)}, bf16[128,8,128]{2,1,0:T(8,128)(2,1)}, u32[]{:S(2)}) %copy-start.1) | copy-done | bytes 262168
  21.1 0.8 %stage.1 = (bf16[4,128,256]{2,1,0:T(8,128)(2,1)S(1)}, bf16[4,128,256]{2,1,0:T(8,128)(2,1)S(1)}, s32[8,16,256]{2,1,0:T(8,128)S(1)}, s32[8,256]{1,0:T(8,128)S(1)}) custom-call(s32[33]{0:T(128)S(1)} %pad_add_fusion.info_ref, bf16[1024,128]{1,0:T(8,128)(2,1)S(1)} %bitcast.11, bf16[1024,128]{1,0:T(8,128)(2,1)S(1)} %bitcast.13), custom_call_target="tpu_custom_call" | custom-call | bytes 1048576 | tf_op jit(solution)/shard_map/stage/pallas_call | solution.py:267
  21.9 2.0 %collective-permute-done.q_ref = bf16[1024,128]{1,0:T(8,128)(2,1)S(1)} collective-permute-done((bf16[1024,128]{1,0:T(8,128)(2,1)}, bf16[1024,128]{1,0:T(8,128)(2,1)S(1)}, u32[]{:S(2)}, u32[]{:S(2)}) %collective-permute-start) | collective-permute-done | bytes 262176 | tf_op jit(solution)/shard_map/ppermute | solution.py:304
  23.9 4.2 %collective-permute-done.1.g_ref = bf16[1024,128]{1,0:T(8,128)(2,1)S(1)} collective-permute-done((bf16[1024,128]{1,0:T(8,128)(2,1)}, bf16[1024,128]{1,0:T(8,128)(2,1)S(1)}, u32[]{:S(2)}, u32[]{:S(2)}) %collective-permute-start.1) | collective-permute-done | bytes 262176 | tf_op jit(solution)/shard_map/ppermute | solution.py:305
  28.1 0.2 flip.1
  28.3 1.8 %all-to-all-done.kv_ref = bf16[8,2,128,128]{3,2,1,0:T(8,128)(2,1)S(1)} async-done(((bf16[8,2,128,128]{3,2,1,0:T(8,128)(2,1)}), bf16[8,2,128,128]{3,2,1,0:T(8,128)(2,1)S(1)}, u32[]{:S(2)}, u32[]{:S(2)}) %all-to-all-start) | async-done | bytes 524320 | tf_op jit(solution)/shard_map/all_to_all | solution.py:303
  30.1 7.3 %forward.1 = (bf16[1024,2048]{1,0:T(8,128)(2,1)S(1)}, f32[4,128,256]{2,1,0:T(8,128)S(1)}, bf16[4,128,256]{2,1,0:T(8,128)(2,1)S(1)}, f32[24,256]{1,0:T(8,128)S(1)}) custom-call(s32[8,16,256]{2,1,0:T(8,128)S(1)} %get-tuple-element.25.limit_ref, bf16[4,128,256]{2,1,0:T(8,128)(2,1)S(1)} %get-tuple-element.21.qt_own, ...), custom_call_target="tpu_custom_call" | custom-call | flops 1073741824 | tf_op jit(solution)/shard_map/forward/pallas_call | solution.py:267
  37.4 4.5 %all-gather = f32[48,256]{1,0:T(8,128)S(1)} all-gather(f32[24,256]{1,0:T(8,128)S(1)} %get-tuple-element.27), channel_id=2, replica_groups={{0,1},{2,3},{4,5},{6,7},{8,9},{10,11},{12,13},{14,15},{16,17},{18,19},{..., dimensions={0}, use_global_device_ids=true | all-gather | bytes 73728 | tf_op jit(solution)/shard_map/all_gather | solution.py:334
  41.9 4.3 %backward.1 = (bf16[8,2,128,128]{3,2,1,0:T(8,128)(2,1)}, bf16[4,128,256]{2,1,0:T(8,128)(2,1)S(1)}, bf16[4,128,256]{2,1,0:T(8,128)(2,1)S(1)}, f32[8,8,256]{2,1,0:T(8,128)S(1)}) custom-call(s32[8,256]{1,0:T(8,128)S(1)} %get-tuple-element.20.side_ref, bf16[4,128,256]{2,1,0:T(8,128)(2,1)S(1)} %get-tuple-element.21.qt_own, ...), custom_call_target="tpu_custom_call" | custom-call | flops 2147483648 | tf_op jit(solution)/shard_map/backward/pallas_call | solution.py:267
  46.2 5.1 %all-to-all-start.1 = ((bf16[8,2,128,128]{3,2,1,0:T(8,128)(2,1)}), bf16[8,2,128,128]{3,2,1,0:T(8,128)(2,1)S(1)}, u32[]{:S(2)}, u32[]{:S(2)}) async-start(bf16[8,2,128,128]{3,2,1,0:T(8,128)(2,1)} %get-tuple-element.33), calls=%async_computation.1 | async-start | bytes 1048576 | tf_op jit(solution)/shard_map/all_to_all | solution.py:357
  51.4 1.9 %collective-permute-start.3 = (bf16[4,128,256]{2,1,0:T(8,128)(2,1)S(1)}, bf16[4,128,256]{2,1,0:T(8,128)(2,1)S(1)}, u32[]{:S(2)}, u32[]{:S(2)}) collective-permute-start(bf16[4,128,256]{2,1,0:T(8,128)(2,1)S(1)} %pack.1), channel_id=1, source_target_pairs={{0,1},{1,0},{2,3},{3,2},{4,5},{5,4},{6,7},{7,6},{8,9},{9,8},{10,11... | collective-permute-start | bytes 786440 | tf_op jit(solution)/shard_map/ppermute | solution.py:362
  53.3 3.9 %collective-permute-start.2 = (bf16[4,128,256]{2,1,0:T(8,128)(2,1)S(1)}, bf16[4,128,256]{2,1,0:T(8,128)(2,1)S(1)}, u32[]{:S(2)}, u32[]{:S(2)}) collective-permute-start(bf16[4,128,256]{2,1,0:T(8,128)(2,1)S(1)} %get-tuple-element.30), channel_id=1, source_target_pairs={{0,1},{1,0},{2,3},{3,2},{4,5},{5,4},{6,7},{7,6},{8,9},{9,8},{10,11... | collective-permute-start | bytes 786440 | tf_op jit(solution)/shard_map/ppermute | solution.py:335
  57.2 4.3 %collective-permute-done.3.dq_recv = bf16[4,128,256]{2,1,0:T(8,128)(2,1)S(1)} collective-permute-done((bf16[4,128,256]{2,1,0:T(8,128)(2,1)S(1)}, bf16[4,128,256]{2,1,0:T(8,128)(2,1)S(1)}, u32[]{:S(2)}, u32[]{:S(2)}) %collective-permute-start.3) | collective-permute-done | bytes 262176 | tf_op jit(solution)/shard_map/ppermute | solution.py:362
  61.5 0.8 %join.1 = bf16[1024,128]{1,0:T(8,128)(2,1)} custom-call(bf16[4,128,256]{2,1,0:T(8,128)(2,1)S(1)} %get-tuple-element.31.dq_own, bf16[4,128,256]{2,1,0:T(8,128)(2,1)S(1)} %collective-permute-done.3.dq_recv), custom_call_target="tpu_custom_call" | custom-call | bytes 1048576 | tf_op jit(solution)/shard_map/join/pallas_call | solution.py:267
  62.4 2.0 %collective-permute-done.2.o_recv = bf16[4,128,256]{2,1,0:T(8,128)(2,1)S(1)} collective-permute-done((bf16[4,128,256]{2,1,0:T(8,128)(2,1)S(1)}, bf16[4,128,256]{2,1,0:T(8,128)(2,1)S(1)}, u32[]{:S(2)}, u32[]{:S(2)}) %collective-permute-start.2) | collective-permute-done | bytes 262176 | tf_op jit(solution)/shard_map/ppermute | solution.py:335
  64.3 0.9 %out.1 = bf16[1024,128]{1,0:T(8,128)(2,1)} custom-call(f32[8,8,256]{2,1,0:T(8,128)S(1)} %get-tuple-element.28.factor_ref, f32[4,128,256]{2,1,0:T(8,128)S(1)} %get-tuple-element.29.o_own, bf16[4,128,256]{2,1,0:T(8,128)(2,1)S(1)} %collective-permute-done.2.o_recv), custom_call_target="tpu_custom_call" | custom-call | bytes 1048576 | tf_op jit(solution)/shard_map/out/pallas_call | solution.py:267
  65.2 1.2 %all-to-all-done.1.terms_ref = bf16[8,2,128,128]{3,2,1,0:T(8,128)(2,1)S(1)} async-done(((bf16[8,2,128,128]{3,2,1,0:T(8,128)(2,1)}), bf16[8,2,128,128]{3,2,1,0:T(8,128)(2,1)S(1)}, u32[]{:S(2)}, u32[]{:S(2)}) %all-to-all-start.1) | async-done | bytes 524320 | tf_op jit(solution)/shard_map/all_to_all | solution.py:357
  66.4 0.7 %total.1 = (bf16[128,128]{1,0:T(8,128)(2,1)}, bf16[128,128]{1,0:T(8,128)(2,1)}) custom-call(bf16[8,2,128,128]{3,2,1,0:T(8,128)(2,1)S(1)} %all-to-all-done.1.terms_ref), custom_call_target="tpu_custom_call" | custom-call | bytes 524288 | tf_op jit(solution)/shard_map/total/pallas_call | solution.py:267
  (1 shorter events, 0.0 us)
Async XLA Ops:
  2.3 27.8 %all-to-all-start = ((bf16[8,2,128,128]{3,2,1,0:T(8,128)(2,1)}), bf16[8,2,128,128]{3,2,1,0:T(8,128)(2,1)S(1)}, u32[]{:S(2)}, u32[]{:S(2)}) async-start(bf16[8,2,128,128]{3,2,1,0:T(8,128)(2,1)} %spread.1), calls=%async_computation | async-start | bytes 1048576 | tf_op jit(solution)/shard_map/all_to_all | solution.py:303
  12.6 11.3 %collective-permute-start = (bf16[1024,128]{1,0:T(8,128)(2,1)}, bf16[1024,128]{1,0:T(8,128)(2,1)S(1)}, u32[]{:S(2)}, u32[]{:S(2)}) collective-permute-start(bf16[1024,128]{1,0:T(8,128)(2,1)} %bitcast.10), channel_id=1, source_target_pairs={{0,1},{1,0},{2,3},{3,2},{4,5},{5,4},{6,7},{7,6},{8,9},{9,8},{10,11... | collective-permute-start | bytes 786440 | tf_op jit(solution)/shard_map/ppermute | solution.py:304
  15.7 12.4 %collective-permute-start.1 = (bf16[1024,128]{1,0:T(8,128)(2,1)}, bf16[1024,128]{1,0:T(8,128)(2,1)S(1)}, u32[]{:S(2)}, u32[]{:S(2)}) collective-permute-start(bf16[1024,128]{1,0:T(8,128)(2,1)} %bitcast.12), channel_id=1, source_target_pairs={{0,1},{1,0},{2,3},{3,2},{4,5},{5,4},{6,7},{7,6},{8,9},{9,8},{10,11... | collective-permute-start | bytes 786440 | tf_op jit(solution)/shard_map/ppermute | solution.py:305
  19.2 0.9 %copy-start = (bf16[128,8,128]{2,1,0:T(8,128)(2,1)S(1)}, bf16[128,8,128]{2,1,0:T(8,128)(2,1)}, u32[]{:S(2)}) copy-start(bf16[128,8,128]{2,1,0:T(8,128)(2,1)} %param.5) | copy-start | bytes 786436
  20.2 0.9 %copy-start.1 = (bf16[128,8,128]{2,1,0:T(8,128)(2,1)S(1)}, bf16[128,8,128]{2,1,0:T(8,128)(2,1)}, u32[]{:S(2)}) copy-start(bf16[128,8,128]{2,1,0:T(8,128)(2,1)} %param.8) | copy-start | bytes 786436
  46.2 20.2 %all-to-all-start.1 = ((bf16[8,2,128,128]{3,2,1,0:T(8,128)(2,1)}), bf16[8,2,128,128]{3,2,1,0:T(8,128)(2,1)S(1)}, u32[]{:S(2)}, u32[]{:S(2)}) async-start(bf16[8,2,128,128]{3,2,1,0:T(8,128)(2,1)} %get-tuple-element.33), calls=%async_computation.1 | async-start | bytes 1048576 | tf_op jit(solution)/shard_map/all_to_all | solution.py:357
  51.4 10.2 %collective-permute-start.3 = (bf16[4,128,256]{2,1,0:T(8,128)(2,1)S(1)}, bf16[4,128,256]{2,1,0:T(8,128)(2,1)S(1)}, u32[]{:S(2)}, u32[]{:S(2)}) collective-permute-start(bf16[4,128,256]{2,1,0:T(8,128)(2,1)S(1)} %pack.1), channel_id=1, source_target_pairs={{0,1},{1,0},{2,3},{3,2},{4,5},{5,4},{6,7},{7,6},{8,9},{9,8},{10,11... | collective-permute-start | bytes 786440 | tf_op jit(solution)/shard_map/ppermute | solution.py:362
  53.3 11.0 %collective-permute-start.2 = (bf16[4,128,256]{2,1,0:T(8,128)(2,1)S(1)}, bf16[4,128,256]{2,1,0:T(8,128)(2,1)S(1)}, u32[]{:S(2)}, u32[]{:S(2)}) collective-permute-start(bf16[4,128,256]{2,1,0:T(8,128)(2,1)S(1)} %get-tuple-element.30), channel_id=1, source_target_pairs={{0,1},{1,0},{2,3},{3,2},{4,5},{5,4},{6,7},{7,6},{8,9},{9,8},{10,11... | collective-permute-start | bytes 786440 | tf_op jit(solution)/shard_map/ppermute | solution.py:335

commit v5 on v4

--- a/solution.py
+++ b/solution.py
@@ -80,7 +80,7 @@
 
 def forward_kernel(
     limit_ref, qt_own, qt_far, gt_own, gt_far, kv_ref, p_ref, o_own, o_far, stat_ref, vt_ref, s_ref,
-    *, scale
+    *, repeat, scale
 ):
     holders, _, rows, width = kv_ref.shape
     col_keys = holders * rows
@@ -129,8 +129,19 @@
 
     def guessed(tile):
         put = slice(tile * TILE, (tile + 1) * TILE)
+        own_block = tile * (TILE // repeat) // BLOCK if tile < own_tiles else None
         for c in range(chunks):
-            p = jnp.exp2(scores(tile, c) - guesses[tile])
+            keys = kv_ref[c * per : (c + 1) * per, 0].reshape(TILE, width)
+            s = dot_nn(keys, rows_of(qt_own, qt_far, tile)) * scale
+            parts = []
+            for b in range(TILE // BLOCK):
+                at = c * (TILE // BLOCK) + b
+                part = s[b * BLOCK : (b + 1) * BLOCK]
+                limit = limit_ref[tile, at : at + 1]
+                if at % (rows // BLOCK) == own_block:
+                    part = jnp.where(key_of <= limit, part, NEG_FILL)
+                parts.append(part - jnp.where(limit >= 0, guesses[tile], -NEG_FILL))
+            p = jnp.exp2(jnp.concatenate(parts, axis=0))
             p_ref[c * TILE : (c + 1) * TILE, put] = p.astype(HALF)
 
     wrong = jnp.zeros((1, TILE), F32)
@@ -320,7 +331,9 @@
     )
 
     weights, o_own, o_far, stats = call(
-        functools.partial(forward_kernel, scale=score_scale * math.log2(math.e)),
+        functools.partial(
+            forward_kernel, repeat=heads, scale=score_scale * math.log2(math.e)
+        ),
         "forward", (limits, qt_own, qt_far, gt_own, gt_far, kv_all),
         [
             ((col_keys, 2 * own_rows), HALF),

time: 67.7 us -> 67.3 us (level)
  the two profiles are of different devices: /device:TPU:36 before, /device:TPU:20 now
where the time goes in v5:
time: 67.3 us; the launch traced here: 66.8 us
  starting transfers between devices  27.2 us (40%)
  Pallas kernels  16.3 us (24%)
  waiting for transfers between devices  15.5 us (23%)
  blocking collectives  4.5 us (7%)
  local copies, waits for them, and re-layouts  1.9 us (3%)
  other arithmetic  0.73 us (1%)
  between operations  0.72 us (1%)
    pallas_call x9, Pallas kernels, call(): pl.pallas_call(kernel, in_specs=specs or [VMEM] * len(ins), out_specs=out...  16.3 us
    all_to_all x1, starting transfers between devices, shards(): lax.all_to_all(spread, 'ctx', 0, 0, axis_index_groups=columns, tiled=True)  10.3 us
    all_to_all x1, starting transfers between devices, shards(): lax.all_to_all(dkv, 'ctx', 0, 0, axis_index_groups=columns, tiled=True)  5.15 us
    all_gather x1, blocking collectives, shards(): both = lax.all_gather(stats, 'ctx', axis_index_groups=pairs)  4.5 us
    ppermute x1, waiting for transfers between devices, shards(): dq_recv = lax.ppermute(dq_sent, 'ctx', swap)  4.29 us
    ppermute x1, waiting for transfers between devices, shards(): g_far = lax.ppermute(g, 'ctx', swap)  4.15 us
    ppermute x1, starting transfers between devices, shards(): o_recv = lax.ppermute(o_far, 'ctx', swap)  3.92 us
    ppermute x1, starting transfers between devices, shards(): q_far = lax.ppermute(q, 'ctx', swap)  3.1 us
  transfers between devices with their start and end apart: 6, of which 6 were waited for; matrix products, arithmetic and copies ran while one was open for 1% of the time, Pallas kernels for 4%

profile of v5, /device:TPU:20, one launch (start us, length us, event | category | flops | bytes accessed | tf_op | source)
XLA Modules:
  0.0 66.8 jit_solution(11941818676420376466)
XLA Ops:
  0.6 1.7 %spread.1 = bf16[8,2,128,128]{3,2,1,0:T(8,128)(2,1)} custom-call(bf16[128,128]{1,0:T(8,128)(2,1)} %bitcast.17, bf16[128,128]{1,0:T(8,128)(2,1)} %bitcast.18), custom_call_target="tpu_custom_call" | custom-call | bytes 262144 | tf_op jit(solution)/shard_map/spread/pallas_call | solution.py:278
  2.3 10.3 %all-to-all-start = ((bf16[8,2,128,128]{3,2,1,0:T(8,128)(2,1)}), bf16[8,2,128,128]{3,2,1,0:T(8,128)(2,1)S(1)}, u32[]{:S(2)}, u32[]{:S(2)}) async-start(bf16[8,2,128,128]{3,2,1,0:T(8,128)(2,1)} %spread.1), calls=%async_computation | async-start | bytes 1048576 | tf_op jit(solution)/shard_map/all_to_all | solution.py:314
  12.6 3.1 %collective-permute-start = (bf16[1024,128]{1,0:T(8,128)(2,1)}, bf16[1024,128]{1,0:T(8,128)(2,1)S(1)}, u32[]{:S(2)}, u32[]{:S(2)}) collective-permute-start(bf16[1024,128]{1,0:T(8,128)(2,1)} %bitcast.10), channel_id=1, source_target_pairs={{0,1},{1,0},{2,3},{3,2},{4,5},{5,4},{6,7},{7,6},{8,9},{9,8},{10,11... | collective-permute-start | bytes 786440 | tf_op jit(solution)/shard_map/ppermute | solution.py:315
  15.7 2.7 %collective-permute-start.1 = (bf16[1024,128]{1,0:T(8,128)(2,1)}, bf16[1024,128]{1,0:T(8,128)(2,1)S(1)}, u32[]{:S(2)}, u32[]{:S(2)}) collective-permute-start(bf16[1024,128]{1,0:T(8,128)(2,1)} %bitcast.12), channel_id=1, source_target_pairs={{0,1},{1,0},{2,3},{3,2},{4,5},{5,4},{6,7},{7,6},{8,9},{9,8},{10,11... | collective-permute-start | bytes 786440 | tf_op jit(solution)/shard_map/ppermute | solution.py:316
  18.5 0.7 %pad_add_fusion.info_ref = s32[33]{0:T(128)S(1)} fusion(s32[1]{0:T(128)} %bitcast, s32[32]{0:T(128)} %param.9), kind=kLoop, calls=%fused_computation | loop fusion | flops 33 | bytes 264 | tf_op jit(solution)/shard_map/concatenate | solution.py:317
  19.2 0.0 copy-start
  19.2 0.9 %copy-done = bf16[128,8,128]{2,1,0:T(8,128)(2,1)S(1)} copy-done((bf16[128,8,128]{2,1,0:T(8,128)(2,1)S(1)}, bf16[128,8,128]{2,1,0:T(8,128)(2,1)}, u32[]{:S(2)}) %copy-start) | copy-done | bytes 262168
  20.2 0.0 copy-start.1
  20.2 0.9 %copy-done.1 = bf16[128,8,128]{2,1,0:T(8,128)(2,1)S(1)} copy-done((bf16[128,8,128]{2,1,0:T(8,128)(2,1)S(1)}, bf16[128,8,128]{2,1,0:T(8,128)(2,1)}, u32[]{:S(2)}) %copy-start.1) | copy-done | bytes 262168
  21.1 0.8 %stage.1 = (bf16[4,128,256]{2,1,0:T(8,128)(2,1)S(1)}, bf16[4,128,256]{2,1,0:T(8,128)(2,1)S(1)}, s32[8,16,256]{2,1,0:T(8,128)S(1)}, s32[8,256]{1,0:T(8,128)S(1)}) custom-call(s32[33]{0:T(128)S(1)} %pad_add_fusion.info_ref, bf16[1024,128]{1,0:T(8,128)(2,1)S(1)} %bitcast.11, bf16[1024,128]{1,0:T(8,128)(2,1)S(1)} %bitcast.13), custom_call_target="tpu_custom_call" | custom-call | bytes 1048576 | tf_op jit(solution)/shard_map/stage/pallas_call | solution.py:278
  21.9 2.0 %collective-permute-done.q_ref = bf16[1024,128]{1,0:T(8,128)(2,1)S(1)} collective-permute-done((bf16[1024,128]{1,0:T(8,128)(2,1)}, bf16[1024,128]{1,0:T(8,128)(2,1)S(1)}, u32[]{:S(2)}, u32[]{:S(2)}) %collective-permute-start) | collective-permute-done | bytes 262176 | tf_op jit(solution)/shard_map/ppermute | solution.py:315
  23.9 4.2 %collective-permute-done.1.g_ref = bf16[1024,128]{1,0:T(8,128)(2,1)S(1)} collective-permute-done((bf16[1024,128]{1,0:T(8,128)(2,1)}, bf16[1024,128]{1,0:T(8,128)(2,1)S(1)}, u32[]{:S(2)}, u32[]{:S(2)}) %collective-permute-start.1) | collective-permute-done | bytes 262176 | tf_op jit(solution)/shard_map/ppermute | solution.py:316
  28.1 0.2 flip.1
  28.3 1.8 %all-to-all-done.kv_ref = bf16[8,2,128,128]{3,2,1,0:T(8,128)(2,1)S(1)} async-done(((bf16[8,2,128,128]{3,2,1,0:T(8,128)(2,1)}), bf16[8,2,128,128]{3,2,1,0:T(8,128)(2,1)S(1)}, u32[]{:S(2)}, u32[]{:S(2)}) %all-to-all-start) | async-done | bytes 524320 | tf_op jit(solution)/shard_map/all_to_all | solution.py:314
  30.1 6.9 %forward.1 = (bf16[1024,2048]{1,0:T(8,128)(2,1)S(1)}, f32[4,128,256]{2,1,0:T(8,128)S(1)}, bf16[4,128,256]{2,1,0:T(8,128)(2,1)S(1)}, f32[24,256]{1,0:T(8,128)S(1)}) custom-call(s32[8,16,256]{2,1,0:T(8,128)S(1)} %get-tuple-element.25.limit_ref, bf16[4,128,256]{2,1,0:T(8,128)(2,1)S(1)} %get-tuple-element.21.qt_own, ...), custom_call_target="tpu_custom_call" | custom-call | flops 1073741824 | tf_op jit(solution)/shard_map/forward/pallas_call | solution.py:278
  37.1 4.5 %all-gather = f32[48,256]{1,0:T(8,128)S(1)} all-gather(f32[24,256]{1,0:T(8,128)S(1)} %get-tuple-element.27), channel_id=2, replica_groups={{0,1},{2,3},{4,5},{6,7},{8,9},{10,11},{12,13},{14,15},{16,17},{18,19},{..., dimensions={0}, use_global_device_ids=true | all-gather | bytes 73728 | tf_op jit(solution)/shard_map/all_gather | solution.py:347
  41.6 4.3 %backward.1 = (bf16[8,2,128,128]{3,2,1,0:T(8,128)(2,1)}, bf16[4,128,256]{2,1,0:T(8,128)(2,1)S(1)}, bf16[4,128,256]{2,1,0:T(8,128)(2,1)S(1)}, f32[8,8,256]{2,1,0:T(8,128)S(1)}) custom-call(s32[8,256]{1,0:T(8,128)S(1)} %get-tuple-element.20.side_ref, bf16[4,128,256]{2,1,0:T(8,128)(2,1)S(1)} %get-tuple-element.21.qt_own, ...), custom_call_target="tpu_custom_call" | custom-call | flops 2147483648 | tf_op jit(solution)/shard_map/backward/pallas_call | solution.py:278
  45.9 5.1 %all-to-all-start.1 = ((bf16[8,2,128,128]{3,2,1,0:T(8,128)(2,1)}), bf16[8,2,128,128]{3,2,1,0:T(8,128)(2,1)S(1)}, u32[]{:S(2)}, u32[]{:S(2)}) async-start(bf16[8,2,128,128]{3,2,1,0:T(8,128)(2,1)} %get-tuple-element.33), calls=%async_computation.1 | async-start | bytes 1048576 | tf_op jit(solution)/shard_map/all_to_all | solution.py:370
  51.0 1.9 %collective-permute-start.3 = (bf16[4,128,256]{2,1,0:T(8,128)(2,1)S(1)}, bf16[4,128,256]{2,1,0:T(8,128)(2,1)S(1)}, u32[]{:S(2)}, u32[]{:S(2)}) collective-permute-start(bf16[4,128,256]{2,1,0:T(8,128)(2,1)S(1)} %pack.1), channel_id=1, source_target_pairs={{0,1},{1,0},{2,3},{3,2},{4,5},{5,4},{6,7},{7,6},{8,9},{9,8},{10,11... | collective-permute-start | bytes 786440 | tf_op jit(solution)/shard_map/ppermute | solution.py:375
  53.0 3.9 %collective-permute-start.2 = (bf16[4,128,256]{2,1,0:T(8,128)(2,1)S(1)}, bf16[4,128,256]{2,1,0:T(8,128)(2,1)S(1)}, u32[]{:S(2)}, u32[]{:S(2)}) collective-permute-start(bf16[4,128,256]{2,1,0:T(8,128)(2,1)S(1)} %get-tuple-element.30), channel_id=1, source_target_pairs={{0,1},{1,0},{2,3},{3,2},{4,5},{5,4},{6,7},{7,6},{8,9},{9,8},{10,11... | collective-permute-start | bytes 786440 | tf_op jit(solution)/shard_map/ppermute | solution.py:348
  56.9 4.3 %collective-permute-done.3.dq_recv = bf16[4,128,256]{2,1,0:T(8,128)(2,1)S(1)} collective-permute-done((bf16[4,128,256]{2,1,0:T(8,128)(2,1)S(1)}, bf16[4,128,256]{2,1,0:T(8,128)(2,1)S(1)}, u32[]{:S(2)}, u32[]{:S(2)}) %collective-permute-start.3) | collective-permute-done | bytes 262176 | tf_op jit(solution)/shard_map/ppermute | solution.py:375
  61.2 0.8 %join.1 = bf16[1024,128]{1,0:T(8,128)(2,1)} custom-call(bf16[4,128,256]{2,1,0:T(8,128)(2,1)S(1)} %get-tuple-element.31.dq_own, bf16[4,128,256]{2,1,0:T(8,128)(2,1)S(1)} %collective-permute-done.3.dq_recv), custom_call_target="tpu_custom_call" | custom-call | bytes 1048576 | tf_op jit(solution)/shard_map/join/pallas_call | solution.py:278
  62.0 2.0 %collective-permute-done.2.o_recv = bf16[4,128,256]{2,1,0:T(8,128)(2,1)S(1)} collective-permute-done((bf16[4,128,256]{2,1,0:T(8,128)(2,1)S(1)}, bf16[4,128,256]{2,1,0:T(8,128)(2,1)S(1)}, u32[]{:S(2)}, u32[]{:S(2)}) %collective-permute-start.2) | collective-permute-done | bytes 262176 | tf_op jit(solution)/shard_map/ppermute | solution.py:348
  64.0 0.9 %out.1 = bf16[1024,128]{1,0:T(8,128)(2,1)} custom-call(f32[8,8,256]{2,1,0:T(8,128)S(1)} %get-tuple-element.28.factor_ref, f32[4,128,256]{2,1,0:T(8,128)S(1)} %get-tuple-element.29.o_own, bf16[4,128,256]{2,1,0:T(8,128)(2,1)S(1)} %collective-permute-done.2.o_recv), custom_call_target="tpu_custom_call" | custom-call | bytes 1048576 | tf_op jit(solution)/shard_map/out/pallas_call | solution.py:278
  64.8 1.2 %all-to-all-done.1.terms_ref = bf16[8,2,128,128]{3,2,1,0:T(8,128)(2,1)S(1)} async-done(((bf16[8,2,128,128]{3,2,1,0:T(8,128)(2,1)}), bf16[8,2,128,128]{3,2,1,0:T(8,128)(2,1)S(1)}, u32[]{:S(2)}, u32[]{:S(2)}) %all-to-all-start.1) | async-done | bytes 524320 | tf_op jit(solution)/shard_map/all_to_all | solution.py:370
  66.1 0.7 %total.1 = (bf16[128,128]{1,0:T(8,128)(2,1)}, bf16[128,128]{1,0:T(8,128)(2,1)}) custom-call(bf16[8,2,128,128]{3,2,1,0:T(8,128)(2,1)S(1)} %all-to-all-done.1.terms_ref), custom_call_target="tpu_custom_call" | custom-call | bytes 524288 | tf_op jit(solution)/shard_map/total/pallas_call | solution.py:278
  (1 shorter events, 0.0 us)
Async XLA Ops:
  2.3 27.8 %all-to-all-start = ((bf16[8,2,128,128]{3,2,1,0:T(8,128)(2,1)}), bf16[8,2,128,128]{3,2,1,0:T(8,128)(2,1)S(1)}, u32[]{:S(2)}, u32[]{:S(2)}) async-start(bf16[8,2,128,128]{3,2,1,0:T(8,128)(2,1)} %spread.1), calls=%async_computation | async-start | bytes 1048576 | tf_op jit(solution)/shard_map/all_to_all | solution.py:314
  12.6 11.3 %collective-permute-start = (bf16[1024,128]{1,0:T(8,128)(2,1)}, bf16[1024,128]{1,0:T(8,128)(2,1)S(1)}, u32[]{:S(2)}, u32[]{:S(2)}) collective-permute-start(bf16[1024,128]{1,0:T(8,128)(2,1)} %bitcast.10), channel_id=1, source_target_pairs={{0,1},{1,0},{2,3},{3,2},{4,5},{5,4},{6,7},{7,6},{8,9},{9,8},{10,11... | collective-permute-start | bytes 786440 | tf_op jit(solution)/shard_map/ppermute | solution.py:315
  15.7 12.4 %collective-permute-start.1 = (bf16[1024,128]{1,0:T(8,128)(2,1)}, bf16[1024,128]{1,0:T(8,128)(2,1)S(1)}, u32[]{:S(2)}, u32[]{:S(2)}) collective-permute-start(bf16[1024,128]{1,0:T(8,128)(2,1)} %bitcast.12), channel_id=1, source_target_pairs={{0,1},{1,0},{2,3},{3,2},{4,5},{5,4},{6,7},{7,6},{8,9},{9,8},{10,11... | collective-permute-start | bytes 786440 | tf_op jit(solution)/shard_map/ppermute | solution.py:316
  19.2 0.9 %copy-start = (bf16[128,8,128]{2,1,0:T(8,128)(2,1)S(1)}, bf16[128,8,128]{2,1,0:T(8,128)(2,1)}, u32[]{:S(2)}) copy-start(bf16[128,8,128]{2,1,0:T(8,128)(2,1)} %param.5) | copy-start | bytes 786436
  20.2 0.9 %copy-start.1 = (bf16[128,8,128]{2,1,0:T(8,128)(2,1)S(1)}, bf16[128,8,128]{2,1,0:T(8,128)(2,1)}, u32[]{:S(2)}) copy-start(bf16[128,8,128]{2,1,0:T(8,128)(2,1)} %param.8) | copy-start | bytes 786436
  45.9 20.2 %all-to-all-start.1 = ((bf16[8,2,128,128]{3,2,1,0:T(8,128)(2,1)}), bf16[8,2,128,128]{3,2,1,0:T(8,128)(2,1)S(1)}, u32[]{:S(2)}, u32[]{:S(2)}) async-start(bf16[8,2,128,128]{3,2,1,0:T(8,128)(2,1)} %get-tuple-element.33), calls=%async_computation.1 | async-start | bytes 1048576 | tf_op jit(solution)/shard_map/all_to_all | solution.py:370
  51.0 10.2 %collective-permute-start.3 = (bf16[4,128,256]{2,1,0:T(8,128)(2,1)S(1)}, bf16[4,128,256]{2,1,0:T(8,128)(2,1)S(1)}, u32[]{:S(2)}, u32[]{:S(2)}) collective-permute-start(bf16[4,128,256]{2,1,0:T(8,128)(2,1)S(1)} %pack.1), channel_id=1, source_target_pairs={{0,1},{1,0},{2,3},{3,2},{4,5},{5,4},{6,7},{7,6},{8,9},{9,8},{10,11... | collective-permute-start | bytes 786440 | tf_op jit(solution)/shard_map/ppermute | solution.py:375
  53.0 11.0 %collective-permute-start.2 = (bf16[4,128,256]{2,1,0:T(8,128)(2,1)S(1)}, bf16[4,128,256]{2,1,0:T(8,128)(2,1)S(1)}, u32[]{:S(2)}, u32[]{:S(2)}) collective-permute-start(bf16[4,128,256]{2,1,0:T(8,128)(2,1)S(1)} %get-tuple-element.30), channel_id=1, source_target_pairs={{0,1},{1,0},{2,3},{3,2},{4,5},{5,4},{6,7},{7,6},{8,9},{9,8},{10,11... | collective-permute-start | bytes 786440 | tf_op jit(solution)/shard_map/ppermute | solution.py:348

commit v6 on v5

--- a/solution.py
+++ b/solution.py
@@ -53,7 +53,7 @@
         out_ref[t] = flipped(source[t * TILE : (t + 1) * TILE]).astype(HALF)
 
 
-def stage_kernel(info_ref, q_ref, g_ref, qt_out, gt_out, limit_ref, side_ref, *, repeat):
+def stage_kernel(info_ref, q_ref, g_ref, qt_out, gt_out, limit_ref, *, repeat):
     own_tiles = gt_out.shape[0]
     tiles, blocks, _ = limit_ref.shape
     last = info_ref.shape[0] - 1
@@ -70,7 +70,6 @@
         for b in range(blocks):
             stored = ((b // blocks_here) * 2 + side) * blocks_here + b % blocks_here
             limit_ref[t, b : b + 1] = token_of + (place - info_ref[stored] * BLOCK)
-    side_ref[...] = jnp.zeros(side_ref.shape, jnp.int32) + side
 
 
 def flip_kernel(q_ref, g_ref, qt_out, gt_out):
@@ -142,19 +141,28 @@
                     part = jnp.where(key_of <= limit, part, NEG_FILL)
                 parts.append(part - jnp.where(limit >= 0, guesses[tile], -NEG_FILL))
             p = jnp.exp2(jnp.concatenate(parts, axis=0))
+            if tile == tiles - 1:
+                sums.append(jnp.sum(p.reshape(TILE // 8, 8, TILE), axis=0))
             p_ref[c * TILE : (c + 1) * TILE, put] = p.astype(HALF)
 
+    def bad(seen, total):
+        fine = jnp.logical_and(total >= 1.0 / WIDEST, total <= WIDEST)
+        return jnp.where(jnp.logical_and(seen, jnp.logical_not(fine)), 1.0, 0.0)
+
     wrong = jnp.zeros((1, TILE), F32)
+    sums = []
     guessed(0)
     for tile in range(tiles):
         if tile + 1 < tiles:
             guessed(tile + 1)
         seen = jnp.max(limit_ref[tile], axis=0, keepdims=True) >= 0
+        if tile == tiles - 1:
+            total = jnp.sum(sum(sums[1:], sums[0]), axis=0, keepdims=True)
+            again = jnp.max(jnp.maximum(wrong, bad(seen, total))) > 0.0
         total = weigh(tile, jnp.where(seen, guesses[tile], NEG_FILL))
-        fine = jnp.logical_and(total >= 1.0 / WIDEST, total <= WIDEST)
-        wrong = jnp.where(jnp.logical_and(seen, jnp.logical_not(fine)), 1.0, wrong)
-
-    @pl.when(jnp.max(wrong) > 0.0)
+        wrong = jnp.maximum(wrong, bad(seen, total))
+
+    @pl.when(again)
     def _():
         for tile in range(tiles):
             put = slice(tile * TILE, (tile + 1) * TILE)
@@ -169,8 +177,20 @@
             weigh(tile, top)
 
 
+def middle_kernel(gt_own, gt_far, kv_ref, dp_ref):
+    holders, _, rows, width = kv_ref.shape
+    per = TILE // rows
+    own_tiles = gt_own.shape[0]
+    for c in range(holders // per):
+        vals = kv_ref[c * per : (c + 1) * per, 1].reshape(TILE, width)
+        for tile in range(2 * own_tiles):
+            gt = (gt_own if tile < own_tiles else gt_far)[tile % own_tiles]
+            span = slice(tile * TILE, (tile + 1) * TILE)
+            dp_ref[c * TILE : (c + 1) * TILE, span] = dot_nn(vals, gt)
+
+
 def backward_kernel(
-    side_ref, qt_own, qt_far, gt_own, gt_far, kv_ref, p_ref, stat_ref,
+    qt_own, qt_far, gt_own, gt_far, kv_ref, p_ref, dp_ref, here_ref, there_ref,
     dkv_ref, dq_own, dq_far, factor_ref, qs_ref, gs_ref, ds_ref, kt_ref, done_ref, sems,
     *, scale
 ):
@@ -181,20 +201,12 @@
     tiles = 2 * own_tiles
     flip_keys(kv_ref, kt_ref)
     deltas, factors = [], []
-    right = side_ref[0:1] > 0
     for tile in range(tiles):
         mine = tile < own_tiles
         local = tile % own_tiles
         other = (tile + own_tiles) % tiles
-        here, there = (
-            [jnp.where(right, stat_ref[1 - s, at], stat_ref[s, at]) for at in spans]
-            for s, spans in (
-                (0, [slice(3 * tile + i, 3 * tile + i + 1) for i in range(3)]),
-                (1, [slice(3 * other + i, 3 * other + i + 1) for i in range(3)]),
-            )
-        )
-        top_a, sum_a, delta_a = here
-        top_b, sum_b, delta_b = there
+        top_a, sum_a, delta_a = (here_ref[3 * tile + i : 3 * tile + i + 1] for i in range(3))
+        top_b, sum_b, delta_b = (there_ref[3 * other + i : 3 * other + i + 1] for i in range(3))
         top = jnp.maximum(top_a, top_b)
         fa, fb = jnp.exp2(top_a - top), jnp.exp2(top_b - top)
         inverse = 1.0 / (sum_a * fa + sum_b * fb)
@@ -212,13 +224,10 @@
 
     def grads(c):
         span = slice(c * TILE, (c + 1) * TILE)
-        vals = kv_ref[c * per : (c + 1) * per, 1].reshape(TILE, width)
         for tile in range(tiles):
-            mine = tile < own_tiles
-            local = tile % own_tiles
-            p = p_ref[span, tile * TILE : (tile + 1) * TILE].astype(F32)
-            grad = p * (dot_nn(vals, (gt_own if mine else gt_far)[local]) - deltas[tile])
-            ds_ref[span, tile * TILE : (tile + 1) * TILE] = grad.astype(HALF)
+            put = slice(tile * TILE, (tile + 1) * TILE)
+            grad = p_ref[span, put].astype(F32) * (dp_ref[span, put] - deltas[tile])
+            ds_ref[span, put] = grad.astype(HALF)
 
     copies = []
     grads(0)
@@ -315,14 +324,12 @@
     q_far = lax.ppermute(q, "ctx", swap)
     g_far = lax.ppermute(g, "ctx", swap)
     info = jnp.concatenate([block_order, lax.axis_index("ctx").astype(jnp.int32).reshape(1)])
-    pairs = [[2 * z, 2 * z + 1] for z in range(holders)]
-    qt_own, gt_own, limits, side = call(
+    qt_own, gt_own, limits = call(
         functools.partial(stage_kernel, repeat=heads), "stage", (info, q, g),
         [
             (flip_shape, HALF),
             (flip_shape, HALF),
             ((tiles, col_keys // BLOCK, TILE), jnp.int32),
-            ((8, TILE), jnp.int32),
         ],
         moved=moved, specs=[SMEM, VMEM, VMEM],
     )
@@ -344,13 +351,17 @@
         [pltpu.VMEM((width + 16, col_keys), HALF), pltpu.VMEM((col_keys, TILE), F32)],
         flops=4 * product, exps=2 * own_rows * col_keys, limit=12,
     )
-    both = lax.all_gather(stats, "ctx", axis_index_groups=pairs)
+    there = lax.ppermute(stats, "ctx", swap)
+    (grad_weights,) = call(
+        middle_kernel, "middle", (gt_own, gt_far, kv_all),
+        [((col_keys, 2 * own_rows), F32)], flops=2 * product, moved=8 * own_rows * col_keys,
+    )
     o_recv = lax.ppermute(o_far, "ctx", swap)
 
     dkv, dq_own, dq_far, factors = call(
         functools.partial(backward_kernel, scale=score_scale),
         "backward",
-        (side, qt_own, qt_far, gt_own, gt_far, kv_all, weights, both),
+        (qt_own, qt_far, gt_own, gt_far, kv_all, weights, grad_weights, stats, there),
         [
             (kv_shape, HALF),
             (flip_shape, HALF),
@@ -365,7 +376,7 @@
             pltpu.VMEM(kv_shape, HALF),
             pltpu.SemaphoreType.DMA((holders,)),
         ],
-        flops=8 * product, limit=16, out_specs=[HBM, VMEM, VMEM, VMEM],
+        flops=6 * product, limit=16, out_specs=[HBM, VMEM, VMEM, VMEM],
     )
     terms = lax.all_to_all(dkv, "ctx", 0, 0, axis_index_groups=columns, tiled=True)
 

time: 67.3 us -> 67.5 us (level)
  the two profiles are of different devices: /device:TPU:20 before, /device:TPU:48 now
where the time goes in v6:
time: 67.5 us; the launch traced here: 66.9 us
  starting transfers between devices  29.1 us (43%)
  waiting for transfers between devices  18 us (27%)
  Pallas kernels  16.5 us (24%)
  local copies, waits for them, and re-layouts  1.9 us (3%)
  other arithmetic  0.73 us (1%)
  between operations  0.73 us (1%)
    pallas_call x10, Pallas kernels, call(): pl.pallas_call(kernel, in_specs=specs or [VMEM] * len(ins), out_specs=out...  16.5 us
    all_to_all x1, starting transfers between devices, shards(): lax.all_to_all(spread, 'ctx', 0, 0, axis_index_groups=columns, tiled=True)  10.3 us
    all_to_all x1, starting transfers between devices, shards(): lax.all_to_all(dkv, 'ctx', 0, 0, axis_index_groups=columns, tiled=True)  5.14 us
    ppermute x1, waiting for transfers between devices, shards(): o_recv = lax.ppermute(o_far, 'ctx', swap)  4.28 us
    ppermute x1, waiting for transfers between devices, shards(): g_far = lax.ppermute(g, 'ctx', swap)  4.15 us
    ppermute x1, starting transfers between devices, shards(): dq_recv = lax.ppermute(dq_sent, 'ctx', swap)  3.92 us
    ppermute x1, starting transfers between devices, shards(): q_far = lax.ppermute(q, 'ctx', swap)  3.39 us
    ppermute x1, waiting for transfers between devices, shards(): there = lax.ppermute(stats, 'ctx', swap)  2.55 us
  transfers between devices with their start and end apart: 7, of which 7 were waited for; matrix products, arithmetic and copies ran while one was open for 1% of the time, Pallas kernels for 6%

profile of v6, /device:TPU:48, one launch (start us, length us, event | category | flops | bytes accessed | tf_op | source)
XLA Modules:
  0.0 66.9 jit_solution(5911987028758275443)
XLA Ops:
  0.6 1.7 %spread.1 = bf16[8,2,128,128]{3,2,1,0:T(8,128)(2,1)} custom-call(bf16[128,128]{1,0:T(8,128)(2,1)} %bitcast.15, bf16[128,128]{1,0:T(8,128)(2,1)} %bitcast.16), custom_call_target="tpu_custom_call" | custom-call | bytes 262144 | tf_op jit(solution)/shard_map/spread/pallas_call | solution.py:287
  2.3 10.3 %all-to-all-start = ((bf16[8,2,128,128]{3,2,1,0:T(8,128)(2,1)}), bf16[8,2,128,128]{3,2,1,0:T(8,128)(2,1)S(1)}, u32[]{:S(2)}, u32[]{:S(2)}) async-start(bf16[8,2,128,128]{3,2,1,0:T(8,128)(2,1)} %spread.1), calls=%async_computation | async-start | bytes 1048576 | tf_op jit(solution)/shard_map/all_to_all | solution.py:323
  12.6 3.4 %collective-permute-start = (bf16[1024,128]{1,0:T(8,128)(2,1)}, bf16[1024,128]{1,0:T(8,128)(2,1)S(1)}, u32[]{:S(2)}, u32[]{:S(2)}) collective-permute-start(bf16[1024,128]{1,0:T(8,128)(2,1)} %bitcast.9), channel_id=1, source_target_pairs={{0,1},{1,0},{2,3},{3,2},{4,5},{5,4},{6,7},{7,6},{8,9},{9,8},{10,11... | collective-permute-start | bytes 786440 | tf_op jit(solution)/shard_map/ppermute | solution.py:324
  16.0 2.4 %collective-permute-start.1 = (bf16[1024,128]{1,0:T(8,128)(2,1)}, bf16[1024,128]{1,0:T(8,128)(2,1)S(1)}, u32[]{:S(2)}, u32[]{:S(2)}) collective-permute-start(bf16[1024,128]{1,0:T(8,128)(2,1)} %bitcast.11), channel_id=1, source_target_pairs={{0,1},{1,0},{2,3},{3,2},{4,5},{5,4},{6,7},{7,6},{8,9},{9,8},{10,11... | collective-permute-start | bytes 786440 | tf_op jit(solution)/shard_map/ppermute | solution.py:325
  18.5 0.7 %pad_add_fusion.info_ref = s32[33]{0:T(128)S(1)} fusion(s32[1]{0:T(128)} %bitcast, s32[32]{0:T(128)} %param.9), kind=kLoop, calls=%fused_computation | loop fusion | flops 33 | bytes 264 | tf_op jit(solution)/shard_map/concatenate | solution.py:326
  19.2 0.0 copy-start
  19.2 0.9 %copy-done = bf16[128,8,128]{2,1,0:T(8,128)(2,1)S(1)} copy-done((bf16[128,8,128]{2,1,0:T(8,128)(2,1)S(1)}, bf16[128,8,128]{2,1,0:T(8,128)(2,1)}, u32[]{:S(2)}) %copy-start) | copy-done | bytes 262168
  20.2 0.0 copy-start.1
  20.2 0.9 %copy-done.1 = bf16[128,8,128]{2,1,0:T(8,128)(2,1)S(1)} copy-done((bf16[128,8,128]{2,1,0:T(8,128)(2,1)S(1)}, bf16[128,8,128]{2,1,0:T(8,128)(2,1)}, u32[]{:S(2)}) %copy-start.1) | copy-done | bytes 262168
  21.1 0.8 %stage.1 = (bf16[4,128,256]{2,1,0:T(8,128)(2,1)S(1)}, bf16[4,128,256]{2,1,0:T(8,128)(2,1)S(1)}, s32[8,16,256]{2,1,0:T(8,128)S(1)}) custom-call(s32[33]{0:T(128)S(1)} %pad_add_fusion.info_ref, bf16[1024,128]{1,0:T(8,128)(2,1)S(1)} %bitcast.10, bf16[1024,128]{1,0:T(8,128)(2,1)S(1)} %bitcast.12), custom_call_target="tpu_custom_call" | custom-call | bytes 1048576 | tf_op jit(solution)/shard_map/stage/pallas_call | solution.py:287
  21.9 2.0 %collective-permute-done.q_ref = bf16[1024,128]{1,0:T(8,128)(2,1)S(1)} collective-permute-done((bf16[1024,128]{1,0:T(8,128)(2,1)}, bf16[1024,128]{1,0:T(8,128)(2,1)S(1)}, u32[]{:S(2)}, u32[]{:S(2)}) %collective-permute-start) | collective-permute-done | bytes 262176 | tf_op jit(solution)/shard_map/ppermute | solution.py:324
  23.9 4.2 %collective-permute-done.1.g_ref = bf16[1024,128]{1,0:T(8,128)(2,1)S(1)} collective-permute-done((bf16[1024,128]{1,0:T(8,128)(2,1)}, bf16[1024,128]{1,0:T(8,128)(2,1)S(1)}, u32[]{:S(2)}, u32[]{:S(2)}) %collective-permute-start.1) | collective-permute-done | bytes 262176 | tf_op jit(solution)/shard_map/ppermute | solution.py:325
  28.1 0.2 flip.1
  28.3 1.8 %all-to-all-done.kv_ref = bf16[8,2,128,128]{3,2,1,0:T(8,128)(2,1)S(1)} async-done(((bf16[8,2,128,128]{3,2,1,0:T(8,128)(2,1)}), bf16[8,2,128,128]{3,2,1,0:T(8,128)(2,1)S(1)}, u32[]{:S(2)}, u32[]{:S(2)}) %all-to-all-start) | async-done | bytes 524320 | tf_op jit(solution)/shard_map/all_to_all | solution.py:323
  30.1 6.8 %forward.1 = (bf16[1024,2048]{1,0:T(8,128)(2,1)S(1)}, f32[4,128,256]{2,1,0:T(8,128)S(1)}, bf16[4,128,256]{2,1,0:T(8,128)(2,1)S(1)}, f32[24,256]{1,0:T(8,128)S(1)}) custom-call(s32[8,16,256]{2,1,0:T(8,128)S(1)} %get-tuple-element.23.limit_ref, bf16[4,128,256]{2,1,0:T(8,128)(2,1)S(1)} %get-tuple-element.19.qt_own, ...), custom_call_target="tpu_custom_call" | custom-call | flops 1073741824 | tf_op jit(solution)/shard_map/forward/pallas_call | solution.py:287
  37.0 1.9 %collective-permute-start.2 = (f32[24,256]{1,0:T(8,128)S(1)}, f32[24,256]{1,0:T(8,128)S(1)}, u32[]{:S(2)}, u32[]{:S(2)}) collective-permute-start(f32[24,256]{1,0:T(8,128)S(1)} %get-tuple-element.25.here_ref), channel_id=1, source_target_pairs={{0,1},{1,0},{2,3},{3,2},{4,5},{5,4},{6,7},{7,6},{8,9},{9,8},{10,11... | collective-permute-start | bytes 73736 | tf_op jit(solution)/shard_map/ppermute | solution.py:354
  38.9 1.2 %middle.1.dp_ref = f32[1024,2048]{1,0:T(8,128)S(1)} custom-call(bf16[4,128,256]{2,1,0:T(8,128)(2,1)S(1)} %get-tuple-element.21.gt_own, bf16[4,128,256]{2,1,0:T(8,128)(2,1)S(1)} %get-tuple-element.22.gt_far, bf16[8,2,128,128]{3,2,1,0:T(8,128)(2,1)S(1)} %all-to-all-done.kv_ref), custom_call_target="tpu_custom_call" | custom-call | flops 536870912 | bytes 8388608 | tf_op jit(solution)/shard_map/middle/pallas_call | solution.py:287
  40.1 2.5 %collective-permute-done.2.there_ref = f32[24,256]{1,0:T(8,128)S(1)} collective-permute-done((f32[24,256]{1,0:T(8,128)S(1)}, f32[24,256]{1,0:T(8,128)S(1)}, u32[]{:S(2)}, u32[]{:S(2)}) %collective-permute-start.2) | collective-permute-done | bytes 24608 | tf_op jit(solution)/shard_map/ppermute | solution.py:354
  42.7 3.3 %backward.1 = (bf16[8,2,128,128]{3,2,1,0:T(8,128)(2,1)}, bf16[4,128,256]{2,1,0:T(8,128)(2,1)S(1)}, bf16[4,128,256]{2,1,0:T(8,128)(2,1)S(1)}, f32[8,8,256]{2,1,0:T(8,128)S(1)}) custom-call(bf16[4,128,256]{2,1,0:T(8,128)(2,1)S(1)} %get-tuple-element.19.qt_own, bf16[4,128,256]{2,1,0:T(8,128)(2,1)S(1)} %get-tuple-element.20.qt_far, ...), custom_call_target="tpu_custom_call" | custom-call | flops 1610612736 | tf_op jit(solution)/shard_map/backward/pallas_call | solution.py:287
  46.0 5.1 %all-to-all-start.1 = ((bf16[8,2,128,128]{3,2,1,0:T(8,128)(2,1)}), bf16[8,2,128,128]{3,2,1,0:T(8,128)(2,1)S(1)}, u32[]{:S(2)}, u32[]{:S(2)}) async-start(bf16[8,2,128,128]{3,2,1,0:T(8,128)(2,1)} %get-tuple-element.31), calls=%async_computation.1 | async-start | bytes 1048576 | tf_op jit(solution)/shard_map/all_to_all | solution.py:381
  51.1 1.9 %collective-permute-start.3 = (bf16[4,128,256]{2,1,0:T(8,128)(2,1)S(1)}, bf16[4,128,256]{2,1,0:T(8,128)(2,1)S(1)}, u32[]{:S(2)}, u32[]{:S(2)}) collective-permute-start(bf16[4,128,256]{2,1,0:T(8,128)(2,1)S(1)} %get-tuple-element.28), channel_id=1, source_target_pairs={{0,1},{1,0},{2,3},{3,2},{4,5},{5,4},{6,7},{7,6},{8,9},{9,8},{10,11... | collective-permute-start | bytes 786440 | tf_op jit(solution)/shard_map/ppermute | solution.py:359
  53.1 3.9 %collective-permute-start.4 = (bf16[4,128,256]{2,1,0:T(8,128)(2,1)S(1)}, bf16[4,128,256]{2,1,0:T(8,128)(2,1)S(1)}, u32[]{:S(2)}, u32[]{:S(2)}) collective-permute-start(bf16[4,128,256]{2,1,0:T(8,128)(2,1)S(1)} %pack.1), channel_id=1, source_target_pairs={{0,1},{1,0},{2,3},{3,2},{4,5},{5,4},{6,7},{7,6},{8,9},{9,8},{10,11... | collective-permute-start | bytes 786440 | tf_op jit(solution)/shard_map/ppermute | solution.py:386
  57.0 4.3 %collective-permute-done.3.o_recv = bf16[4,128,256]{2,1,0:T(8,128)(2,1)S(1)} collective-permute-done((bf16[4,128,256]{2,1,0:T(8,128)(2,1)S(1)}, bf16[4,128,256]{2,1,0:T(8,128)(2,1)S(1)}, u32[]{:S(2)}, u32[]{:S(2)}) %collective-permute-start.3) | collective-permute-done | bytes 262176 | tf_op jit(solution)/shard_map/ppermute | solution.py:359
  61.3 0.9 %out.1 = bf16[1024,128]{1,0:T(8,128)(2,1)} custom-call(f32[8,8,256]{2,1,0:T(8,128)S(1)} %get-tuple-element.26.factor_ref, f32[4,128,256]{2,1,0:T(8,128)S(1)} %get-tuple-element.27.o_own, bf16[4,128,256]{2,1,0:T(8,128)(2,1)S(1)} %collective-permute-done.3.o_recv), custom_call_target="tpu_custom_call" | custom-call | bytes 1048576 | tf_op jit(solution)/shard_map/out/pallas_call | solution.py:287
  62.2 2.0 %collective-permute-done.4.dq_recv = bf16[4,128,256]{2,1,0:T(8,128)(2,1)S(1)} collective-permute-done((bf16[4,128,256]{2,1,0:T(8,128)(2,1)S(1)}, bf16[4,128,256]{2,1,0:T(8,128)(2,1)S(1)}, u32[]{:S(2)}, u32[]{:S(2)}) %collective-permute-start.4) | collective-permute-done | bytes 262176 | tf_op jit(solution)/shard_map/ppermute | solution.py:386
  64.1 0.8 %join.1 = bf16[1024,128]{1,0:T(8,128)(2,1)} custom-call(bf16[4,128,256]{2,1,0:T(8,128)(2,1)S(1)} %get-tuple-element.29.dq_own, bf16[4,128,256]{2,1,0:T(8,128)(2,1)S(1)} %collective-permute-done.4.dq_recv), custom_call_target="tpu_custom_call" | custom-call | bytes 1048576 | tf_op jit(solution)/shard_map/join/pallas_call | solution.py:287
  65.0 1.3 %all-to-all-done.1.terms_ref = bf16[8,2,128,128]{3,2,1,0:T(8,128)(2,1)S(1)} async-done(((bf16[8,2,128,128]{3,2,1,0:T(8,128)(2,1)}), bf16[8,2,128,128]{3,2,1,0:T(8,128)(2,1)S(1)}, u32[]{:S(2)}, u32[]{:S(2)}) %all-to-all-start.1) | async-done | bytes 524320 | tf_op jit(solution)/shard_map/all_to_all | solution.py:381
  66.2 0.7 %total.1 = (bf16[128,128]{1,0:T(8,128)(2,1)}, bf16[128,128]{1,0:T(8,128)(2,1)}) custom-call(bf16[8,2,128,128]{3,2,1,0:T(8,128)(2,1)S(1)} %all-to-all-done.1.terms_ref), custom_call_target="tpu_custom_call" | custom-call | bytes 524288 | tf_op jit(solution)/shard_map/total/pallas_call | solution.py:287
  (1 shorter events, 0.0 us)
Async XLA Ops:
  2.3 27.8 %all-to-all-start = ((bf16[8,2,128,128]{3,2,1,0:T(8,128)(2,1)}), bf16[8,2,128,128]{3,2,1,0:T(8,128)(2,1)S(1)}, u32[]{:S(2)}, u32[]{:S(2)}) async-start(bf16[8,2,128,128]{3,2,1,0:T(8,128)(2,1)} %spread.1), calls=%async_computation | async-start | bytes 1048576 | tf_op jit(solution)/shard_map/all_to_all | solution.py:323
  12.6 11.3 %collective-permute-start = (bf16[1024,128]{1,0:T(8,128)(2,1)}, bf16[1024,128]{1,0:T(8,128)(2,1)S(1)}, u32[]{:S(2)}, u32[]{:S(2)}) collective-permute-start(bf16[1024,128]{1,0:T(8,128)(2,1)} %bitcast.9), channel_id=1, source_target_pairs={{0,1},{1,0},{2,3},{3,2},{4,5},{5,4},{6,7},{7,6},{8,9},{9,8},{10,11... | collective-permute-start | bytes 786440 | tf_op jit(solution)/shard_map/ppermute | solution.py:324
  16.0 12.1 %collective-permute-start.1 = (bf16[1024,128]{1,0:T(8,128)(2,1)}, bf16[1024,128]{1,0:T(8,128)(2,1)S(1)}, u32[]{:S(2)}, u32[]{:S(2)}) collective-permute-start(bf16[1024,128]{1,0:T(8,128)(2,1)} %bitcast.11), channel_id=1, source_target_pairs={{0,1},{1,0},{2,3},{3,2},{4,5},{5,4},{6,7},{7,6},{8,9},{9,8},{10,11... | collective-permute-start | bytes 786440 | tf_op jit(solution)/shard_map/ppermute | solution.py:325
  19.2 0.9 %copy-start = (bf16[128,8,128]{2,1,0:T(8,128)(2,1)S(1)}, bf16[128,8,128]{2,1,0:T(8,128)(2,1)}, u32[]{:S(2)}) copy-start(bf16[128,8,128]{2,1,0:T(8,128)(2,1)} %param.5) | copy-start | bytes 786436
  20.2 0.9 %copy-start.1 = (bf16[128,8,128]{2,1,0:T(8,128)(2,1)S(1)}, bf16[128,8,128]{2,1,0:T(8,128)(2,1)}, u32[]{:S(2)}) copy-start(bf16[128,8,128]{2,1,0:T(8,128)(2,1)} %param.8) | copy-start | bytes 786436
  37.0 5.7 %collective-permute-start.2 = (f32[24,256]{1,0:T(8,128)S(1)}, f32[24,256]{1,0:T(8,128)S(1)}, u32[]{:S(2)}, u32[]{:S(2)}) collective-permute-start(f32[24,256]{1,0:T(8,128)S(1)} %get-tuple-element.25.here_ref), channel_id=1, source_target_pairs={{0,1},{1,0},{2,3},{3,2},{4,5},{5,4},{6,7},{7,6},{8,9},{9,8},{10,11... | collective-permute-start | bytes 73736 | tf_op jit(solution)/shard_map/ppermute | solution.py:354
  46.0 20.2 %all-to-all-start.1 = ((bf16[8,2,128,128]{3,2,1,0:T(8,128)(2,1)}), bf16[8,2,128,128]{3,2,1,0:T(8,128)(2,1)S(1)}, u32[]{:S(2)}, u32[]{:S(2)}) async-start(bf16[8,2,128,128]{3,2,1,0:T(8,128)(2,1)} %get-tuple-element.31), calls=%async_computation.1 | async-start | bytes 1048576 | tf_op jit(solution)/shard_map/all_to_all | solution.py:381
  51.1 10.2 %collective-permute-start.3 = (bf16[4,128,256]{2,1,0:T(8,128)(2,1)S(1)}, bf16[4,128,256]{2,1,0:T(8,128)(2,1)S(1)}, u32[]{:S(2)}, u32[]{:S(2)}) collective-permute-start(bf16[4,128,256]{2,1,0:T(8,128)(2,1)S(1)} %get-tuple-element.28), channel_id=1, source_target_pairs={{0,1},{1,0},{2,3},{3,2},{4,5},{5,4},{6,7},{7,6},{8,9},{9,8},{10,11... | collective-permute-start | bytes 786440 | tf_op jit(solution)/shard_map/ppermute | solution.py:359
  53.1 11.0 %collective-permute-start.4 = (bf16[4,128,256]{2,1,0:T(8,128)(2,1)S(1)}, bf16[4,128,256]{2,1,0:T(8,128)(2,1)S(1)}, u32[]{:S(2)}, u32[]{:S(2)}) collective-permute-start(bf16[4,128,256]{2,1,0:T(8,128)(2,1)S(1)} %pack.1), channel_id=1, source_target_pairs={{0,1},{1,0},{2,3},{3,2},{4,5},{5,4},{6,7},{7,6},{8,9},{9,8},{10,11... | collective-permute-start | bytes 786440 | tf_op jit(solution)/shard_map/ppermute | solution.py:386

commit v7 on v5

--- a/solution.py
+++ b/solution.py
@@ -142,19 +142,28 @@
                     part = jnp.where(key_of <= limit, part, NEG_FILL)
                 parts.append(part - jnp.where(limit >= 0, guesses[tile], -NEG_FILL))
             p = jnp.exp2(jnp.concatenate(parts, axis=0))
+            if tile == tiles - 1:
+                sums.append(jnp.sum(p.reshape(TILE // 8, 8, TILE), axis=0))
             p_ref[c * TILE : (c + 1) * TILE, put] = p.astype(HALF)
 
+    def bad(seen, total):
+        fine = jnp.logical_and(total >= 1.0 / WIDEST, total <= WIDEST)
+        return jnp.where(jnp.logical_and(seen, jnp.logical_not(fine)), 1.0, 0.0)
+
     wrong = jnp.zeros((1, TILE), F32)
+    sums = []
     guessed(0)
     for tile in range(tiles):
         if tile + 1 < tiles:
             guessed(tile + 1)
         seen = jnp.max(limit_ref[tile], axis=0, keepdims=True) >= 0
+        if tile == tiles - 1:
+            total = jnp.sum(sum(sums[1:], sums[0]), axis=0, keepdims=True)
+            again = jnp.max(jnp.maximum(wrong, bad(seen, total))) > 0.0
         total = weigh(tile, jnp.where(seen, guesses[tile], NEG_FILL))
-        fine = jnp.logical_and(total >= 1.0 / WIDEST, total <= WIDEST)
-        wrong = jnp.where(jnp.logical_and(seen, jnp.logical_not(fine)), 1.0, wrong)
-
-    @pl.when(jnp.max(wrong) > 0.0)
+        wrong = jnp.maximum(wrong, bad(seen, total))
+
+    @pl.when(again)
     def _():
         for tile in range(tiles):
             put = slice(tile * TILE, (tile + 1) * TILE)

time: 67.3 us -> 67.3 us (level)
  no operation moved by 1% of the time
where the time goes in v7:
time: 67.3 us; the launch traced here: 66.8 us
  starting transfers between devices  27.2 us (40%)
  Pallas kernels  16.3 us (24%)
  waiting for transfers between devices  15.5 us (23%)
  blocking collectives  4.5 us (7%)
  local copies, waits for them, and re-layouts  1.9 us (3%)
  other arithmetic  0.73 us (1%)
  between operations  0.72 us (1%)
    pallas_call x9, Pallas kernels, call(): pl.pallas_call(kernel, in_specs=specs or [VMEM] * len(ins), out_specs=out...  16.3 us
    all_to_all x1, starting transfers between devices, shards(): lax.all_to_all(spread, 'ctx', 0, 0, axis_index_groups=columns, tiled=True)  10.3 us
    all_to_all x1, starting transfers between devices, shards(): lax.all_to_all(dkv, 'ctx', 0, 0, axis_index_groups=columns, tiled=True)  5.15 us
    all_gather x1, blocking collectives, shards(): both = lax.all_gather(stats, 'ctx', axis_index_groups=pairs)  4.5 us
    ppermute x1, waiting for transfers between devices, shards(): dq_recv = lax.ppermute(dq_sent, 'ctx', swap)  4.3 us
    ppermute x1, waiting for transfers between devices, shards(): g_far = lax.ppermute(g, 'ctx', swap)  4.15 us
    ppermute x1, starting transfers between devices, shards(): o_recv = lax.ppermute(o_far, 'ctx', swap)  3.92 us
    ppermute x1, starting transfers between devices, shards(): q_far = lax.ppermute(q, 'ctx', swap)  3.1 us
  transfers between devices with their start and end apart: 6, of which 6 were waited for; matrix products, arithmetic and copies ran while one was open for 1% of the time, Pallas kernels for 4%

profile of v7, /device:TPU:20, one launch (start us, length us, event | category | flops | bytes accessed | tf_op | source)
XLA Modules:
  0.0 66.8 jit_solution(2127042588873265635)
XLA Ops:
  0.6 1.7 %spread.1 = bf16[8,2,128,128]{3,2,1,0:T(8,128)(2,1)} custom-call(bf16[128,128]{1,0:T(8,128)(2,1)} %bitcast.17, bf16[128,128]{1,0:T(8,128)(2,1)} %bitcast.18), custom_call_target="tpu_custom_call" | custom-call | bytes 262144 | tf_op jit(solution)/shard_map/spread/pallas_call | solution.py:287
  2.3 10.3 %all-to-all-start = ((bf16[8,2,128,128]{3,2,1,0:T(8,128)(2,1)}), bf16[8,2,128,128]{3,2,1,0:T(8,128)(2,1)S(1)}, u32[]{:S(2)}, u32[]{:S(2)}) async-start(bf16[8,2,128,128]{3,2,1,0:T(8,128)(2,1)} %spread.1), calls=%async_computation | async-start | bytes 1048576 | tf_op jit(solution)/shard_map/all_to_all | solution.py:323
  12.6 3.1 %collective-permute-start = (bf16[1024,128]{1,0:T(8,128)(2,1)}, bf16[1024,128]{1,0:T(8,128)(2,1)S(1)}, u32[]{:S(2)}, u32[]{:S(2)}) collective-permute-start(bf16[1024,128]{1,0:T(8,128)(2,1)} %bitcast.10), channel_id=1, source_target_pairs={{0,1},{1,0},{2,3},{3,2},{4,5},{5,4},{6,7},{7,6},{8,9},{9,8},{10,11... | collective-permute-start | bytes 786440 | tf_op jit(solution)/shard_map/ppermute | solution.py:324
  15.7 2.7 %collective-permute-start.1 = (bf16[1024,128]{1,0:T(8,128)(2,1)}, bf16[1024,128]{1,0:T(8,128)(2,1)S(1)}, u32[]{:S(2)}, u32[]{:S(2)}) collective-permute-start(bf16[1024,128]{1,0:T(8,128)(2,1)} %bitcast.12), channel_id=1, source_target_pairs={{0,1},{1,0},{2,3},{3,2},{4,5},{5,4},{6,7},{7,6},{8,9},{9,8},{10,11... | collective-permute-start | bytes 786440 | tf_op jit(solution)/shard_map/ppermute | solution.py:325
  18.5 0.7 %pad_add_fusion.info_ref = s32[33]{0:T(128)S(1)} fusion(s32[1]{0:T(128)} %bitcast, s32[32]{0:T(128)} %param.9), kind=kLoop, calls=%fused_computation | loop fusion | flops 33 | bytes 264 | tf_op jit(solution)/shard_map/concatenate | solution.py:326
  19.2 0.0 copy-start
  19.2 0.9 %copy-done = bf16[128,8,128]{2,1,0:T(8,128)(2,1)S(1)} copy-done((bf16[128,8,128]{2,1,0:T(8,128)(2,1)S(1)}, bf16[128,8,128]{2,1,0:T(8,128)(2,1)}, u32[]{:S(2)}) %copy-start) | copy-done | bytes 262168
  20.2 0.0 copy-start.1
  20.2 0.9 %copy-done.1 = bf16[128,8,128]{2,1,0:T(8,128)(2,1)S(1)} copy-done((bf16[128,8,128]{2,1,0:T(8,128)(2,1)S(1)}, bf16[128,8,128]{2,1,0:T(8,128)(2,1)}, u32[]{:S(2)}) %copy-start.1) | copy-done | bytes 262168
  21.1 0.8 %stage.1 = (bf16[4,128,256]{2,1,0:T(8,128)(2,1)S(1)}, bf16[4,128,256]{2,1,0:T(8,128)(2,1)S(1)}, s32[8,16,256]{2,1,0:T(8,128)S(1)}, s32[8,256]{1,0:T(8,128)S(1)}) custom-call(s32[33]{0:T(128)S(1)} %pad_add_fusion.info_ref, bf16[1024,128]{1,0:T(8,128)(2,1)S(1)} %bitcast.11, bf16[1024,128]{1,0:T(8,128)(2,1)S(1)} %bitcast.13), custom_call_target="tpu_custom_call" | custom-call | bytes 1048576 | tf_op jit(solution)/shard_map/stage/pallas_call | solution.py:287
  21.9 2.0 %collective-permute-done.q_ref = bf16[1024,128]{1,0:T(8,128)(2,1)S(1)} collective-permute-done((bf16[1024,128]{1,0:T(8,128)(2,1)}, bf16[1024,128]{1,0:T(8,128)(2,1)S(1)}, u32[]{:S(2)}, u32[]{:S(2)}) %collective-permute-start) | collective-permute-done | bytes 262176 | tf_op jit(solution)/shard_map/ppermute | solution.py:324
  23.9 4.2 %collective-permute-done.1.g_ref = bf16[1024,128]{1,0:T(8,128)(2,1)S(1)} collective-permute-done((bf16[1024,128]{1,0:T(8,128)(2,1)}, bf16[1024,128]{1,0:T(8,128)(2,1)S(1)}, u32[]{:S(2)}, u32[]{:S(2)}) %collective-permute-start.1) | collective-permute-done | bytes 262176 | tf_op jit(solution)/shard_map/ppermute | solution.py:325
  28.1 0.2 flip.1
  28.3 1.8 %all-to-all-done.kv_ref = bf16[8,2,128,128]{3,2,1,0:T(8,128)(2,1)S(1)} async-done(((bf16[8,2,128,128]{3,2,1,0:T(8,128)(2,1)}), bf16[8,2,128,128]{3,2,1,0:T(8,128)(2,1)S(1)}, u32[]{:S(2)}, u32[]{:S(2)}) %all-to-all-start) | async-done | bytes 524320 | tf_op jit(solution)/shard_map/all_to_all | solution.py:323
  30.1 6.9 %forward.1 = (bf16[1024,2048]{1,0:T(8,128)(2,1)S(1)}, f32[4,128,256]{2,1,0:T(8,128)S(1)}, bf16[4,128,256]{2,1,0:T(8,128)(2,1)S(1)}, f32[24,256]{1,0:T(8,128)S(1)}) custom-call(s32[8,16,256]{2,1,0:T(8,128)S(1)} %get-tuple-element.25.limit_ref, bf16[4,128,256]{2,1,0:T(8,128)(2,1)S(1)} %get-tuple-element.21.qt_own, ...), custom_call_target="tpu_custom_call" | custom-call | flops 1073741824 | tf_op jit(solution)/shard_map/forward/pallas_call | solution.py:287
  37.0 4.5 %all-gather = f32[48,256]{1,0:T(8,128)S(1)} all-gather(f32[24,256]{1,0:T(8,128)S(1)} %get-tuple-element.27), channel_id=2, replica_groups={{0,1},{2,3},{4,5},{6,7},{8,9},{10,11},{12,13},{14,15},{16,17},{18,19},{..., dimensions={0}, use_global_device_ids=true | all-gather | bytes 73728 | tf_op jit(solution)/shard_map/all_gather | solution.py:356
  41.5 4.3 %backward.1 = (bf16[8,2,128,128]{3,2,1,0:T(8,128)(2,1)}, bf16[4,128,256]{2,1,0:T(8,128)(2,1)S(1)}, bf16[4,128,256]{2,1,0:T(8,128)(2,1)S(1)}, f32[8,8,256]{2,1,0:T(8,128)S(1)}) custom-call(s32[8,256]{1,0:T(8,128)S(1)} %get-tuple-element.20.side_ref, bf16[4,128,256]{2,1,0:T(8,128)(2,1)S(1)} %get-tuple-element.21.qt_own, ...), custom_call_target="tpu_custom_call" | custom-call | flops 2147483648 | tf_op jit(solution)/shard_map/backward/pallas_call | solution.py:287
  45.8 5.1 %all-to-all-start.1 = ((bf16[8,2,128,128]{3,2,1,0:T(8,128)(2,1)}), bf16[8,2,128,128]{3,2,1,0:T(8,128)(2,1)S(1)}, u32[]{:S(2)}, u32[]{:S(2)}) async-start(bf16[8,2,128,128]{3,2,1,0:T(8,128)(2,1)} %get-tuple-element.33), calls=%async_computation.1 | async-start | bytes 1048576 | tf_op jit(solution)/shard_map/all_to_all | solution.py:379
  51.0 1.9 %collective-permute-start.3 = (bf16[4,128,256]{2,1,0:T(8,128)(2,1)S(1)}, bf16[4,128,256]{2,1,0:T(8,128)(2,1)S(1)}, u32[]{:S(2)}, u32[]{:S(2)}) collective-permute-start(bf16[4,128,256]{2,1,0:T(8,128)(2,1)S(1)} %pack.1), channel_id=1, source_target_pairs={{0,1},{1,0},{2,3},{3,2},{4,5},{5,4},{6,7},{7,6},{8,9},{9,8},{10,11... | collective-permute-start | bytes 786440 | tf_op jit(solution)/shard_map/ppermute | solution.py:384
  52.9 3.9 %collective-permute-start.2 = (bf16[4,128,256]{2,1,0:T(8,128)(2,1)S(1)}, bf16[4,128,256]{2,1,0:T(8,128)(2,1)S(1)}, u32[]{:S(2)}, u32[]{:S(2)}) collective-permute-start(bf16[4,128,256]{2,1,0:T(8,128)(2,1)S(1)} %get-tuple-element.30), channel_id=1, source_target_pairs={{0,1},{1,0},{2,3},{3,2},{4,5},{5,4},{6,7},{7,6},{8,9},{9,8},{10,11... | collective-permute-start | bytes 786440 | tf_op jit(solution)/shard_map/ppermute | solution.py:357
  56.9 4.3 %collective-permute-done.3.dq_recv = bf16[4,128,256]{2,1,0:T(8,128)(2,1)S(1)} collective-permute-done((bf16[4,128,256]{2,1,0:T(8,128)(2,1)S(1)}, bf16[4,128,256]{2,1,0:T(8,128)(2,1)S(1)}, u32[]{:S(2)}, u32[]{:S(2)}) %collective-permute-start.3) | collective-permute-done | bytes 262176 | tf_op jit(solution)/shard_map/ppermute | solution.py:384
  61.2 0.8 %join.1 = bf16[1024,128]{1,0:T(8,128)(2,1)} custom-call(bf16[4,128,256]{2,1,0:T(8,128)(2,1)S(1)} %get-tuple-element.31.dq_own, bf16[4,128,256]{2,1,0:T(8,128)(2,1)S(1)} %collective-permute-done.3.dq_recv), custom_call_target="tpu_custom_call" | custom-call | bytes 1048576 | tf_op jit(solution)/shard_map/join/pallas_call | solution.py:287
  62.0 2.0 %collective-permute-done.2.o_recv = bf16[4,128,256]{2,1,0:T(8,128)(2,1)S(1)} collective-permute-done((bf16[4,128,256]{2,1,0:T(8,128)(2,1)S(1)}, bf16[4,128,256]{2,1,0:T(8,128)(2,1)S(1)}, u32[]{:S(2)}, u32[]{:S(2)}) %collective-permute-start.2) | collective-permute-done | bytes 262176 | tf_op jit(solution)/shard_map/ppermute | solution.py:357
  64.0 0.9 %out.1 = bf16[1024,128]{1,0:T(8,128)(2,1)} custom-call(f32[8,8,256]{2,1,0:T(8,128)S(1)} %get-tuple-element.28.factor_ref, f32[4,128,256]{2,1,0:T(8,128)S(1)} %get-tuple-element.29.o_own, bf16[4,128,256]{2,1,0:T(8,128)(2,1)S(1)} %collective-permute-done.2.o_recv), custom_call_target="tpu_custom_call" | custom-call | bytes 1048576 | tf_op jit(solution)/shard_map/out/pallas_call | solution.py:287
  64.8 1.2 %all-to-all-done.1.terms_ref = bf16[8,2,128,128]{3,2,1,0:T(8,128)(2,1)S(1)} async-done(((bf16[8,2,128,128]{3,2,1,0:T(8,128)(2,1)}), bf16[8,2,128,128]{3,2,1,0:T(8,128)(2,1)S(1)}, u32[]{:S(2)}, u32[]{:S(2)}) %all-to-all-start.1) | async-done | bytes 524320 | tf_op jit(solution)/shard_map/all_to_all | solution.py:379
  66.1 0.7 %total.1 = (bf16[128,128]{1,0:T(8,128)(2,1)}, bf16[128,128]{1,0:T(8,128)(2,1)}) custom-call(bf16[8,2,128,128]{3,2,1,0:T(8,128)(2,1)S(1)} %all-to-all-done.1.terms_ref), custom_call_target="tpu_custom_call" | custom-call | bytes 524288 | tf_op jit(solution)/shard_map/total/pallas_call | solution.py:287
  (1 shorter events, 0.0 us)
Async XLA Ops:
  2.3 27.8 %all-to-all-start = ((bf16[8,2,128,128]{3,2,1,0:T(8,128)(2,1)}), bf16[8,2,128,128]{3,2,1,0:T(8,128)(2,1)S(1)}, u32[]{:S(2)}, u32[]{:S(2)}) async-start(bf16[8,2,128,128]{3,2,1,0:T(8,128)(2,1)} %spread.1), calls=%async_computation | async-start | bytes 1048576 | tf_op jit(solution)/shard_map/all_to_all | solution.py:323
  12.6 11.3 %collective-permute-start = (bf16[1024,128]{1,0:T(8,128)(2,1)}, bf16[1024,128]{1,0:T(8,128)(2,1)S(1)}, u32[]{:S(2)}, u32[]{:S(2)}) collective-permute-start(bf16[1024,128]{1,0:T(8,128)(2,1)} %bitcast.10), channel_id=1, source_target_pairs={{0,1},{1,0},{2,3},{3,2},{4,5},{5,4},{6,7},{7,6},{8,9},{9,8},{10,11... | collective-permute-start | bytes 786440 | tf_op jit(solution)/shard_map/ppermute | solution.py:324
  15.7 12.4 %collective-permute-start.1 = (bf16[1024,128]{1,0:T(8,128)(2,1)}, bf16[1024,128]{1,0:T(8,128)(2,1)S(1)}, u32[]{:S(2)}, u32[]{:S(2)}) collective-permute-start(bf16[1024,128]{1,0:T(8,128)(2,1)} %bitcast.12), channel_id=1, source_target_pairs={{0,1},{1,0},{2,3},{3,2},{4,5},{5,4},{6,7},{7,6},{8,9},{9,8},{10,11... | collective-permute-start | bytes 786440 | tf_op jit(solution)/shard_map/ppermute | solution.py:325
  19.2 0.9 %copy-start = (bf16[128,8,128]{2,1,0:T(8,128)(2,1)S(1)}, bf16[128,8,128]{2,1,0:T(8,128)(2,1)}, u32[]{:S(2)}) copy-start(bf16[128,8,128]{2,1,0:T(8,128)(2,1)} %param.5) | copy-start | bytes 786436
  20.2 0.9 %copy-start.1 = (bf16[128,8,128]{2,1,0:T(8,128)(2,1)S(1)}, bf16[128,8,128]{2,1,0:T(8,128)(2,1)}, u32[]{:S(2)}) copy-start(bf16[128,8,128]{2,1,0:T(8,128)(2,1)} %param.8) | copy-start | bytes 786436
  45.8 20.2 %all-to-all-start.1 = ((bf16[8,2,128,128]{3,2,1,0:T(8,128)(2,1)}), bf16[8,2,128,128]{3,2,1,0:T(8,128)(2,1)S(1)}, u32[]{:S(2)}, u32[]{:S(2)}) async-start(bf16[8,2,128,128]{3,2,1,0:T(8,128)(2,1)} %get-tuple-element.33), calls=%async_computation.1 | async-start | bytes 1048576 | tf_op jit(solution)/shard_map/all_to_all | solution.py:379
  51.0 10.2 %collective-permute-start.3 = (bf16[4,128,256]{2,1,0:T(8,128)(2,1)S(1)}, bf16[4,128,256]{2,1,0:T(8,128)(2,1)S(1)}, u32[]{:S(2)}, u32[]{:S(2)}) collective-permute-start(bf16[4,128,256]{2,1,0:T(8,128)(2,1)S(1)} %pack.1), channel_id=1, source_target_pairs={{0,1},{1,0},{2,3},{3,2},{4,5},{5,4},{6,7},{7,6},{8,9},{9,8},{10,11... | collective-permute-start | bytes 786440 | tf_op jit(solution)/shard_map/ppermute | solution.py:384
  52.9 11.0 %collective-permute-start.2 = (bf16[4,128,256]{2,1,0:T(8,128)(2,1)S(1)}, bf16[4,128,256]{2,1,0:T(8,128)(2,1)S(1)}, u32[]{:S(2)}, u32[]{:S(2)}) collective-permute-start(bf16[4,128,256]{2,1,0:T(8,128)(2,1)S(1)} %get-tuple-element.30), channel_id=1, source_target_pairs={{0,1},{1,0},{2,3},{3,2},{4,5},{5,4},{6,7},{7,6},{8,9},{9,8},{10,11... | collective-permute-start | bytes 786440 | tf_op jit(solution)/shard_map/ppermute | solution.py:357
